TPU v7x, 512 devices: a whole 4x8x8 slice. The times are simulated.
512 devices in a mesh: lat: 16 (over x_lo, y), lon: 32 (over x_hi, z, core).
Axes of the slice: x: 4 (x_hi: 2, x_lo: 2; x = x_hi * 2 + x_lo), y: 8, z: 8, core: 2. Of those that a mesh axis runs over, the one named last changes fastest.
Arguments:
- latent: bfloat16 [4, 96, 384, 512], P(None, 'lat', 'lon'), may hold values from -21 to 21
- qkv_weight: bfloat16 [512, 1536], P('lon'), may hold values from -0.25 to 0.25
- proj_weight: bfloat16 [512, 512], P('lon'), may hold values from -0.25 to 0.25
- position_bias: bfloat16 [16, 288, 288], replicated, may hold values from -4 to 4
- attn_gain: float32 [512], replicated, may hold values from 0.1 to 1.9
- up_weight: bfloat16 [2048, 512], P('lon'), may hold values from -0.25 to 0.25
- down_weight: bfloat16 [2048, 512], P('lon'), may hold values from -0.125 to 0.125
- mlp_gain: float32 [512], replicated, may hold values from 0.1 to 1.9
Outputs:
- block_out: bfloat16 [4, 96, 384, 512], P(None, 'lat', 'lon')
All inputs are finite; a program needn't handle non-finite values.
Results may differ from a plain program's by a relative error of at most 0.0072.
Values may be sent and summed in bfloat16 or wider, within the bound.
No kernel may reach another device: no remote copies, remote signals or barrier semaphores. Data moves between devices by JAX's collectives and lax.ppermute only.
A program may use at most 64 MiB of HBM per device.

v0:
```python
import jax
import jax.numpy as jnp
from jax import lax
from jax.sharding import PartitionSpec as P

WLAT = 6
WLON = 12


epsilon = 1e-05


def passed_along(value, axis, steps):
    count = lax.axis_size(axis)
    pairs = [(source, (source + steps) % count) for source in range(count)]
    return lax.ppermute(value, axis, pairs)


def layer_norm(values, gain):
    average = jnp.mean(values, -1, keepdims=True)
    centered = values - average
    variance = jnp.mean(centered * centered, -1, keepdims=True)
    return centered * lax.rsqrt(variance + epsilon) * gain


def roll_block(cells, direction):
    half_lat = WLAT // 2
    half_lon = WLON // 2
    lat_rows = cells.shape[1]
    rim_cells = cells[:, lat_rows - half_lat :] if direction > 0 else cells[:, :half_lat]
    arrived = passed_along(rim_cells, "lat", direction)
    if direction > 0:
        cells = jnp.concatenate((arrived, cells[:, : lat_rows - half_lat]), 1)
    else:
        cells = jnp.concatenate((cells[:, half_lat:], arrived), 1)
    lon_cols = cells.shape[2]
    rim_cols = cells[:, :, lon_cols - half_lon :] if direction > 0 else cells[:, :, :half_lon]
    arrived_cols = passed_along(rim_cols, "lon", direction)
    if direction > 0:
        cells = jnp.concatenate((arrived_cols, cells[:, :, : lon_cols - half_lon]), 2)
    else:
        cells = jnp.concatenate((cells[:, :, half_lon:], arrived_cols), 2)
    return cells


def attend(cells, labels, qkv_weight, position_bias):
    levels, lat_rows, lon_cols, features = cells.shape
    head_count = position_bias.shape[0]
    head_dim = features // head_count
    lat_bands = lat_rows // WLAT
    strips = lon_cols // WLON
    windows = lat_bands * strips
    window_len = levels * WLAT * WLON
    packed = jnp.dot(
        cells.reshape(-1, features), qkv_weight, preferred_element_type=jnp.float32
    ).astype(jnp.bfloat16)
    packed = packed.reshape(levels, lat_bands, WLAT, strips, WLON, 3, head_count, head_dim)
    packed = packed.transpose(5, 1, 3, 6, 0, 2, 4, 7).reshape(
        3, windows, head_count, window_len, head_dim
    )
    queries = packed[0]
    key_rows = packed[1]
    values = packed[2]
    scores = jnp.einsum(
        "wgqd,wgkd->wgqk", queries, key_rows, preferred_element_type=jnp.float32
    ) * head_dim ** (-0.5)
    scores = scores + position_bias.astype(jnp.float32)[None]
    region_tags = jnp.broadcast_to(
        labels.reshape(lat_bands, 1, 1, WLAT, 1), (lat_bands, strips, levels, WLAT, WLON)
    ).reshape(windows, window_len)
    same_region = region_tags[:, :, None] == region_tags[:, None, :]
    scores = jnp.where(same_region[:, None], scores, -1e30)
    row_max = jnp.max(scores, -1, keepdims=True)
    weights = jnp.exp(scores - row_max)
    weights = (weights / jnp.sum(weights, -1, keepdims=True)).astype(jnp.bfloat16)
    attn_out = jnp.einsum(
        "wgqk,wgkd->wgqd", weights, values, preferred_element_type=jnp.float32
    ).astype(jnp.bfloat16)
    attn_out = attn_out.reshape(
        lat_bands, strips, head_count, levels, WLAT, WLON, head_dim
    ).transpose(3, 0, 4, 1, 5, 2, 6)
    return attn_out.reshape(levels * lat_rows * lon_cols, features)


def shards(
    latent, qkv_weight, proj_weight, position_bias, attn_gain, up_weight, down_weight, mlp_gain
):
    levels, lat_rows, lon_cols, features = latent.shape
    full_qkv, full_proj, full_up, full_down = (
        lax.all_gather(qkv_weight, "lon", axis=0, tiled=True),
        lax.all_gather(proj_weight, "lon", axis=0, tiled=True),
        lax.all_gather(up_weight, "lon", axis=0, tiled=True),
        lax.all_gather(down_weight, "lon", axis=0, tiled=True),
    )
    rolled = roll_block(latent, 1)
    first_row = lax.axis_index("lat") * lat_rows
    labels = first_row + jnp.arange(lat_rows, dtype=jnp.int32) < WLAT // 2
    attn_out = attend(rolled, labels, full_qkv, position_bias)
    projected = jnp.dot(attn_out, full_proj, preferred_element_type=jnp.float32)
    mixed = (
        rolled.reshape(-1, features).astype(jnp.float32) + layer_norm(projected, attn_gain)
    ).astype(jnp.bfloat16)
    mixed = mixed.reshape(latent.shape)
    cells = roll_block(mixed, -1)
    token_rows = cells.reshape(-1, features)
    raised = lax.dot_general(
        token_rows, full_up, (((1,), (1,)), ((), ())), preferred_element_type=jnp.float32
    )
    hidden = jax.nn.gelu(raised, approximate=False).astype(jnp.bfloat16)
    lowered = jnp.dot(hidden, full_down, preferred_element_type=jnp.float32)
    updated = token_rows.astype(jnp.float32) + layer_norm(lowered, mlp_gain)
    return updated.astype(jnp.bfloat16).reshape(cells.shape)


def solution(mesh):
    placed = (
        P(None, "lat", "lon", None),
        P("lon", None),
        P("lon", None),
        P(),
        P(),
        P("lon", None),
        P("lon", None),
        P(),
    )
    return jax.shard_map(
        shards, mesh=mesh, in_specs=placed, out_specs=P(None, "lat", "lon", None), check_vma=False
    )
```

profile of v0, /device:TPU:1, one launch (start us, length us, event | category | flops | bytes accessed | tf_op | source)
XLA Modules:
  0.0 289.0 jit_solution(14574946388448211298)
XLA Ops:
  6.5 0.7 all-gather.4.cloned.1.call-update
  7.3 0.7 all-gather.6.cloned.1.call-update
  8.1 1.1 fusion.72
  9.1 4.0 %collective-permute-start = (bf16[4,3,12,512]{3,0,2,1:T(4,128)(2,1)S(1)}, bf16[4,3,12,512]{3,0,2,1:T(4,128)(2,1)S(1)}, u32[]{:S(2)}, u32[]{:S(2)}) collective-permute-start(bf16[4,3,12,512]{3,0,2,1:T(4,128)(2,1)S(1)} %get-tuple-element.12), channel_id=1, source_target_pairs={{0,32},{32,64},{64,96},{96,128},{128,160},{160,192},{192,224},{224... | collective-permute-start | bytes 442376 | tf_op jit(solution)/shard_map/ppermute | solution.py:16
  13.2 6.0 %copy.20 = bf16[16,288,288]{1,2,0:T(8,128)(2,1)} copy(bf16[16,288,288]{2,1,0:T(8,128)(2,1)} %param.11) | data formatting | bytes 5308416 | tf_op args[3]
  19.5 52.8 %all_gather.13 = bf16[512,512]{1,0:T(8,128)(2,1)} all-gather(bf16[16,512]{1,0:T(8,128)(2,1)S(1)} %copy-done.4), channel_id=1, replica_groups=mesh['lat'=16,'lon'=32] {'lon'}, dimensions={0}, use_global_device_ids=true | all-gather | bytes 540672 | tf_op jit(solution)/shard_map/all_gather | solution.py:91
  72.3 1.9 collective-permute-start.1
  74.3 0.8 broadcast_compare_fusion
  75.0 1.3 collective-permute-done.1
  76.4 0.2 fusion.23
  76.7 24.7 %all-gather.4.cloned.1.call-done = bf16[512,1536]{1,0:T(8,128)(2,1)} async-done(((bf16[16,1536]{1,0:T(8,128)(2,1)}), bf16[512,1536]{1,0:T(8,128)(2,1)}) %all-gather.4.cloned.1.call-update) | async-done | bytes 1572880 | tf_op jit(solution)/shard_map/all_gather | solution.py:90
  101.4 3.0 %convolution_convert_fusion = bf16[288,1536]{1,0:T(8,128)(2,1)} fusion(bf16[288,512]{1,0:T(8,128)(2,1)S(1)} %reshape.145, bf16[512,1536]{1,0:T(8,128)(2,1)} %all-gather.4.cloned.1.call-done), kind=kOutput, calls=%fused_computation.11 | convolution fusion | flops 453427200 | bytes 2752512 | tf_op jit(solution)/shard_map/dot_general | solution.py:54
  104.4 3.7 %reshape.146 = bf16[4,1,6,1,12,3,16,32]{7,6,5,4,2,0,3,1:T(8,128)(2,1)S(1)} reshape(bf16[288,1536]{1,0:T(8,128)(2,1)} %convolution_convert_fusion) | data formatting | bytes 1769472 | tf_op jit(solution)/shard_map/reshape | solution.py:57
  108.0 1.0 copy.49
  109.1 2.1 fusion.70
  111.2 1.2 copy-done
  112.3 8.4 %fusion.73 = (f32[16,288]{1,0:T(8,128)}, f32[16,288,288]{1,2,0:T(8,128)}) fusion(bf16[16,288,288]{1,2,0:T(8,128)(2,1)S(1)} %copy-done, pred[288,288]{0,1:T(8,128)(4,1)} %broadcast_compare_fusion, bf16[16,288,32]{2,0,1:T(8,128)(2,1)} %bitcast.23, bf16[16,288,32]{2,0,1:T(8,128)(2,1)} %bitcast.24), kind=kOutput, calls=%fused_computation.91 | convolution fusion | flops 92897568 | bytes 8653824 | tf_op jit(solution)/shard_map/sub | solution.py:74
  120.8 4.3 %fusion.16 = bf16[16,288,32]{1,2,0:T(8,128)(2,1)S(1)} fusion(f32[16,288,288]{1,2,0:T(8,128)} %get-tuple-element.15, f32[16,288]{1,0:T(8,128)} %get-tuple-element.14, bf16[16,288,32]{2,0,1:T(8,128)(2,1)} %bitcast.22), kind=kOutput, calls=%fused_computation.30 | convolution fusion | flops 87736320 | bytes 5916672 | tf_op jit(solution)/shard_map/wgqk,wgkd->wgqd/dot_general | solution.py:76
  125.1 1.1 copy.23
  126.2 1.1 reshape.151
  127.3 0.4 fusion.78
  127.8 0.2 multiply_reduce_fusion.1
  128.3 4.5 %collective-permute-start.2 = (bf16[4,3,12,512]{3,2,1,0:T(8,128)(2,1)S(1)}, bf16[4,3,12,512]{3,2,1,0:T(8,128)(2,1)S(1)}, u32[]{:S(2)}, u32[]{:S(2)}) collective-permute-start(bf16[4,3,12,512]{3,2,1,0:T(8,128)(2,1)S(1)} %get-tuple-element.11), channel_id=1, source_target_pairs={{0,480},{32,0},{64,32},{96,64},{128,96},{160,128},{192,160},{224,1... | collective-permute-start | bytes 442376 | tf_op jit(solution)/shard_map/ppermute | solution.py:16
  132.8 4.0 %collective-permute-done.2 = bf16[4,3,12,512]{3,2,1,0:T(8,128)(2,1)S(1)} collective-permute-done((bf16[4,3,12,512]{3,2,1,0:T(8,128)(2,1)S(1)}, bf16[4,3,12,512]{3,2,1,0:T(8,128)(2,1)S(1)}, u32[]{:S(2)}, u32[]{:S(2)}) %collective-permute-start.2) | collective-permute-done | bytes 147488 | tf_op jit(solution)/shard_map/ppermute | solution.py:16
  136.9 3.1 %collective-permute-start.3 = (bf16[4,6,6,512]{3,2,1,0:T(8,128)(2,1)S(1)}, bf16[4,6,6,512]{3,2,1,0:T(8,128)(2,1)S(1)}, u32[]{:S(2)}, u32[]{:S(2)}) collective-permute-start(bf16[4,6,6,512]{3,2,1,0:T(8,128)(2,1)S(1)} %get-tuple-element.9), channel_id=1, source_target_pairs={{0,31},{1,0},{2,1},{3,2},{4,3},{5,4},{6,5},{7,6},{8,7},{9,8},{10,9... | collective-permute-start | bytes 442376 | tf_op jit(solution)/shard_map/ppermute | solution.py:16
  140.1 4.0 %collective-permute-done.3 = bf16[4,6,6,512]{3,2,1,0:T(8,128)(2,1)S(1)} collective-permute-done((bf16[4,6,6,512]{3,2,1,0:T(8,128)(2,1)S(1)}, bf16[4,6,6,512]{3,2,1,0:T(8,128)(2,1)S(1)}, u32[]{:S(2)}, u32[]{:S(2)}) %collective-permute-start.3) | collective-permute-done | bytes 147488 | tf_op jit(solution)/shard_map/ppermute | solution.py:16
  144.3 42.6 %all-gather.6.cloned.1.call-done = bf16[2048,512]{1,0:T(8,128)(2,1)} async-done(((bf16[64,512]{1,0:T(8,128)(2,1)}), bf16[2048,512]{1,0:T(8,128)(2,1)}) %all-gather.6.cloned.1.call-update) | async-done | bytes 2097168 | tf_op jit(solution)/shard_map/all_gather | solution.py:92
  186.9 85.7 %all-gather.8.cloned.1.call-done = bf16[2048,512]{1,0:T(8,128)(2,1)} async-done(((bf16[64,512]{1,0:T(8,128)(2,1)}), bf16[2048,512]{1,0:T(8,128)(2,1)}) %all-gather.8.cloned.1.call-update) | async-done | bytes 2097168 | tf_op jit(solution)/shard_map/all_gather | solution.py:93
  272.6 8.4 %fusion.79 = (f32[288]{0:T(512)S(1)}, f32[288,512]{1,0:T(8,128)S(1)}) fusion(bf16[2048,512]{1,0:T(8,128)(2,1)} %all-gather.8.cloned.1.call-done, bf16[288,512]{1,0:T(8,128)(2,1)S(1)} %reshape.153, bf16[2048,512]{1,0:T(8,128)(2,1)} %all-gather.6.cloned.1.call-done), kind=kOutput, calls=%fused_computation.93 | convolution fusion | flops 1246445312 | bytes 5080192 | tf_op jit(solution)/shard_map/dot_general | solution.py:110
  281.0 0.2 multiply_reduce_fusion
  281.2 0.2 add_convert_fusion
  281.5 0.9 copy.24
  (35 shorter events, 1.2 us)
Async XLA Ops:
  6.5 94.8 %all-gather.4.cloned.1.call-start = ((), (), s32[]{:S(2)}) async-start(), calls=%async_computation | async-start | bytes 1622016 | tf_op jit(solution)/shard_map/all_gather | solution.py:90
  7.3 179.6 %all-gather.6.cloned.1.call-start = ((), (), s32[]{:S(2)}) async-start(), calls=%async_computation.1 | async-start | bytes 2162688 | tf_op jit(solution)/shard_map/all_gather | solution.py:92
  8.0 264.6 %all-gather.8.cloned.1.call-start = ((), (), s32[]{:S(2)}) async-start(), calls=%async_computation.2 | async-start | bytes 2162688 | tf_op jit(solution)/shard_map/all_gather | solution.py:93
  9.1 63.1 %collective-permute-start = (bf16[4,3,12,512]{3,0,2,1:T(4,128)(2,1)S(1)}, bf16[4,3,12,512]{3,0,2,1:T(4,128)(2,1)S(1)}, u32[]{:S(2)}, u32[]{:S(2)}) collective-permute-start(bf16[4,3,12,512]{3,0,2,1:T(4,128)(2,1)S(1)} %get-tuple-element.12), channel_id=1, source_target_pairs={{0,32},{32,64},{64,96},{96,128},{128,160},{160,192},{192,224},{224... | collective-permute-start | bytes 442376 | tf_op jit(solution)/shard_map/ppermute | solution.py:16
  13.2 6.2 %copy-start.4 = (bf16[16,512]{1,0:T(8,128)(2,1)S(1)}, bf16[16,512]{1,0:T(8,128)(2,1)}, u32[]{:S(2)}) copy-start(bf16[16,512]{1,0:T(8,128)(2,1)} %param.10) | copy-start | bytes 49156
  72.3 4.0 %collective-permute-start.1 = (bf16[4,6,6,512]{3,0,2,1:T(4,128)(2,1)S(1)}, bf16[4,6,6,512]{3,0,2,1:T(4,128)(2,1)S(1)}, u32[]{:S(2)}, u32[]{:S(2)}) collective-permute-start(bf16[4,6,6,512]{3,0,2,1:T(4,128)(2,1)S(1)} %fusion.33), channel_id=1, source_target_pairs={{0,1},{1,2},{2,3},{3,4},{4,5},{5,6},{6,7},{7,8},{8,9},{9,10},{10,1... | collective-permute-start | bytes 442376 | tf_op jit(solution)/shard_map/ppermute | solution.py:16
  76.7 24.7 %copy-start.2 = (bf16[288,512]{1,0:T(8,128)(2,1)}, bf16[288,512]{1,0:T(8,128)(2,1)S(1)}, u32[]{:S(2)}) copy-start(bf16[288,512]{1,0:T(8,128)(2,1)S(1)} %reshape.145) | copy-start | bytes 884740
  109.1 3.3 %copy-start = (bf16[16,288,288]{1,2,0:T(8,128)(2,1)S(1)}, bf16[16,288,288]{1,2,0:T(8,128)(2,1)}, u32[]{:S(2)}) copy-start(bf16[16,288,288]{1,2,0:T(8,128)(2,1)} %copy.20) | copy-start | bytes 7962628
  125.0 2.3 copy-start.1
  125.1 3.0 %copy-start.3 = (bf16[288,512]{1,0:T(8,128)(2,1)S(1)}, bf16[288,512]{1,0:T(8,128)(2,1)}, u32[]{:S(2)}) copy-start(bf16[288,512]{1,0:T(8,128)(2,1)} %copy-done.2) | copy-start | bytes 884740
  125.1 3.0 %copy-start.5 = (f32[512]{0:T(512)S(1)}, f32[512]{0:T(512)}, u32[]{:S(2)}) copy-start(f32[512]{0:T(512)} %param.12) | copy-start | bytes 6148
  128.3 8.5 %collective-permute-start.2 = (bf16[4,3,12,512]{3,2,1,0:T(8,128)(2,1)S(1)}, bf16[4,3,12,512]{3,2,1,0:T(8,128)(2,1)S(1)}, u32[]{:S(2)}, u32[]{:S(2)}) collective-permute-start(bf16[4,3,12,512]{3,2,1,0:T(8,128)(2,1)S(1)} %get-tuple-element.11), channel_id=1, source_target_pairs={{0,480},{32,0},{64,32},{96,64},{128,96},{160,128},{192,160},{224,1... | collective-permute-start | bytes 442376 | tf_op jit(solution)/shard_map/ppermute | solution.py:16
  136.9 7.1 %collective-permute-start.3 = (bf16[4,6,6,512]{3,2,1,0:T(8,128)(2,1)S(1)}, bf16[4,6,6,512]{3,2,1,0:T(8,128)(2,1)S(1)}, u32[]{:S(2)}, u32[]{:S(2)}) collective-permute-start(bf16[4,6,6,512]{3,2,1,0:T(8,128)(2,1)S(1)} %get-tuple-element.9), channel_id=1, source_target_pairs={{0,31},{1,0},{2,1},{3,2},{4,3},{5,4},{6,5},{7,6},{8,7},{9,8},{10,9... | collective-permute-start | bytes 442376 | tf_op jit(solution)/shard_map/ppermute | solution.py:16
  144.3 136.9 %copy-start.6 = (f32[512]{0:T(512)S(1)}, f32[512]{0:T(512)}, u32[]{:S(2)}) copy-start(f32[512]{0:T(512)} %param.15) | copy-start | bytes 6148
Sparse Core Ops, SparseCore 0:
  10.7 90.6 all-gather.3
  104.7 82.0 all-gather.5
  190.3 82.2 all-gather.7
where the time goes:
time: 289 us
  waiting for transfers between devices  164 us (57%)
  blocking collectives  52.8 us (18%)
  matrix products  24.4 us (8%)
  local copies, waits for them, and re-layouts  18.9 us (7%)
  starting transfers between devices  13.6 us (5%)
  between operations  13.4 us (5%)
    all_gather x1, waiting for transfers between devices, shards(): lax.all_gather(down_weight, 'lon', axis=0, tiled=True)  85.7 us
    all_gather x1, blocking collectives, shards(): lax.all_gather(proj_weight, 'lon', axis=0, tiled=True)  52.8 us
    all_gather x1, waiting for transfers between devices, shards(): lax.all_gather(up_weight, 'lon', axis=0, tiled=True)  42.6 us
    all_gather x1, waiting for transfers between devices, shards(): lax.all_gather(qkv_weight, 'lon', axis=0, tiled=True)  24.7 us
    ppermute x4, starting transfers between devices, passed_along(): return lax.ppermute(value, axis, pairs)  13.6 us
    ppermute x4, waiting for transfers between devices, passed_along(): return lax.ppermute(value, axis, pairs)  9.31 us
    sub x1, matrix products, attend(): weights = jnp.exp(scores - row_max)  8.42 us
    dot_general x1, matrix products, shards(): lowered = jnp.dot(hidden, full_down, preferred_element_type=jnp.float32)  8.36 us
  transfers between devices with their start and end apart: 7, of which 6 were waited for; matrix products, arithmetic and copies ran while one was open for 12% of the time, Pallas kernels for 0%

commit v1 on v0

v1 whole, which is shorter than its diff:
```python
import jax
import jax.numpy as jnp
import numpy as np
from jax import lax
from jax.experimental import pallas as pl
from jax.experimental.pallas import tpu as pltpu
from jax.sharding import Mesh, PartitionSpec as P

WLAT = 6
WLON = 12
LEVELS = 4
HALF_LAT = WLAT // 2
HALF_LON = WLON // 2
QUARTER = LEVELS * HALF_LAT * HALF_LON
WN = 4 * QUARTER
D = 512
CORNER = (HALF_LAT, HALF_LON, LEVELS, D)
HEADS = 16
HEAD_DIM = D // HEADS
FF = 2048
LANES = 128
PER_GROUP = LANES // HEAD_DIM
MASKED = -1e30
EPSILON = 1e-05
F32 = jnp.float32
BF16 = jnp.bfloat16
VMEM_LIMIT = 48 * 1024 * 1024

AXES = ("xl", "y", "xh", "z", "c")
SIZES = (2, 8, 2, 8, 2)
LAT = ("xl", "y")
LON = ("xh", "z", "c")


def place(lat, lon):
    return (lat % 16) * 32 + lon % 32


def shifted(dlat, dlon):
    return [(place(a, o), place(a + dlat, o + dlon)) for a in range(16) for o in range(32)]


def mirrored():
    def at(x, y, z, c):
        return (((x % 2) * 8 + y) * 2 + x // 2) * 16 + z * 2 + c

    return [
        (at(x, y, z, c), at(3 - x, y, z, c))
        for x in range(4)
        for y in range(8)
        for z in range(8)
        for c in range(2)
    ]


def to_quarters():
    hot = np.zeros((WN, LEVELS, WLAT, WLON), np.float32)
    place_of = 0
    for i in range(2):
        for j in range(2):
            for row in range(HALF_LAT):
                for col in range(HALF_LON):
                    for lev in range(LEVELS):
                        hot[place_of, lev, i * HALF_LAT + row, j * HALF_LON + col] = 1
                        place_of += 1
    return hot.reshape(WN, WN)


def normed(values, gain):
    average = jnp.mean(values, -1, keepdims=True)
    centered = values - average
    variance = jnp.mean(centered * centered, -1, keepdims=True)
    return centered * lax.rsqrt(variance + EPSILON) * gain


def dot(a, b):
    return jnp.dot(a, b, preferred_element_type=F32)


def dot_t(a, b):
    return lax.dot_general(a, b, (((1,), (1,)), ((), ())), preferred_element_type=F32)


def stacked(quarter_refs):
    return jnp.concatenate([q[...].astype(F32).reshape(QUARTER, D) for q in quarter_refs], 0)


def project(rows, weight_ref):
    first = weight_ref[:, 0].reshape(D // 2, D)
    second = weight_ref[:, 1].reshape(D // 2, D)
    return dot(rows[:, : D // 2], first) + dot(rows[:, D // 2 :], second)


def bias_kernel(edge_ref, hot_ref, bias_ref, out_ref):
    moved = dot(hot_ref[...], bias_ref[0]).astype(BF16)
    moved = dot_t(moved, hot_ref[...])
    upper_q = lax.broadcasted_iota(jnp.int32, (WN, WN), 0) < WN // 2
    upper_k = lax.broadcasted_iota(jnp.int32, (WN, WN), 1) < WN // 2
    apart = jnp.logical_and(upper_q != upper_k, edge_ref[0] == 1)
    out_ref[0] = jnp.where(apart, MASKED, moved).astype(BF16)


def attention_kernel(
    r0, r1, r2, r3, wq, wk, wv, wp, bias_ref, gain_ref, o0, o1, o2, o3
):
    cells = stacked((r0, r1, r2, r3))
    rows = cells.astype(BF16)
    queries = project(rows, wq).astype(BF16)
    keys = project(rows, wk).astype(BF16)
    values = project(rows, wv).astype(BF16)
    lane_head = lax.broadcasted_iota(jnp.int32, (1, LANES), 1) // HEAD_DIM
    zero = jnp.zeros((), BF16)
    groups = []
    for group in range(HEADS // PER_GROUP):
        lanes = slice(group * LANES, (group + 1) * LANES)
        group_q, group_k, group_v = queries[:, lanes], keys[:, lanes], values[:, lanes]
        total = None
        for j in range(PER_GROUP):
            mine = lane_head == j
            head_q = jnp.where(mine, group_q, zero)
            scores = dot_t(head_q, group_k) * HEAD_DIM ** (-0.5)
            scores = scores + bias_ref[group * PER_GROUP + j].astype(F32)
            weights = jnp.exp(scores - jnp.max(scores, -1, keepdims=True))
            weights = weights * (1.0 / jnp.sum(weights, -1, keepdims=True))
            part = dot(weights.astype(BF16), jnp.where(mine, group_v, zero))
            total = part if total is None else total + part
        groups.append(total.astype(BF16))
    projected = project(jnp.concatenate(groups, 1), wp)
    mixed = cells + normed(projected, gain_ref[...])
    for i, out in enumerate((o0, o1, o2, o3)):
        out[...] = mixed[i * QUARTER : (i + 1) * QUARTER].reshape(CORNER).astype(BF16)


def mlp_kernel(m0, m1, m2, m3, wu, wd, gain_ref, out_ref):
    cells = stacked((m0, m1, m2, m3))
    rows = cells.astype(BF16)
    lowered = None
    step = 4
    units = FF // 16 * step
    for i in range(0, 16, step):
        up = wu[i : i + step].reshape(units, D)
        down = wd[i : i + step].reshape(units, D)
        raised = dot_t(rows, up)
        hidden = 0.5 * raised * (1.0 + lax.erf(raised * (0.5**0.5)))
        part = dot(hidden.astype(BF16), down)
        lowered = part if lowered is None else lowered + part
    updated = cells + normed(lowered, gain_ref[...])
    run = HALF_LON * LEVELS
    for i in range(2):
        for j in range(2):
            for row in range(HALF_LAT):
                start = (i * 2 + j) * QUARTER + row * run
                piece = updated[start : start + run].reshape(HALF_LON, LEVELS, D)
                out_ref[i * HALF_LAT + row, j * HALF_LON : (j + 1) * HALF_LON] = piece.astype(BF16)


def whole(shape):
    return pl.BlockSpec(shape, lambda i: (0,) * len(shape))


def weight_block(rows, at):
    return pl.BlockSpec((16, 2, rows, D), lambda i: (0, 0, at, 0))


def params():
    return pltpu.CompilerParams(vmem_limit_bytes=VMEM_LIMIT)


def arranged_bias(position_bias, edge):
    one_head = pl.BlockSpec((1, WN, WN), lambda h: (h, 0, 0))
    return pl.pallas_call(
        bias_kernel,
        grid=(HEADS,),
        in_specs=[
            pl.BlockSpec(memory_space=pltpu.SMEM),
            pl.BlockSpec((WN, WN), lambda h: (0, 0)),
            one_head,
        ],
        out_specs=one_head,
        out_shape=jax.ShapeDtypeStruct(position_bias.shape, BF16),
        compiler_params=params(),
        name="bias",
    )(edge, jnp.asarray(to_quarters(), BF16), position_bias)


def attention(quarters, gathered, bias, gain):
    quarter = whole(CORNER)
    return pl.pallas_call(
        attention_kernel,
        grid=(1,),
        in_specs=[quarter] * 4
        + [weight_block(16, i) for i in range(4)]
        + [whole((HEADS, WN, WN)), whole((1, D))],
        out_specs=[quarter] * 4,
        out_shape=[jax.ShapeDtypeStruct(CORNER, BF16)] * 4,
        compiler_params=params(),
        name="attention",
    )(*quarters, gathered, gathered, gathered, gathered, bias, gain.reshape(1, D))


def feed_forward(quarters, gathered, gain):
    quarter = whole(CORNER)
    out = (WLAT, WLON, LEVELS, D)
    return pl.pallas_call(
        mlp_kernel,
        grid=(1,),
        in_specs=[quarter] * 4
        + [weight_block(64, i) for i in (1, 2)]
        + [whole((1, D))],
        out_specs=whole(out),
        out_shape=jax.ShapeDtypeStruct(out, BF16),
        compiler_params=params(),
        name="mlp",
    )(*quarters, gathered, gathered, gain.reshape(1, D))


def shards(
    latent, qkv_weight, proj_weight, position_bias, attn_gain, up_weight, down_weight, mlp_gain
):
    own = jnp.concatenate(
        [qkv_weight[:, i * D : (i + 1) * D] for i in range(3)]
        + [proj_weight, up_weight, down_weight],
        0,
    )
    other = lax.ppermute(own, AXES, mirrored())
    low_half = lax.axis_index("xh") == 0
    both = jnp.stack([jnp.where(low_half, own, other), jnp.where(low_half, other, own)])
    gathered = lax.all_gather(both, ("z", "c"), axis=0, tiled=False)

    cells = latent.transpose(1, 2, 0, 3)

    def corner(i, j):
        return cells[i * HALF_LAT : (i + 1) * HALF_LAT, j * HALF_LON : (j + 1) * HALF_LON]

    rolled = [
        lax.ppermute(corner(1, 1), AXES, shifted(1, 1)),
        lax.ppermute(corner(1, 0), AXES, shifted(1, 0)),
        lax.ppermute(corner(0, 1), AXES, shifted(0, 1)),
        corner(0, 0),
    ]
    edge = (lax.axis_index(LAT) == 0).astype(jnp.int32).reshape(1)
    bias = arranged_bias(position_bias, edge)
    mixed = attention(rolled, gathered, bias, attn_gain)
    restored = [
        mixed[3],
        lax.ppermute(mixed[2], AXES, shifted(0, -1)),
        lax.ppermute(mixed[1], AXES, shifted(-1, 0)),
        lax.ppermute(mixed[0], AXES, shifted(-1, -1)),
    ]
    return feed_forward(restored, gathered, mlp_gain).transpose(2, 0, 1, 3)


def solution(mesh):
    mesh = Mesh(mesh.devices.reshape(SIZES), AXES)
    placed = (
        P(None, LAT, LON, None),
        P(LON, None),
        P(LON, None),
        P(),
        P(),
        P(LON, None),
        P(LON, None),
        P(),
    )
    return jax.shard_map(
        shards, mesh=mesh, in_specs=placed, out_specs=P(None, LAT, LON, None), check_vma=False
    )
```

time: 289 us -> 115 us (0.40)
  waiting for transfers between devices: 164 us -> 32.9 us
  blocking collectives: 52.8 us -> 0 us
  Pallas kernels: 0 us -> 26 us
  matrix products: 24.4 us -> 0 us
  starting transfers between devices: 13.6 us -> 32.3 us
  local copies, waits for them, and re-layouts: 18.9 us -> 8.17 us
    all_gather x3 -> x1, waiting for transfers between devices: 153 us -> 28.1 us  [shards(): gathered = lax.all_gather(both, ('z', 'c'), axis=0, tiled=False)]
    all_gather x1 -> x0, blocking collectives: 52.8 us -> none  [shards(): lax.all_gather(proj_weight, 'lon', axis=0, tiled=True)]
    pallas_call x0 -> x3, Pallas kernels: none -> 26 us  [the longest x1 12.6 us: arranged_bias(): pl.pallas_call(bias_kernel, grid=(HEADS,), in_specs=[pl.BlockSpec(memory_...]
    ppermute x4 -> x7, starting transfers between devices: 13.6 us -> 32.3 us  [the longest x1 6.86 us: shards(): lax.ppermute(corner(0, 1), AXES, shifted(0, 1))]
    dot_general x4 -> x0, matrix products: 16 us -> none  [the longest x1 8.36 us: shards(): lowered = jnp.dot(hidden, full_down, preferred_element_type=jnp.float32)]
    sub x1 -> x0, matrix products: 8.42 us -> none  [attend(): weights = jnp.exp(scores - row_max)]
    reshape x8 -> x0, local copies, waits for them, and re-layouts: 7.04 us -> none  [the longest x2 4.69 us: attend(): packed.reshape(levels, lat_bands, WLAT, strips, WLON, 3, head_count, head...]
    ppermute x4 -> x7, waiting for transfers between devices: 9.31 us -> 4.8 us  [the longest x1 3.04 us: shards(): other = lax.ppermute(own, AXES, mirrored())]
  transfers between devices with their start and end apart: 7 -> 8, of which waited for: 6 -> 3; matrix products, arithmetic and copies ran while one was open for 12% -> 2% of each run, Pallas kernels for 0% -> 11%
where the time goes in v1:
time: 115 us; the launch traced here: 114 us
  waiting for transfers between devices  32.9 us (29%)
  starting transfers between devices  32.3 us (28%)
  Pallas kernels  26 us (23%)
  between operations  13.5 us (12%)
  local copies, waits for them, and re-layouts  8.17 us (7%)
    all_gather x1, waiting for transfers between devices, shards(): gathered = lax.all_gather(both, ('z', 'c'), axis=0, tiled=False)  28.1 us
    pallas_call x1, Pallas kernels, arranged_bias(): pl.pallas_call(bias_kernel, grid=(HEADS,), in_specs=[pl.BlockSpec(memory_...  12.6 us
    pallas_call x1, Pallas kernels, attention(): pl.pallas_call(attention_kernel, grid=(1,), in_specs=[quarter] * 4 + [wei...  8.45 us
    ppermute x1, starting transfers between devices, shards(): lax.ppermute(corner(0, 1), AXES, shifted(0, 1))  6.86 us
    ppermute x1, starting transfers between devices, shards(): lax.ppermute(mixed[0], AXES, shifted(-1, -1))  6.26 us
    unnamed x13, local copies, waits for them, and re-layouts  5.54 us
    ppermute x1, starting transfers between devices, shards(): lax.ppermute(mixed[1], AXES, shifted(-1, 0))  5.35 us
    ppermute x1, starting transfers between devices, shards(): other = lax.ppermute(own, AXES, mirrored())  5.2 us
  transfers between devices with their start and end apart: 8, of which 3 were waited for; matrix products, arithmetic and copies ran while one was open for 2% of the time, Pallas kernels for 11%

profile of v1, /device:TPU:1, one launch (start us, length us, event | category | flops | bytes accessed | tf_op | source)
XLA Modules:
  0.0 113.7 jit_solution(7890439571796366644)
XLA Ops:
  6.5 0.0 all-gather.3.cloned.1.call-start
  6.5 0.7 slice_dynamic-update-slice_fusion.2
  7.3 0.7 slice_dynamic-update-slice_fusion.1
  8.0 0.7 slice_dynamic-update-slice_fusion
  8.7 0.7 constant_dynamic-update-slice_fusion.2
  9.4 0.8 constant_dynamic-update-slice_fusion.1
  10.3 0.8 constant_dynamic-update-slice_fusion
  11.1 5.2 %collective-permute-start.3 = (bf16[192,512]{1,0:T(8,128)(2,1)S(1)}, bf16[192,512]{1,0:T(8,128)(2,1)S(1)}, u32[]{:S(2)}, u32[]{:S(2)}) collective-permute-start(bf16[192,512]{1,0:T(8,128)(2,1)S(1)} %constant_dynamic-update-slice_fusion), channel_id=1, source_target_pairs={{0,272},{1,273},{2,274},{3,275},{4,276},{5,277},{6,278},{7,279},{8... | collective-permute-start | bytes 589832 | tf_op jit(solution)/shard_map/ppermute | solution.py:225
  16.3 3.0 %collective-permute-done.3 = bf16[192,512]{1,0:T(8,128)(2,1)S(1)} collective-permute-done((bf16[192,512]{1,0:T(8,128)(2,1)S(1)}, bf16[192,512]{1,0:T(8,128)(2,1)S(1)}, u32[]{:S(2)}, u32[]{:S(2)}) %collective-permute-start.3) | collective-permute-done | bytes 196640 | tf_op jit(solution)/shard_map/ppermute | solution.py:225
  19.4 0.8 pad_maximum_fusion
  20.2 0.0 all-gather.3.cloned.1.call-update
  20.2 1.8 %fusion = (bf16[3,6,4,512]{3,2,1,0:T(4,128)(2,1)}, bf16[3,6,4,512]{3,2,1,0:T(4,128)(2,1)}, bf16[3,6,4,512]{3,2,1,0:T(4,128)(2,1)}, bf16[3,6,4,512]{3,2,1,0:T(4,128)(2,1)}) fusion(bf16[6,12,4,512]{3,2,1,0:T(4,128)(2,1)} %bitcast.18), kind=kLoop, calls=%fused_computation.9 | loop fusion | bytes 589824 | tf_op jit(solution)/shard_map/slice | solution.py:233
  22.0 6.9 %collective-permute-start.2 = (bf16[3,6,4,512]{3,2,1,0:T(4,128)(2,1)}, bf16[3,6,4,512]{3,2,1,0:T(4,128)(2,1)}, u32[]{:S(2)}, u32[]{:S(2)}) collective-permute-start(bf16[3,6,4,512]{3,2,1,0:T(4,128)(2,1)} %get-tuple-element.16), channel_id=1, source_target_pairs={{0,1},{1,2},{2,3},{3,4},{4,5},{5,6},{6,7},{7,8},{8,9},{9,10},{10,1... | collective-permute-start | bytes 221192 | tf_op jit(solution)/shard_map/ppermute | solution.py:238
  28.9 3.2 %collective-permute-start.1 = (bf16[3,6,4,512]{3,2,1,0:T(4,128)(2,1)}, bf16[3,6,4,512]{3,2,1,0:T(4,128)(2,1)}, u32[]{:S(2)}, u32[]{:S(2)}) collective-permute-start(bf16[3,6,4,512]{3,2,1,0:T(4,128)(2,1)} %get-tuple-element.17), channel_id=1, source_target_pairs={{0,32},{1,33},{2,34},{3,35},{4,36},{5,37},{6,38},{7,39},{8,40},{9,... | collective-permute-start | bytes 221192 | tf_op jit(solution)/shard_map/ppermute | solution.py:237
  32.1 3.2 %collective-permute-start = (bf16[3,6,4,512]{3,2,1,0:T(4,128)(2,1)}, bf16[3,6,4,512]{3,2,1,0:T(4,128)(2,1)}, u32[]{:S(2)}, u32[]{:S(2)}) collective-permute-start(bf16[3,6,4,512]{3,2,1,0:T(4,128)(2,1)} %get-tuple-element.18), channel_id=1, source_target_pairs={{0,33},{1,34},{2,35},{3,36},{4,37},{5,38},{6,39},{7,40},{8,41},{9,... | collective-permute-start | bytes 221192 | tf_op jit(solution)/shard_map/ppermute | solution.py:236
  35.3 0.0 copy-start.1
  35.3 0.9 copy-done.1
  36.3 12.6 %bias.1.bias_ref = bf16[16,288,288]{2,1,0:T(8,128)(2,1)S(1)} custom-call(s32[1]{0:T(128)} %bitcast.4.edge_ref, bf16[288,288]{1,0:T(8,128)(2,1)S(1)} %copy-done.1, bf16[16,288,288]{2,1,0:T(8,128)(2,1)} %bias_ref.1), custom_call_target="tpu_custom_call" | custom-call | tf_op jit(solution)/shard_map/bias/pallas_call | solution.py:171
  48.8 0.0 collective-permute-done.2.r2
  48.9 0.0 collective-permute-done.1.r1
  48.9 0.0 collective-permute-done.r0
  48.9 28.1 %all-gather.3.cloned.1.call-done = bf16[32,192,512]{2,1,0:T(8,128)(2,1)} async-done(((bf16[2,192,512]{2,1,0:T(8,128)(2,1)}), bf16[32,192,512]{2,1,0:T(8,128)(2,1)}) %all-gather.3.cloned.1.call-update) | async-done | bytes 6291472 | tf_op jit(solution)/shard_map/all_gather | solution.py:228
  77.0 0.0 copy-done.2
  77.0 0.9 copy-done
  77.9 8.5 %attention.1 = (bf16[3,6,4,512]{3,2,1,0:T(4,128)(2,1)S(1)}, bf16[3,6,4,512]{3,2,1,0:T(4,128)(2,1)S(1)}, bf16[3,6,4,512]{3,2,1,0:T(4,128)(2,1)S(1)}, bf16[3,6,4,512]{3,2,1,0:T(4,128)(2,1)S(1)}) custom-call(bf16[3,6,4,512]{3,2,1,0:T(4,128)(2,1)} %collective-permute-done.r0, bf16[3,6,4,512]{3,2,1,0:T(4,128)(2,1)} %collective-permute-done.1.r1, ...), custom_call_target="tpu_custom_call" | custom-call | tf_op jit(solution)/shard_map/attention/pallas_call | solution.py:188
  86.3 2.2 %collective-permute-start.4 = (bf16[3,6,4,512]{3,2,1,0:T(4,128)(2,1)S(1)}, bf16[3,6,4,512]{3,2,1,0:T(4,128)(2,1)S(1)}, u32[]{:S(2)}, u32[]{:S(2)}) collective-permute-start(bf16[3,6,4,512]{3,2,1,0:T(4,128)(2,1)S(1)} %get-tuple-element.10), channel_id=1, source_target_pairs={{0,31},{1,0},{2,1},{3,2},{4,3},{5,4},{6,5},{7,6},{8,7},{9,8},{10,9... | collective-permute-start | bytes 221192 | tf_op jit(solution)/shard_map/ppermute | solution.py:246
  88.5 5.4 %collective-permute-start.5 = (bf16[3,6,4,512]{3,2,1,0:T(4,128)(2,1)S(1)}, bf16[3,6,4,512]{3,2,1,0:T(4,128)(2,1)S(1)}, u32[]{:S(2)}, u32[]{:S(2)}) collective-permute-start(bf16[3,6,4,512]{3,2,1,0:T(4,128)(2,1)S(1)} %get-tuple-element.11), channel_id=1, source_target_pairs={{0,480},{1,481},{2,482},{3,483},{4,484},{5,485},{6,486},{7,487},{8... | collective-permute-start | bytes 221192 | tf_op jit(solution)/shard_map/ppermute | solution.py:247
  93.9 6.3 %collective-permute-start.6 = (bf16[3,6,4,512]{3,2,1,0:T(4,128)(2,1)S(1)}, bf16[3,6,4,512]{3,2,1,0:T(4,128)(2,1)S(1)}, u32[]{:S(2)}, u32[]{:S(2)}) collective-permute-start(bf16[3,6,4,512]{3,2,1,0:T(4,128)(2,1)S(1)} %get-tuple-element.12), channel_id=1, source_target_pairs={{0,511},{1,480},{2,481},{3,482},{4,483},{5,484},{6,485},{7,486},{8... | collective-permute-start | bytes 221192 | tf_op jit(solution)/shard_map/ppermute | solution.py:248
  100.1 0.0 collective-permute-done.4.m1
  100.1 0.0 collective-permute-done.5.m2
  100.1 1.8 %collective-permute-done.6.m3 = bf16[3,6,4,512]{3,2,1,0:T(4,128)(2,1)S(1)} collective-permute-done((bf16[3,6,4,512]{3,2,1,0:T(4,128)(2,1)S(1)}, bf16[3,6,4,512]{3,2,1,0:T(4,128)(2,1)S(1)}, u32[]{:S(2)}, u32[]{:S(2)}) %collective-permute-start.6) | collective-permute-done | bytes 73760 | tf_op jit(solution)/shard_map/ppermute | solution.py:248
  101.9 4.9 %mlp.1 = bf16[6,12,4,512]{3,2,1,0:T(4,128)(2,1)} custom-call(bf16[3,6,4,512]{3,2,1,0:T(4,128)(2,1)S(1)} %get-tuple-element.9.m0, bf16[3,6,4,512]{3,2,1,0:T(4,128)(2,1)S(1)} %collective-permute-done.4.m1, bf16[3,6,4,512]{3,2,1,0:T(4,128)(2,1)S(1)} %collective-permute-done.5.m2, bf16[3,6,4,512]{3,2,1,0:T(4,128)(2,1)S(1)} %collective-permute-done.6.m3, ...), custom_call_target="tpu_custom_call" | custom-call | tf_op jit(solution)/shard_map/mlp/pallas_call | solution.py:204
  (5 shorter events, 0.0 us)
Async XLA Ops:
  6.5 70.4 %all-gather.3.cloned.1.call-start = ((), (), s32[]{:S(2)}) async-start(), calls=%async_computation | async-start | bytes 6684672 | tf_op jit(solution)/shard_map/all_gather | solution.py:228
  11.1 8.3 %collective-permute-start.3 = (bf16[192,512]{1,0:T(8,128)(2,1)S(1)}, bf16[192,512]{1,0:T(8,128)(2,1)S(1)}, u32[]{:S(2)}, u32[]{:S(2)}) collective-permute-start(bf16[192,512]{1,0:T(8,128)(2,1)S(1)} %constant_dynamic-update-slice_fusion), channel_id=1, source_target_pairs={{0,272},{1,273},{2,274},{3,275},{4,276},{5,277},{6,278},{7,279},{8... | collective-permute-start | bytes 589832 | tf_op jit(solution)/shard_map/ppermute | solution.py:225
  22.0 26.8 %collective-permute-start.2 = (bf16[3,6,4,512]{3,2,1,0:T(4,128)(2,1)}, bf16[3,6,4,512]{3,2,1,0:T(4,128)(2,1)}, u32[]{:S(2)}, u32[]{:S(2)}) collective-permute-start(bf16[3,6,4,512]{3,2,1,0:T(4,128)(2,1)} %get-tuple-element.16), channel_id=1, source_target_pairs={{0,1},{1,2},{2,3},{3,4},{4,5},{5,6},{6,7},{7,8},{8,9},{9,10},{10,1... | collective-permute-start | bytes 221192 | tf_op jit(solution)/shard_map/ppermute | solution.py:238
  28.9 20.0 %collective-permute-start.1 = (bf16[3,6,4,512]{3,2,1,0:T(4,128)(2,1)}, bf16[3,6,4,512]{3,2,1,0:T(4,128)(2,1)}, u32[]{:S(2)}, u32[]{:S(2)}) collective-permute-start(bf16[3,6,4,512]{3,2,1,0:T(4,128)(2,1)} %get-tuple-element.17), channel_id=1, source_target_pairs={{0,32},{1,33},{2,34},{3,35},{4,36},{5,37},{6,38},{7,39},{8,40},{9,... | collective-permute-start | bytes 221192 | tf_op jit(solution)/shard_map/ppermute | solution.py:237
  32.1 16.8 %collective-permute-start = (bf16[3,6,4,512]{3,2,1,0:T(4,128)(2,1)}, bf16[3,6,4,512]{3,2,1,0:T(4,128)(2,1)}, u32[]{:S(2)}, u32[]{:S(2)}) collective-permute-start(bf16[3,6,4,512]{3,2,1,0:T(4,128)(2,1)} %get-tuple-element.18), channel_id=1, source_target_pairs={{0,33},{1,34},{2,35},{3,36},{4,37},{5,38},{6,39},{7,40},{8,41},{9,... | collective-permute-start | bytes 221192 | tf_op jit(solution)/shard_map/ppermute | solution.py:236
  35.3 0.9 copy-start.1
  36.2 40.7 %copy-start.2 = (f32[512]{0:T(512)S(1)}, f32[512]{0:T(512)}, u32[]{:S(2)}) copy-start(f32[512]{0:T(512)} %param.13) | copy-start | bytes 6148
  77.0 0.9 copy-start
  77.8 24.1 %copy-start.3 = (f32[512]{0:T(512)S(1)}, f32[512]{0:T(512)}, u32[]{:S(2)}) copy-start(f32[512]{0:T(512)} %param.16) | copy-start | bytes 6148
  86.3 13.8 %collective-permute-start.4 = (bf16[3,6,4,512]{3,2,1,0:T(4,128)(2,1)S(1)}, bf16[3,6,4,512]{3,2,1,0:T(4,128)(2,1)S(1)}, u32[]{:S(2)}, u32[]{:S(2)}) collective-permute-start(bf16[3,6,4,512]{3,2,1,0:T(4,128)(2,1)S(1)} %get-tuple-element.10), channel_id=1, source_target_pairs={{0,31},{1,0},{2,1},{3,2},{4,3},{5,4},{6,5},{7,6},{8,7},{9,8},{10,9... | collective-permute-start | bytes 221192 | tf_op jit(solution)/shard_map/ppermute | solution.py:246
  88.5 11.6 %collective-permute-start.5 = (bf16[3,6,4,512]{3,2,1,0:T(4,128)(2,1)S(1)}, bf16[3,6,4,512]{3,2,1,0:T(4,128)(2,1)S(1)}, u32[]{:S(2)}, u32[]{:S(2)}) collective-permute-start(bf16[3,6,4,512]{3,2,1,0:T(4,128)(2,1)S(1)} %get-tuple-element.11), channel_id=1, source_target_pairs={{0,480},{1,481},{2,482},{3,483},{4,484},{5,485},{6,486},{7,487},{8... | collective-permute-start | bytes 221192 | tf_op jit(solution)/shard_map/ppermute | solution.py:247
  93.9 8.0 %collective-permute-start.6 = (bf16[3,6,4,512]{3,2,1,0:T(4,128)(2,1)S(1)}, bf16[3,6,4,512]{3,2,1,0:T(4,128)(2,1)S(1)}, u32[]{:S(2)}, u32[]{:S(2)}) collective-permute-start(bf16[3,6,4,512]{3,2,1,0:T(4,128)(2,1)S(1)} %get-tuple-element.12), channel_id=1, source_target_pairs={{0,511},{1,480},{2,481},{3,482},{4,483},{5,484},{6,485},{7,486},{8... | collective-permute-start | bytes 221192 | tf_op jit(solution)/shard_map/ppermute | solution.py:248
Sparse Core Ops, SparseCore 0:
  20.3 56.5 all-gather.2

commit v2 on v1

v2 whole, which is shorter than its diff:
```python
import jax
import jax.numpy as jnp
import numpy as np
from jax import lax
from jax.experimental import pallas as pl
from jax.experimental.pallas import tpu as pltpu
from jax.sharding import Mesh, PartitionSpec as P

WLAT = 6
WLON = 12
LEVELS = 4
HALF_LAT = WLAT // 2
HALF_LON = WLON // 2
QUARTER = LEVELS * HALF_LAT * HALF_LON
WN = 4 * QUARTER
D = 512
CORNER = (HALF_LAT, HALF_LON, LEVELS, D)
HEADS = 16
HEAD_DIM = D // HEADS
FF = 2048
LANES = 128
PER_GROUP = LANES // HEAD_DIM
MASKED = -1e30
EPSILON = 1e-05
F32 = jnp.float32
BF16 = jnp.bfloat16
VMEM_LIMIT = 48 * 1024 * 1024

AXES = ("xl", "y", "xh", "z", "c")
SIZES = (2, 8, 2, 8, 2)
LAT = ("xl", "y")
LON = ("xh", "z", "c")


def place(lat, lon):
    return (lat % 16) * 32 + lon % 32


def shifted(dlat, dlon):
    return [(place(a, o), place(a + dlat, o + dlon)) for a in range(16) for o in range(32)]


def mirrored():
    def at(x, y, z, c):
        return (((x % 2) * 8 + y) * 2 + x // 2) * 16 + z * 2 + c

    return [
        (at(x, y, z, c), at(3 - x, y, z, c))
        for x in range(4)
        for y in range(8)
        for z in range(8)
        for c in range(2)
    ]


def swapped():
    return [(d, d ^ 1) for d in range(512)]


def to_quarters():
    hot = np.zeros((WN, LEVELS, WLAT, WLON), np.float32)
    place_of = 0
    for i in range(2):
        for j in range(2):
            for row in range(HALF_LAT):
                for col in range(HALF_LON):
                    for lev in range(LEVELS):
                        hot[place_of, lev, i * HALF_LAT + row, j * HALF_LON + col] = 1
                        place_of += 1
    return hot.reshape(WN, WN)


def apart():
    upper = np.arange(WN) // WLON % WLAT < HALF_LAT
    return np.where(upper[:, None] != upper[None], MASKED, 0.0).astype(np.float32)


def normed(values, gain):
    average = jnp.mean(values, -1, keepdims=True)
    centered = values - average
    variance = jnp.mean(centered * centered, -1, keepdims=True)
    return centered * lax.rsqrt(variance + EPSILON) * gain


def dot(a, b):
    return jnp.dot(a, b, preferred_element_type=F32)


def dot_t(a, b):
    return lax.dot_general(a, b, (((1,), (1,)), ((), ())), preferred_element_type=F32)


def stacked(quarters):
    return jnp.concatenate([q.astype(F32).reshape(QUARTER, D) for q in quarters], 0)


def corner(cells, i, j):
    return cells[i * HALF_LAT : (i + 1) * HALF_LAT, j * HALF_LON : (j + 1) * HALF_LON]


def pack_kernel(qkv_ref, proj_ref, up_ref, down_ref, out_ref):
    for i in range(3):
        out_ref[i * 16 : (i + 1) * 16] = qkv_ref[:, i * D : (i + 1) * D]
    out_ref[48:112] = up_ref[...]
    out_ref[112:176] = down_ref[...]
    out_ref[176:192] = proj_ref[...]


def attention_kernel(
    spot_ref, r0, r1, r2, r3, mine_ref, other_ref, bias_ref, hot_ref, away_ref, o0, o1, o2, o3
):
    hot = hot_ref[...]
    rows = stacked([r[...] for r in (r0, r1, r2, r3)]).astype(BF16)
    rows = lax.dot_general(hot, rows, (((0,), (0,)), ((), ())), preferred_element_type=F32)
    rows = rows.astype(BF16)
    first_core = spot_ref[0] == 0
    away = jnp.where(spot_ref[1] == 1, away_ref[...], 0.0)

    def projected(which):
        total = None
        for half in range(2):
            mine, other = mine_ref[:, half, which], other_ref[:, half, which]
            even = jnp.where(first_core, mine, other)
            odd = jnp.where(first_core, other, mine)
            weight = jnp.stack([even, odd], 1).reshape(D // 2, D)
            part = dot(rows[:, half * (D // 2) : (half + 1) * (D // 2)], weight)
            total = part if total is None else total + part
        return total.astype(BF16)

    queries, keys, values = projected(0), projected(1), projected(2)
    lane_head = lax.broadcasted_iota(jnp.int32, (1, LANES), 1) // HEAD_DIM
    zero = jnp.zeros((), BF16)
    groups = []
    for group in range(HEADS // PER_GROUP):
        lanes = slice(group * LANES, (group + 1) * LANES)
        group_q, group_k, group_v = queries[:, lanes], keys[:, lanes], values[:, lanes]
        total = None
        for j in range(PER_GROUP):
            mine = lane_head == j
            head_q = jnp.where(mine, group_q, zero)
            scores = dot_t(head_q, group_k) * HEAD_DIM ** (-0.5)
            scores = scores + bias_ref[group * PER_GROUP + j].astype(F32) + away
            weights = jnp.exp(scores - jnp.max(scores, -1, keepdims=True))
            weights = weights * (1.0 / jnp.sum(weights, -1, keepdims=True))
            part = dot(weights.astype(BF16), jnp.where(mine, group_v, zero))
            total = part if total is None else total + part
        groups.append(total.astype(BF16))
    attended = dot(hot, jnp.concatenate(groups, 1))
    for i, out in enumerate((o0, o1, o2, o3)):
        out[...] = attended[i * QUARTER : (i + 1) * QUARTER].reshape(CORNER).astype(BF16)


def token_kernel(m0, m1, m2, m3, cells_ref, wp, wu, wd, attn_gain_ref, mlp_gain_ref, out_ref):
    attended = stacked([m[...] for m in (m0, m1, m2, m3)]).astype(BF16)
    cells = stacked([corner(cells_ref, i, j) for i in range(2) for j in range(2)])
    projected = dot(attended[:, : D // 2], wp[:, 0].reshape(D // 2, D)) + dot(
        attended[:, D // 2 :], wp[:, 1].reshape(D // 2, D)
    )
    rows = (cells + normed(projected, attn_gain_ref[...])).astype(BF16)
    lowered = None
    step = 4
    units = FF // 16 * step
    for i in range(0, 16, step):
        up = wu[i : i + step].reshape(units, D)
        down = wd[i : i + step].reshape(units, D)
        raised = dot_t(rows, up)
        hidden = 0.5 * raised * (1.0 + lax.erf(raised * (0.5**0.5)))
        part = dot(hidden.astype(BF16), down)
        lowered = part if lowered is None else lowered + part
    updated = rows.astype(F32) + normed(lowered, mlp_gain_ref[...])
    run = HALF_LON * LEVELS
    for i in range(2):
        for j in range(2):
            for row in range(HALF_LAT):
                start = (i * 2 + j) * QUARTER + row * run
                piece = updated[start : start + run].reshape(HALF_LON, LEVELS, D)
                out_ref[i * HALF_LAT + row, j * HALF_LON : (j + 1) * HALF_LON] = piece.astype(BF16)


def whole(shape):
    return pl.BlockSpec(shape, lambda i: (0,) * len(shape))


def weight_block(rows, at):
    return pl.BlockSpec((16, 2, rows, D), lambda i: (0, 0, at, 0))


def scalars():
    return pl.BlockSpec(memory_space=pltpu.SMEM)


def params():
    return pltpu.CompilerParams(vmem_limit_bytes=VMEM_LIMIT)


def packed(qkv_weight, proj_weight, up_weight, down_weight):
    weights = (qkv_weight, proj_weight, up_weight, down_weight)
    return pl.pallas_call(
        pack_kernel,
        grid=(1,),
        in_specs=[whole(w.shape) for w in weights],
        out_specs=whole((192, D)),
        out_shape=jax.ShapeDtypeStruct((192, D), BF16),
        compiler_params=params(),
        name="pack",
    )(*weights)


def attention(spot, quarters, mine, other, bias):
    quarter = whole(CORNER)
    weight = whole(mine.shape)
    return pl.pallas_call(
        attention_kernel,
        grid=(1,),
        in_specs=[scalars()]
        + [quarter] * 4
        + [weight] * 2
        + [whole(bias.shape), whole((WN, WN)), whole((WN, WN))],
        out_specs=[quarter] * 4,
        out_shape=[jax.ShapeDtypeStruct(CORNER, BF16)] * 4,
        compiler_params=params(),
        name="attention",
    )(spot, *quarters, mine, other, bias, jnp.asarray(to_quarters(), BF16), jnp.asarray(apart()))


def tokens(quarters, cells, gathered, attn_gain, mlp_gain):
    quarter = whole(CORNER)
    out = (WLAT, WLON, LEVELS, D)
    return pl.pallas_call(
        token_kernel,
        grid=(1,),
        in_specs=[quarter] * 4
        + [whole(out), weight_block(16, 8), weight_block(64, 0), weight_block(64, 1)]
        + [whole((1, D))] * 2,
        out_specs=whole(out),
        out_shape=jax.ShapeDtypeStruct(out, BF16),
        compiler_params=params(),
        name="tokens",
    )(*quarters, cells, gathered, gathered, gathered, attn_gain.reshape(1, D), mlp_gain.reshape(1, D))


def shards(
    latent, qkv_weight, proj_weight, position_bias, attn_gain, up_weight, down_weight, mlp_gain
):
    own = packed(qkv_weight, proj_weight, up_weight, down_weight)
    other = lax.ppermute(own, AXES, mirrored())
    low_half = lax.axis_index("xh") == 0

    def halves(start, stop):
        ours, theirs = own[start:stop], other[start:stop]
        return jnp.stack([jnp.where(low_half, ours, theirs), jnp.where(low_half, theirs, ours)])

    gathered = lax.all_gather(halves(48, 192), ("z", "c"), axis=0, tiled=False)
    mine = lax.all_gather(halves(0, 48), "z", axis=0, tiled=False)
    theirs = lax.ppermute(mine, AXES, swapped())
    by_shard = (8, 2, 3, 16, D)

    cells = latent.transpose(1, 2, 0, 3)
    rolled = [
        lax.ppermute(corner(cells, 1, 1), AXES, shifted(1, 1)),
        lax.ppermute(corner(cells, 1, 0), AXES, shifted(1, 0)),
        lax.ppermute(corner(cells, 0, 1), AXES, shifted(0, 1)),
        corner(cells, 0, 0),
    ]
    spot = jnp.stack([lax.axis_index("c"), (lax.axis_index(LAT) == 0).astype(jnp.int32)])
    attended = attention(
        spot, rolled, mine.reshape(by_shard), theirs.reshape(by_shard), position_bias
    )
    restored = [
        attended[3],
        lax.ppermute(attended[2], AXES, shifted(0, -1)),
        lax.ppermute(attended[1], AXES, shifted(-1, 0)),
        lax.ppermute(attended[0], AXES, shifted(-1, -1)),
    ]
    return tokens(restored, cells, gathered, attn_gain, mlp_gain).transpose(2, 0, 1, 3)


def solution(mesh):
    mesh = Mesh(mesh.devices.reshape(SIZES), AXES)
    placed = (
        P(None, LAT, LON, None),
        P(LON, None),
        P(LON, None),
        P(),
        P(),
        P(LON, None),
        P(LON, None),
        P(),
    )
    return jax.shard_map(
        shards, mesh=mesh, in_specs=placed, out_specs=P(None, LAT, LON, None), check_vma=False
    )
```

time: 115 us -> 112 us (0.974)
  blocking collectives: 0 us -> 29.9 us
  waiting for transfers between devices: 32.9 us -> 8.85 us
  Pallas kernels: 26 us -> 12.1 us
  starting transfers between devices: 32.3 us -> 37.3 us
    all_gather x0 -> x1, blocking collectives: none -> 29.9 us  [shards(): mine = lax.all_gather(halves(0, 48), 'z', axis=0, tiled=False)]
    all_gather x1, waiting for transfers between devices: 28.1 us -> 0.01 us  [shards(): gathered = lax.all_gather(halves(48, 192), ('z', 'c'), axis=0, tiled=False)]
    pallas_call x3, Pallas kernels: 26 us -> 12.1 us  [the longest x1 8.96 us: attention(): pl.pallas_call(attention_kernel, grid=(1,), in_specs=[scalars()] + [quart...]
    ppermute x6 -> x7, starting transfers between devices: 27.1 us -> 32.1 us  [the longest x1 9.07 us: shards(): theirs = lax.ppermute(mine, AXES, swapped())]
    ppermute x6 -> x7, waiting for transfers between devices: 1.76 us -> 5.83 us  [the longest x1 3.62 us: shards(): lax.ppermute(attended[0], AXES, shifted(-1, -1))]
    unnamed x13 -> x20, local copies, waits for them, and re-layouts: 5.54 us -> 7.49 us
  transfers between devices with their start and end apart: 8 -> 9, of which waited for: 3 -> 3; matrix products, arithmetic and copies ran while one was open for 2% -> 1% of each run, Pallas kernels for 11% -> 8%
where the time goes in v2:
time: 112 us; the launch traced here: 111 us
  starting transfers between devices  37.3 us (33%)
  blocking collectives  29.9 us (27%)
  between operations  13.6 us (12%)
  Pallas kernels  12.1 us (11%)
  waiting for transfers between devices  8.85 us (8%)
  local copies, waits for them, and re-layouts  8.6 us (8%)
    all_gather x1, blocking collectives, shards(): mine = lax.all_gather(halves(0, 48), 'z', axis=0, tiled=False)  29.9 us
    ppermute x1, starting transfers between devices, shards(): theirs = lax.ppermute(mine, AXES, swapped())  9.07 us
    pallas_call x1, Pallas kernels, attention(): pl.pallas_call(attention_kernel, grid=(1,), in_specs=[scalars()] + [quart...  8.96 us
    unnamed x20, local copies, waits for them, and re-layouts  7.49 us
    ppermute x1, starting transfers between devices, shards(): lax.ppermute(attended[2], AXES, shifted(0, -1))  6.62 us
    ppermute x1, starting transfers between devices, shards(): other = lax.ppermute(own, AXES, mirrored())  5.22 us
    ppermute x1, starting transfers between devices, shards(): lax.ppermute(corner(cells, 1, 1), AXES, shifted(1, 1))  3.76 us
    ppermute x1, starting transfers between devices, shards(): lax.ppermute(attended[1], AXES, shifted(-1, 0))  3.74 us
  transfers between devices with their start and end apart: 9, of which 3 were waited for; matrix products, arithmetic and copies ran while one was open for 1% of the time, Pallas kernels for 8%

profile of v2, /device:TPU:1, one launch (start us, length us, event | category | flops | bytes accessed | tf_op | source)
XLA Modules:
  0.0 111.2 jit_solution(17539026900218981141)
XLA Ops:
  6.5 0.8 copy-done.4
  7.4 0.8 copy-done.5
  8.2 0.8 copy-done.6
  9.0 0.7 copy-done.7
  9.8 5.2 %collective-permute-start.3 = (bf16[192,512]{1,0:T(8,128)(2,1)S(1)}, bf16[192,512]{1,0:T(8,128)(2,1)S(1)}, u32[]{:S(2)}, u32[]{:S(2)}) collective-permute-start(bf16[192,512]{1,0:T(8,128)(2,1)S(1)} %pack.1), channel_id=1, source_target_pairs={{0,272},{1,273},{2,274},{3,275},{4,276},{5,277},{6,278},{7,279},{8... | collective-permute-start | bytes 589832 | tf_op jit(solution)/shard_map/ppermute | solution.py:246
  15.0 0.0 copy-start.1
  15.0 0.0 copy-start.8
  15.0 0.0 copy-start.9
  15.0 3.0 %collective-permute-done.3 = bf16[192,512]{1,0:T(8,128)(2,1)S(1)} collective-permute-done((bf16[192,512]{1,0:T(8,128)(2,1)S(1)}, bf16[192,512]{1,0:T(8,128)(2,1)S(1)}, u32[]{:S(2)}, u32[]{:S(2)}) %collective-permute-start.3) | collective-permute-done | bytes 196640 | tf_op jit(solution)/shard_map/ppermute | solution.py:246
  18.0 0.7 pad_maximum_fusion
  18.8 0.0 all-gather.4.cloned.1.call-update
  18.9 29.9 %all-gather = bf16[16,48,512]{2,1,0:T(8,128)(2,1)S(1)} all-gather(bf16[2,48,512]{2,1,0:T(8,128)(2,1)S(1)} %pad_maximum_fusion.1), channel_id=2, replica_groups=mesh['xl'=2,'y'=8,'xh'=2,'z'=8,'c'=2] {'z'}, dimensions={0}, use_global_device_ids=true | all-gather | bytes 884736 | tf_op jit(solution)/shard_map/all_gather | solution.py:254
  48.7 9.1 %collective-permute-start.4 = (bf16[8,2,48,512]{3,2,1,0:T(8,128)(2,1)S(1)}, bf16[8,2,48,512]{3,2,1,0:T(8,128)(2,1)S(1)}, u32[]{:S(2)}, u32[]{:S(2)}) collective-permute-start(bf16[8,2,48,512]{3,2,1,0:T(8,128)(2,1)S(1)} %bitcast.21), channel_id=1, source_target_pairs={{0,1},{1,0},{2,3},{3,2},{4,5},{5,4},{6,7},{7,6},{8,9},{9,8},{10,11... | collective-permute-start | bytes 2359304 | tf_op jit(solution)/shard_map/ppermute | solution.py:255
  57.8 1.1 %fusion = (bf16[3,6,4,512]{3,2,1,0:T(4,128)(2,1)S(1)}, bf16[3,6,4,512]{3,2,1,0:T(4,128)(2,1)S(1)}, bf16[3,6,4,512]{3,2,1,0:T(4,128)(2,1)S(1)}, bf16[3,6,4,512]{3,2,1,0:T(4,128)(2,1)S(1)}) fusion(bf16[6,12,4,512]{3,2,1,0:T(4,128)(2,1)} %bitcast.23), kind=kLoop, calls=%fused_computation.7 | loop fusion | bytes 589824 | tf_op jit(solution)/shard_map/slice | solution.py:98
  58.9 3.8 %collective-permute-start = (bf16[3,6,4,512]{3,2,1,0:T(4,128)(2,1)S(1)}, bf16[3,6,4,512]{3,2,1,0:T(4,128)(2,1)S(1)}, u32[]{:S(2)}, u32[]{:S(2)}) collective-permute-start(bf16[3,6,4,512]{3,2,1,0:T(4,128)(2,1)S(1)} %get-tuple-element.20), channel_id=1, source_target_pairs={{0,33},{1,34},{2,35},{3,36},{4,37},{5,38},{6,39},{7,40},{8,41},{9,... | collective-permute-start | bytes 221192 | tf_op jit(solution)/shard_map/ppermute | solution.py:260
  62.7 3.1 %collective-permute-start.1 = (bf16[3,6,4,512]{3,2,1,0:T(4,128)(2,1)S(1)}, bf16[3,6,4,512]{3,2,1,0:T(4,128)(2,1)S(1)}, u32[]{:S(2)}, u32[]{:S(2)}) collective-permute-start(bf16[3,6,4,512]{3,2,1,0:T(4,128)(2,1)S(1)} %get-tuple-element.19), channel_id=1, source_target_pairs={{0,32},{1,33},{2,34},{3,35},{4,36},{5,37},{6,38},{7,39},{8,40},{9,... | collective-permute-start | bytes 221192 | tf_op jit(solution)/shard_map/ppermute | solution.py:261
  65.8 2.9 %collective-permute-start.2 = (bf16[3,6,4,512]{3,2,1,0:T(4,128)(2,1)S(1)}, bf16[3,6,4,512]{3,2,1,0:T(4,128)(2,1)S(1)}, u32[]{:S(2)}, u32[]{:S(2)}) collective-permute-start(bf16[3,6,4,512]{3,2,1,0:T(4,128)(2,1)S(1)} %get-tuple-element.18), channel_id=1, source_target_pairs={{0,1},{1,2},{2,3},{3,4},{4,5},{5,6},{6,7},{7,8},{8,9},{9,10},{10,1... | collective-permute-start | bytes 221192 | tf_op jit(solution)/shard_map/ppermute | solution.py:262
  68.7 0.1 pad_add_fusion.spot_ref
  68.8 0.0 collective-permute-done.r0
  68.8 2.2 %collective-permute-done.1.r1 = bf16[3,6,4,512]{3,2,1,0:T(4,128)(2,1)S(1)} collective-permute-done((bf16[3,6,4,512]{3,2,1,0:T(4,128)(2,1)S(1)}, bf16[3,6,4,512]{3,2,1,0:T(4,128)(2,1)S(1)}, u32[]{:S(2)}, u32[]{:S(2)}) %collective-permute-start.1) | collective-permute-done | bytes 73760 | tf_op jit(solution)/shard_map/ppermute | solution.py:261
  71.0 0.0 collective-permute-done.2.r2
  71.0 1.0 copy-done.2
  72.0 0.9 copy-done.3
  72.9 9.0 %attention.1 = (bf16[3,6,4,512]{3,2,1,0:T(4,128)(2,1)S(1)}, bf16[3,6,4,512]{3,2,1,0:T(4,128)(2,1)S(1)}, bf16[3,6,4,512]{3,2,1,0:T(4,128)(2,1)S(1)}, bf16[3,6,4,512]{3,2,1,0:T(4,128)(2,1)S(1)}) custom-call(s32[2]{0:T(128)S(1)} %pad_add_fusion.spot_ref, bf16[3,6,4,512]{3,2,1,0:T(4,128)(2,1)S(1)} %collective-permute-done.r0, ...), custom_call_target="tpu_custom_call" | custom-call | tf_op jit(solution)/shard_map/attention/pallas_call | solution.py:212
  81.9 6.6 %collective-permute-start.5 = (bf16[3,6,4,512]{3,2,1,0:T(4,128)(2,1)S(1)}, bf16[3,6,4,512]{3,2,1,0:T(4,128)(2,1)S(1)}, u32[]{:S(2)}, u32[]{:S(2)}) collective-permute-start(bf16[3,6,4,512]{3,2,1,0:T(4,128)(2,1)S(1)} %get-tuple-element.10), channel_id=1, source_target_pairs={{0,31},{1,0},{2,1},{3,2},{4,3},{5,4},{6,5},{7,6},{8,7},{9,8},{10,9... | collective-permute-start | bytes 221192 | tf_op jit(solution)/shard_map/ppermute | solution.py:271
  88.5 3.7 %collective-permute-start.6 = (bf16[3,6,4,512]{3,2,1,0:T(4,128)(2,1)S(1)}, bf16[3,6,4,512]{3,2,1,0:T(4,128)(2,1)S(1)}, u32[]{:S(2)}, u32[]{:S(2)}) collective-permute-start(bf16[3,6,4,512]{3,2,1,0:T(4,128)(2,1)S(1)} %get-tuple-element.11), channel_id=1, source_target_pairs={{0,480},{1,481},{2,482},{3,483},{4,484},{5,485},{6,486},{7,487},{8... | collective-permute-start | bytes 221192 | tf_op jit(solution)/shard_map/ppermute | solution.py:272
  92.3 2.9 %collective-permute-start.7 = (bf16[3,6,4,512]{3,2,1,0:T(4,128)(2,1)S(1)}, bf16[3,6,4,512]{3,2,1,0:T(4,128)(2,1)S(1)}, u32[]{:S(2)}, u32[]{:S(2)}) collective-permute-start(bf16[3,6,4,512]{3,2,1,0:T(4,128)(2,1)S(1)} %get-tuple-element.12), channel_id=1, source_target_pairs={{0,511},{1,480},{2,481},{3,482},{4,483},{5,484},{6,485},{7,486},{8... | collective-permute-start | bytes 221192 | tf_op jit(solution)/shard_map/ppermute | solution.py:273
  95.2 0.0 collective-permute-done.5.m1
  95.2 0.0 collective-permute-done.6.m2
  95.2 3.6 %collective-permute-done.7.m3 = bf16[3,6,4,512]{3,2,1,0:T(4,128)(2,1)S(1)} collective-permute-done((bf16[3,6,4,512]{3,2,1,0:T(4,128)(2,1)S(1)}, bf16[3,6,4,512]{3,2,1,0:T(4,128)(2,1)S(1)}, u32[]{:S(2)}, u32[]{:S(2)}) %collective-permute-start.7) | collective-permute-done | bytes 73760 | tf_op jit(solution)/shard_map/ppermute | solution.py:273
  98.9 2.3 %copy-done = bf16[32,144,512]{2,1,0:T(8,128)(2,1)S(1)} copy-done((bf16[32,144,512]{2,1,0:T(8,128)(2,1)S(1)}, bf16[32,144,512]{2,1,0:T(8,128)(2,1)}, u32[]{:S(2)}) %copy-start) | copy-done | bytes 4718616
  101.2 3.2 %tokens.1 = bf16[6,12,4,512]{3,2,1,0:T(4,128)(2,1)} custom-call(bf16[3,6,4,512]{3,2,1,0:T(4,128)(2,1)S(1)} %get-tuple-element.9.m0, bf16[3,6,4,512]{3,2,1,0:T(4,128)(2,1)S(1)} %collective-permute-done.5.m1, bf16[3,6,4,512]{3,2,1,0:T(4,128)(2,1)S(1)} %collective-permute-done.6.m2, bf16[3,6,4,512]{3,2,1,0:T(4,128)(2,1)S(1)} %collective-permute-done.7.m3, ...), custom_call_target="tpu_custom_call" | custom-call | tf_op jit(solution)/shard_map/tokens/pallas_call | solution.py:229
  (17 shorter events, 0.1 us)
Async XLA Ops:
  6.5 92.3 %all-gather.4.cloned.1.call-start = ((), (), s32[]{:S(2)}) async-start(), calls=%async_computation | async-start | bytes 5013504 | tf_op jit(solution)/shard_map/all_gather | solution.py:253
  6.5 0.8 copy-start.4
  7.4 0.8 copy-start.5
  8.2 0.8 copy-start.6
  9.0 0.7 copy-start.7
  9.8 8.3 %collective-permute-start.3 = (bf16[192,512]{1,0:T(8,128)(2,1)S(1)}, bf16[192,512]{1,0:T(8,128)(2,1)S(1)}, u32[]{:S(2)}, u32[]{:S(2)}) collective-permute-start(bf16[192,512]{1,0:T(8,128)(2,1)S(1)} %pack.1), channel_id=1, source_target_pairs={{0,272},{1,273},{2,274},{3,275},{4,276},{5,277},{6,278},{7,279},{8... | collective-permute-start | bytes 589832 | tf_op jit(solution)/shard_map/ppermute | solution.py:246
  15.0 83.9 %copy-start.1 = (bf16[4,6,12,512]{3,0,2,1:T(4,128)(2,1)S(1)}, bf16[4,6,12,512]{3,0,2,1:T(4,128)(2,1)}, u32[]{:S(2)}) copy-start(bf16[4,6,12,512]{3,0,2,1:T(4,128)(2,1)} %param.10) | copy-start | bytes 884740
  15.0 83.9 %copy-start.8 = (f32[512]{0:T(512)S(1)}, f32[512]{0:T(512)}, u32[]{:S(2)}) copy-start(f32[512]{0:T(512)} %param.14) | copy-start | bytes 6148
  15.0 83.8 %copy-start.9 = (f32[512]{0:T(512)S(1)}, f32[512]{0:T(512)}, u32[]{:S(2)}) copy-start(f32[512]{0:T(512)} %param.17) | copy-start | bytes 6148
  48.7 22.2 %collective-permute-start.4 = (bf16[8,2,48,512]{3,2,1,0:T(8,128)(2,1)S(1)}, bf16[8,2,48,512]{3,2,1,0:T(8,128)(2,1)S(1)}, u32[]{:S(2)}, u32[]{:S(2)}) collective-permute-start(bf16[8,2,48,512]{3,2,1,0:T(8,128)(2,1)S(1)} %bitcast.21), channel_id=1, source_target_pairs={{0,1},{1,0},{2,3},{3,2},{4,5},{5,4},{6,7},{7,6},{8,9},{9,8},{10,11... | collective-permute-start | bytes 2359304 | tf_op jit(solution)/shard_map/ppermute | solution.py:255
  58.9 9.8 %collective-permute-start = (bf16[3,6,4,512]{3,2,1,0:T(4,128)(2,1)S(1)}, bf16[3,6,4,512]{3,2,1,0:T(4,128)(2,1)S(1)}, u32[]{:S(2)}, u32[]{:S(2)}) collective-permute-start(bf16[3,6,4,512]{3,2,1,0:T(4,128)(2,1)S(1)} %get-tuple-element.20), channel_id=1, source_target_pairs={{0,33},{1,34},{2,35},{3,36},{4,37},{5,38},{6,39},{7,40},{8,41},{9,... | collective-permute-start | bytes 221192 | tf_op jit(solution)/shard_map/ppermute | solution.py:260
  62.7 8.3 %collective-permute-start.1 = (bf16[3,6,4,512]{3,2,1,0:T(4,128)(2,1)S(1)}, bf16[3,6,4,512]{3,2,1,0:T(4,128)(2,1)S(1)}, u32[]{:S(2)}, u32[]{:S(2)}) collective-permute-start(bf16[3,6,4,512]{3,2,1,0:T(4,128)(2,1)S(1)} %get-tuple-element.19), channel_id=1, source_target_pairs={{0,32},{1,33},{2,34},{3,35},{4,36},{5,37},{6,38},{7,39},{8,40},{9,... | collective-permute-start | bytes 221192 | tf_op jit(solution)/shard_map/ppermute | solution.py:261
  65.8 5.2 %collective-permute-start.2 = (bf16[3,6,4,512]{3,2,1,0:T(4,128)(2,1)S(1)}, bf16[3,6,4,512]{3,2,1,0:T(4,128)(2,1)S(1)}, u32[]{:S(2)}, u32[]{:S(2)}) collective-permute-start(bf16[3,6,4,512]{3,2,1,0:T(4,128)(2,1)S(1)} %get-tuple-element.18), channel_id=1, source_target_pairs={{0,1},{1,2},{2,3},{3,4},{4,5},{5,6},{6,7},{7,8},{8,9},{9,10},{10,1... | collective-permute-start | bytes 221192 | tf_op jit(solution)/shard_map/ppermute | solution.py:262
  71.0 1.0 copy-start.2
  72.0 0.9 copy-start.3
  81.9 13.3 %collective-permute-start.5 = (bf16[3,6,4,512]{3,2,1,0:T(4,128)(2,1)S(1)}, bf16[3,6,4,512]{3,2,1,0:T(4,128)(2,1)S(1)}, u32[]{:S(2)}, u32[]{:S(2)}) collective-permute-start(bf16[3,6,4,512]{3,2,1,0:T(4,128)(2,1)S(1)} %get-tuple-element.10), channel_id=1, source_target_pairs={{0,31},{1,0},{2,1},{3,2},{4,3},{5,4},{6,5},{7,6},{8,7},{9,8},{10,9... | collective-permute-start | bytes 221192 | tf_op jit(solution)/shard_map/ppermute | solution.py:271
  88.5 6.7 %collective-permute-start.6 = (bf16[3,6,4,512]{3,2,1,0:T(4,128)(2,1)S(1)}, bf16[3,6,4,512]{3,2,1,0:T(4,128)(2,1)S(1)}, u32[]{:S(2)}, u32[]{:S(2)}) collective-permute-start(bf16[3,6,4,512]{3,2,1,0:T(4,128)(2,1)S(1)} %get-tuple-element.11), channel_id=1, source_target_pairs={{0,480},{1,481},{2,482},{3,483},{4,484},{5,485},{6,486},{7,487},{8... | collective-permute-start | bytes 221192 | tf_op jit(solution)/shard_map/ppermute | solution.py:272
  92.3 6.6 %collective-permute-start.7 = (bf16[3,6,4,512]{3,2,1,0:T(4,128)(2,1)S(1)}, bf16[3,6,4,512]{3,2,1,0:T(4,128)(2,1)S(1)}, u32[]{:S(2)}, u32[]{:S(2)}) collective-permute-start(bf16[3,6,4,512]{3,2,1,0:T(4,128)(2,1)S(1)} %get-tuple-element.12), channel_id=1, source_target_pairs={{0,511},{1,480},{2,481},{3,482},{4,483},{5,484},{6,485},{7,486},{8... | collective-permute-start | bytes 221192 | tf_op jit(solution)/shard_map/ppermute | solution.py:273
  98.9 2.3 %copy-start = (bf16[32,144,512]{2,1,0:T(8,128)(2,1)S(1)}, bf16[32,144,512]{2,1,0:T(8,128)(2,1)}, u32[]{:S(2)}) copy-start(bf16[32,144,512]{2,1,0:T(8,128)(2,1)} %all-gather.4.cloned.1.call-done) | copy-start | bytes 14155780
Sparse Core Ops, SparseCore 0:
  18.9 55.0 all-gather.3

commit v3 on v2

v3 whole, which is shorter than its diff:
```python
import jax
import jax.numpy as jnp
import numpy as np
from jax import lax
from jax.experimental import pallas as pl
from jax.experimental.pallas import tpu as pltpu
from jax.sharding import Mesh, PartitionSpec as P

WLAT = 6
WLON = 12
LEVELS = 4
HALF_LAT = WLAT // 2
HALF_LON = WLON // 2
QUARTER = LEVELS * HALF_LAT * HALF_LON
WN = 4 * QUARTER
D = 512
CORNER = (HALF_LAT, HALF_LON, LEVELS, D)
HEADS = 16
HEAD_DIM = D // HEADS
FF = 2048
LANES = 128
PER_GROUP = LANES // HEAD_DIM
GROUPS = HEADS // PER_GROUP
PIECES = 4
MASKED = -1e30
EPSILON = 1e-05
F32 = jnp.float32
BF16 = jnp.bfloat16
VMEM_LIMIT = 60 * 1024 * 1024

AXES = ("xl", "y", "xh", "z", "c")
SIZES = (2, 8, 2, 8, 2)
LAT = ("xl", "y")
LON = ("xh", "z", "c")


def place(lat, lon):
    return (lat % 16) * 32 + lon % 32


def shifted(dlat, dlon):
    return [(place(a, o), place(a + dlat, o + dlon)) for a in range(16) for o in range(32)]


def mirrored():
    def at(x, y, z, c):
        return (((x % 2) * 8 + y) * 2 + x // 2) * 16 + z * 2 + c

    return [
        (at(x, y, z, c), at(3 - x, y, z, c))
        for x in range(4)
        for y in range(8)
        for z in range(8)
        for c in range(2)
    ]


def to_quarters():
    hot = np.zeros((WN, LEVELS, WLAT, WLON), np.float32)
    place_of = 0
    for i in range(2):
        for j in range(2):
            for row in range(HALF_LAT):
                for col in range(HALF_LON):
                    for lev in range(LEVELS):
                        hot[place_of, lev, i * HALF_LAT + row, j * HALF_LON + col] = 1
                        place_of += 1
    return hot.reshape(WN, WN)


def tags():
    upper = (np.arange(WN) // WLON % WLAT < HALF_LAT).astype(np.float32)
    columns = np.zeros((2, WN, LANES), np.float32)
    columns[0, :, 0], columns[0, :, 1] = upper, 1 - upper
    columns[1, :, 0], columns[1, :, 1] = MASKED * (1 - upper), MASKED * upper
    return columns


def normed(values, gain):
    average = jnp.mean(values, -1, keepdims=True)
    centered = values - average
    variance = jnp.mean(centered * centered, -1, keepdims=True)
    return centered * lax.rsqrt(variance + EPSILON) * gain


def dot(a, b):
    return jnp.dot(a, b, preferred_element_type=F32)


def dot_t(a, b):
    return lax.dot_general(a, b, (((1,), (1,)), ((), ())), preferred_element_type=F32)


def stacked(quarters):
    return jnp.concatenate([q.astype(F32).reshape(QUARTER, D) for q in quarters], 0)


def corner(cells, i, j):
    return cells[i * HALF_LAT : (i + 1) * HALF_LAT, j * HALF_LON : (j + 1) * HALF_LON]


def pack_kernel(up_ref, down_ref, proj_ref, out_ref, sems):
    copies = [
        pltpu.make_async_copy(source, out_ref.at[start : start + source.shape[0]], sems.at[i])
        for i, (source, start) in enumerate(((up_ref, 0), (down_ref, 64), (proj_ref, 128)))
    ]
    for copy in copies:
        copy.start()
    for copy in copies:
        copy.wait()


def attention_kernel(
    spot_ref, r0, r1, r2, r3, mine_ref, other_ref, hot_ref, tags_ref, bias_hbm,
    o0, o1, o2, o3, bias_ref, sems,
):
    fetches = [
        pltpu.make_async_copy(
            bias_hbm.at[g * PER_GROUP : (g + 1) * PER_GROUP],
            bias_ref.at[g * PER_GROUP : (g + 1) * PER_GROUP],
            sems.at[g],
        )
        for g in range(GROUPS)
    ]
    for fetch in fetches:
        fetch.start()
    hot = hot_ref[...]
    rows = stacked([r[...] for r in (r0, r1, r2, r3)]).astype(BF16)
    rows = lax.dot_general(hot, rows, (((0,), (0,)), ((), ())), preferred_element_type=F32)
    rows = rows.astype(BF16)
    low_half = spot_ref[0] == 0

    def projected(which):
        columns = slice(which * D, (which + 1) * D)
        mine = mine_ref[:, :, columns].reshape(D // 2, D)
        other = jnp.stack([other_ref[0, :, :, columns], other_ref[1, :, :, columns]], 1)
        other = other.reshape(D // 2, D)
        low = dot(rows[:, : D // 2], jnp.where(low_half, mine, other))
        return (low + dot(rows[:, D // 2 :], jnp.where(low_half, other, mine))).astype(BF16)

    queries, keys, values = projected(0), projected(1), projected(2)
    lane_head = lax.broadcasted_iota(jnp.int32, (1, LANES), 1) // HEAD_DIM
    zero = jnp.zeros((), BF16)
    ones = jnp.ones((WN, LANES), BF16)
    query_tags = jnp.where(spot_ref[1] == 1, tags_ref[0], zero)
    key_tags = tags_ref[1]
    groups = []
    for group in range(GROUPS):
        fetches[group].wait()
        lanes = slice(group * LANES, (group + 1) * LANES)
        group_q, group_v = queries[:, lanes], values[:, lanes]
        group_k = jnp.concatenate([keys[:, lanes], key_tags], 1)
        total = None
        for j in range(PER_GROUP):
            mine = lane_head == j
            head_q = jnp.concatenate([jnp.where(mine, group_q, zero), query_tags], 1)
            scores = dot_t(head_q, group_k) * HEAD_DIM ** (-0.5)
            scores = scores + bias_ref[group * PER_GROUP + j].astype(F32)
            weights = jnp.exp(scores - jnp.max(scores, -1, keepdims=True)).astype(BF16)
            head_v = jnp.concatenate([jnp.where(mine, group_v, zero), ones], 1)
            product = dot(weights, head_v)
            part = product[:, :LANES] / product[:, LANES:]
            total = part if total is None else total + part
        groups.append(total.astype(BF16))
    attended = dot(hot, jnp.concatenate(groups, 1))
    for i, out in enumerate((o0, o1, o2, o3)):
        out[...] = attended[i * QUARTER : (i + 1) * QUARTER].reshape(CORNER).astype(BF16)


def token_kernel(
    m0, m1, m2, m3, cells_ref, attn_gain_ref, mlp_gain_ref, weights_hbm, out_ref, wp, wu, wd, sems
):
    fetch_proj = pltpu.make_async_copy(weights_hbm.at[:, :, 128:144], wp, sems.at[0])
    fetch_proj.start()
    fetches = []
    step = 16 // PIECES
    for i in range(PIECES):
        shards_of = slice(i * step, (i + 1) * step)
        fetches.append(
            [
                pltpu.make_async_copy(
                    weights_hbm.at[shards_of, :, 64 * k : 64 * (k + 1)],
                    target.at[shards_of],
                    sems.at[1 + 2 * i + k],
                )
                for k, target in enumerate((wu, wd))
            ]
        )
        for fetch in fetches[-1]:
            fetch.start()
    attended = stacked([m[...] for m in (m0, m1, m2, m3)]).astype(BF16)
    cells = stacked([corner(cells_ref, i, j) for i in range(2) for j in range(2)])
    fetch_proj.wait()
    projected = dot(attended[:, : D // 2], wp[:, 0].reshape(D // 2, D)) + dot(
        attended[:, D // 2 :], wp[:, 1].reshape(D // 2, D)
    )
    rows = (cells + normed(projected, attn_gain_ref[...])).astype(BF16)
    lowered = None
    units = FF // PIECES
    for i in range(PIECES):
        for fetch in fetches[i]:
            fetch.wait()
        up = wu[i * step : (i + 1) * step].reshape(units, D)
        down = wd[i * step : (i + 1) * step].reshape(units, D)
        raised = dot_t(rows, up)
        hidden = 0.5 * raised * (1.0 + lax.erf(raised * (0.5**0.5)))
        part = dot(hidden.astype(BF16), down)
        lowered = part if lowered is None else lowered + part
    updated = rows.astype(F32) + normed(lowered, mlp_gain_ref[...])
    run = HALF_LON * LEVELS
    for i in range(2):
        for j in range(2):
            for row in range(HALF_LAT):
                start = (i * 2 + j) * QUARTER + row * run
                piece = updated[start : start + run].reshape(HALF_LON, LEVELS, D)
                out_ref[i * HALF_LAT + row, j * HALF_LON : (j + 1) * HALF_LON] = piece.astype(BF16)


def whole(shape):
    return pl.BlockSpec(shape, lambda i: (0,) * len(shape))


def scalars():
    return pl.BlockSpec(memory_space=pltpu.SMEM)


def fetched():
    return pl.BlockSpec(memory_space=pl.ANY)


def params():
    return pltpu.CompilerParams(vmem_limit_bytes=VMEM_LIMIT)


def packed(up_weight, down_weight, proj_weight):
    return pl.pallas_call(
        pack_kernel,
        grid=(1,),
        in_specs=[fetched()] * 3,
        out_specs=whole((144, D)),
        out_shape=jax.ShapeDtypeStruct((144, D), BF16),
        scratch_shapes=[pltpu.SemaphoreType.DMA((3,))],
        compiler_params=params(),
        name="pack",
    )(up_weight, down_weight, proj_weight)


def attention(spot, quarters, mine, other, bias):
    quarter = whole(CORNER)
    constants = (jnp.asarray(to_quarters(), BF16), jnp.asarray(tags(), BF16))
    return pl.pallas_call(
        attention_kernel,
        grid=(1,),
        in_specs=[scalars()]
        + [quarter] * 4
        + [whole(a.shape) for a in (mine, other, *constants)]
        + [fetched()],
        out_specs=[quarter] * 4,
        out_shape=[jax.ShapeDtypeStruct(CORNER, BF16)] * 4,
        scratch_shapes=[pltpu.VMEM(bias.shape, BF16), pltpu.SemaphoreType.DMA((GROUPS,))],
        compiler_params=params(),
        name="attention",
    )(spot, *quarters, mine, other, *constants, bias)


def tokens(quarters, cells, gathered, attn_gain, mlp_gain):
    out = (WLAT, WLON, LEVELS, D)
    return pl.pallas_call(
        token_kernel,
        grid=(1,),
        in_specs=[whole(CORNER)] * 4 + [whole(out)] + [whole((1, D))] * 2 + [fetched()],
        out_specs=whole(out),
        out_shape=jax.ShapeDtypeStruct(out, BF16),
        scratch_shapes=[pltpu.VMEM((16, 2, rows, D), BF16) for rows in (16, 64, 64)]
        + [pltpu.SemaphoreType.DMA((1 + 2 * PIECES,))],
        compiler_params=params(),
        name="tokens",
    )(*quarters, cells, attn_gain.reshape(1, D), mlp_gain.reshape(1, D), gathered)


def shards(
    latent, qkv_weight, proj_weight, position_bias, attn_gain, up_weight, down_weight, mlp_gain
):
    own = packed(up_weight, down_weight, proj_weight)
    other = lax.ppermute(own, AXES, mirrored())
    low_half = lax.axis_index("xh") == 0
    both = jnp.stack([jnp.where(low_half, own, other), jnp.where(low_half, other, own)])
    gathered = lax.all_gather(both, ("z", "c"), axis=0, tiled=False)

    cells = latent.transpose(1, 2, 0, 3)
    rolled = [
        lax.ppermute(corner(cells, 1, 1), AXES, shifted(1, 1)),
        lax.ppermute(corner(cells, 1, 0), AXES, shifted(1, 0)),
        lax.ppermute(corner(cells, 0, 1), AXES, shifted(0, 1)),
        corner(cells, 0, 0),
    ]
    qkv_weight, _, rolled = lax.optimization_barrier((qkv_weight, both, rolled))
    mine = lax.all_gather(qkv_weight, ("z", "c"), axis=0, tiled=False)
    core = lax.axis_index("c")
    sent = lax.dynamic_index_in_dim(mine.reshape(8, 2, 16, 3 * D), core, 1, keepdims=False)
    theirs = lax.all_gather(lax.ppermute(sent, AXES, mirrored()), "c", axis=0, tiled=False)

    spot = jnp.stack([lax.axis_index("xh"), (lax.axis_index(LAT) == 0).astype(jnp.int32)])
    attended = attention(spot, rolled, mine, theirs, position_bias)
    restored = [
        attended[3],
        lax.ppermute(attended[2], AXES, shifted(0, -1)),
        lax.ppermute(attended[1], AXES, shifted(-1, 0)),
        lax.ppermute(attended[0], AXES, shifted(-1, -1)),
    ]
    return tokens(restored, cells, gathered, attn_gain, mlp_gain).transpose(2, 0, 1, 3)


def solution(mesh):
    mesh = Mesh(mesh.devices.reshape(SIZES), AXES)
    placed = (
        P(None, LAT, LON, None),
        P(LON, None),
        P(LON, None),
        P(),
        P(),
        P(LON, None),
        P(LON, None),
        P(),
    )
    return jax.shard_map(
        shards, mesh=mesh, in_specs=placed, out_specs=P(None, LAT, LON, None), check_vma=False
    )
```

time: 112 us -> 115 us (1.027)
  waiting for transfers between devices: 8.85 us -> 15.6 us
  local copies, waits for them, and re-layouts: 8.6 us -> 2.4 us
  Pallas kernels: 12.1 us -> 15.6 us
  starting transfers between devices: 37.3 us -> 34 us
  other arithmetic: 0.87 us -> 2.33 us
    ppermute x1, waiting for transfers between devices: 0.01 us -> 8.65 us  [shards(): lax.ppermute(sent, AXES, mirrored())]
    unnamed x20 -> x14, local copies, waits for them, and re-layouts: 7.49 us -> 0.65 us
    ppermute x1, starting transfers between devices: 9.07 us -> 4.34 us  [shards(): lax.ppermute(sent, AXES, mirrored())]
    ppermute x1, starting transfers between devices: 6.62 us -> 2.28 us  [shards(): lax.ppermute(attended[2], AXES, shifted(0, -1))]
    pallas_call x2, Pallas kernels: 3.18 us -> 7.49 us  [the longest x1 5.93 us: tokens(): pl.pallas_call(token_kernel, grid=(1,), in_specs=[whole(CORNER)] * 4 + [w...]
    ppermute x1, starting transfers between devices: 2.92 us -> 6.53 us  [shards(): lax.ppermute(attended[0], AXES, shifted(-1, -1))]
    ppermute x1, starting transfers between devices: 3.76 us -> 7.34 us  [shards(): lax.ppermute(corner(cells, 1, 1), AXES, shifted(1, 1))]
    ppermute x1, waiting for transfers between devices: 3.62 us -> 2.15 us  [shards(): lax.ppermute(attended[0], AXES, shifted(-1, -1))]
  transfers between devices with their start and end apart: 9 -> 9, of which waited for: 3 -> 4; matrix products, arithmetic and copies ran while one was open for 1% -> 2% of each run, Pallas kernels for 8% -> 7%
where the time goes in v3:
time: 115 us; the launch traced here: 114 us
  starting transfers between devices  34 us (30%)
  blocking collectives  31 us (27%)
  Pallas kernels  15.6 us (14%)
  waiting for transfers between devices  15.6 us (14%)
  between operations  13.6 us (12%)
  local copies, waits for them, and re-layouts  2.4 us (2%)
  other arithmetic  2.33 us (2%)
    all_gather x1, blocking collectives, shards(): mine = lax.all_gather(qkv_weight, ('z', 'c'), axis=0, tiled=False)  27.9 us
    ppermute x1, waiting for transfers between devices, shards(): lax.ppermute(sent, AXES, mirrored())  8.65 us
    pallas_call x1, Pallas kernels, attention(): pl.pallas_call(attention_kernel, grid=(1,), in_specs=[scalars()] + [quart...  8.06 us
    ppermute x1, starting transfers between devices, shards(): lax.ppermute(corner(cells, 1, 1), AXES, shifted(1, 1))  7.34 us
    ppermute x1, starting transfers between devices, shards(): lax.ppermute(attended[0], AXES, shifted(-1, -1))  6.53 us
    pallas_call x1, Pallas kernels, tokens(): pl.pallas_call(token_kernel, grid=(1,), in_specs=[whole(CORNER)] * 4 + [w...  5.93 us
    ppermute x1, starting transfers between devices, shards(): other = lax.ppermute(own, AXES, mirrored())  5.22 us
    ppermute x1, starting transfers between devices, shards(): lax.ppermute(sent, AXES, mirrored())  4.34 us
  transfers between devices with their start and end apart: 9, of which 4 were waited for; matrix products, arithmetic and copies ran while one was open for 2% of the time, Pallas kernels for 7%

profile of v3, /device:TPU:1, one launch (start us, length us, event | category | flops | bytes accessed | tf_op | source)
XLA Modules:
  0.0 114.5 jit_solution(5172806861649318853)
XLA Ops:
  6.5 0.0 all-gather.5.cloned.1.call-start
  6.5 1.6 %pack.1 = bf16[144,512]{1,0:T(8,128)(2,1)} custom-call(bf16[64,512]{1,0:T(8,128)(2,1)} %up_ref.1, bf16[64,512]{1,0:T(8,128)(2,1)} %down_ref.1, bf16[16,512]{1,0:T(8,128)(2,1)} %proj_ref.1), custom_call_target="tpu_custom_call" | custom-call | tf_op jit(solution)/shard_map/pack/pallas_call | solution.py:236
  8.1 5.2 %collective-permute-start = (bf16[144,512]{1,0:T(8,128)(2,1)}, bf16[144,512]{1,0:T(8,128)(2,1)S(1)}, u32[]{:S(2)}, u32[]{:S(2)}) collective-permute-start(bf16[144,512]{1,0:T(8,128)(2,1)} %pack.1), channel_id=1, source_target_pairs={{0,272},{1,273},{2,274},{3,275},{4,276},{5,277},{6,278},{7,279},{8... | collective-permute-start | bytes 442376 | tf_op jit(solution)/shard_map/ppermute | solution.py:285
  13.3 2.7 %collective-permute-done = bf16[144,512]{1,0:T(8,128)(2,1)S(1)} collective-permute-done((bf16[144,512]{1,0:T(8,128)(2,1)}, bf16[144,512]{1,0:T(8,128)(2,1)S(1)}, u32[]{:S(2)}, u32[]{:S(2)}) %collective-permute-start) | collective-permute-done | bytes 147488 | tf_op jit(solution)/shard_map/ppermute | solution.py:285
  16.1 0.9 select_bitcast_fusion.1
  17.0 0.7 pad_maximum_fusion
  17.7 0.0 all-gather.5.cloned.1.call-update
  17.8 1.7 %fusion = (bf16[3,6,4,512]{3,2,1,0:T(4,128)(2,1)}, bf16[3,6,4,512]{3,2,1,0:T(4,128)(2,1)S(1)}, bf16[3,6,4,512]{3,2,1,0:T(4,128)(2,1)S(1)}, bf16[3,6,4,512]{3,2,1,0:T(4,128)(2,1)S(1)}) fusion(bf16[6,12,4,512]{3,2,1,0:T(4,128)(2,1)} %bitcast.22), kind=kLoop, calls=%fused_computation.5 | loop fusion | bytes 589824 | tf_op jit(solution)/shard_map/slice | solution.py:99
  19.5 7.3 %collective-permute-start.1 = (bf16[3,6,4,512]{3,2,1,0:T(4,128)(2,1)S(1)}, bf16[3,6,4,512]{3,2,1,0:T(4,128)(2,1)S(1)}, u32[]{:S(2)}, u32[]{:S(2)}) collective-permute-start(bf16[3,6,4,512]{3,2,1,0:T(4,128)(2,1)S(1)} %get-tuple-element.26), channel_id=1, source_target_pairs={{0,33},{1,34},{2,35},{3,36},{4,37},{5,38},{6,39},{7,40},{8,41},{9,... | collective-permute-start | bytes 221192 | tf_op jit(solution)/shard_map/ppermute | solution.py:292
  26.8 3.2 %collective-permute-start.2 = (bf16[3,6,4,512]{3,2,1,0:T(4,128)(2,1)S(1)}, bf16[3,6,4,512]{3,2,1,0:T(4,128)(2,1)S(1)}, u32[]{:S(2)}, u32[]{:S(2)}) collective-permute-start(bf16[3,6,4,512]{3,2,1,0:T(4,128)(2,1)S(1)} %get-tuple-element.25), channel_id=1, source_target_pairs={{0,32},{1,33},{2,34},{3,35},{4,36},{5,37},{6,38},{7,39},{8,40},{9,... | collective-permute-start | bytes 221192 | tf_op jit(solution)/shard_map/ppermute | solution.py:293
  30.1 1.9 %collective-permute-start.3 = (bf16[3,6,4,512]{3,2,1,0:T(4,128)(2,1)S(1)}, bf16[3,6,4,512]{3,2,1,0:T(4,128)(2,1)S(1)}, u32[]{:S(2)}, u32[]{:S(2)}) collective-permute-start(bf16[3,6,4,512]{3,2,1,0:T(4,128)(2,1)S(1)} %get-tuple-element.24), channel_id=1, source_target_pairs={{0,1},{1,2},{2,3},{3,4},{4,5},{5,6},{6,7},{7,8},{8,9},{9,10},{10,1... | collective-permute-start | bytes 221192 | tf_op jit(solution)/shard_map/ppermute | solution.py:294
  32.0 0.0 collective-permute-done.1.r0
  32.0 0.0 copy-start.1
  32.0 2.0 %collective-permute-done.2.r1 = bf16[3,6,4,512]{3,2,1,0:T(4,128)(2,1)S(1)} collective-permute-done((bf16[3,6,4,512]{3,2,1,0:T(4,128)(2,1)S(1)}, bf16[3,6,4,512]{3,2,1,0:T(4,128)(2,1)S(1)}, u32[]{:S(2)}, u32[]{:S(2)}) %collective-permute-start.2) | collective-permute-done | bytes 73760 | tf_op jit(solution)/shard_map/ppermute | solution.py:293
  34.0 0.0 collective-permute-done.3.r2
  34.1 27.9 %all-gather = bf16[256,1536]{1,0:T(8,128)(2,1)S(1)} all-gather(bf16[16,1536]{1,0:T(8,128)(2,1)} %param.11), channel_id=2, replica_groups=mesh['xl'=2,'y'=8,'xh'=2,'z'=8,'c'=2] {'z','c'}, dimensions={0}, use_global_device_ids=true | all-gather | bytes 835584 | tf_op jit(solution)/shard_map/all_gather | solution.py:298
  62.0 4.3 %collective-permute-start.4 = (bf16[8,16,1536]{2,1,0:T(8,128)(2,1)S(1)}, bf16[8,16,1536]{2,1,0:T(8,128)(2,1)S(1)}, u32[]{:S(2)}, u32[]{:S(2)}) collective-permute-start(bf16[8,16,1536]{2,1,0:T(8,128)(2,1)S(1)} %dynamic-slice_bitcast_fusion), channel_id=1, source_target_pairs={{0,272},{1,273},{2,274},{3,275},{4,276},{5,277},{6,278},{7,279},{8... | collective-permute-start | bytes 1179656 | tf_op jit(solution)/shard_map/ppermute | solution.py:301
  66.4 0.7 pad_add_fusion.spot_ref
  67.0 8.7 %collective-permute-done.4 = bf16[8,16,1536]{2,1,0:T(8,128)(2,1)S(1)} collective-permute-done((bf16[8,16,1536]{2,1,0:T(8,128)(2,1)S(1)}, bf16[8,16,1536]{2,1,0:T(8,128)(2,1)S(1)}, u32[]{:S(2)}, u32[]{:S(2)}) %collective-permute-start.4) | collective-permute-done | bytes 393248 | tf_op jit(solution)/shard_map/ppermute | solution.py:301
  75.7 3.1 %all-gather.1 = bf16[16,16,1536]{2,1,0:T(8,128)(2,1)} all-gather(bf16[8,16,1536]{2,1,0:T(8,128)(2,1)S(1)} %collective-permute-done.4), channel_id=3, replica_groups=mesh['xl'=2,'y'=8,'xh'=2,'z'=8,'c'=2] {'c'}, dimensions={0}, use_global_device_ids=true | all-gather | bytes 1179648 | tf_op jit(solution)/shard_map/all_gather | solution.py:301
  78.8 0.0 copy-done.1
  78.8 0.0 copy-done.2
  78.8 8.1 %attention.1 = (bf16[3,6,4,512]{3,2,1,0:T(4,128)(2,1)}, bf16[3,6,4,512]{3,2,1,0:T(4,128)(2,1)}, bf16[3,6,4,512]{3,2,1,0:T(4,128)(2,1)}, bf16[3,6,4,512]{3,2,1,0:T(4,128)(2,1)}) custom-call(s32[2]{0:T(128)} %pad_add_fusion.spot_ref, bf16[3,6,4,512]{3,2,1,0:T(4,128)(2,1)} %copy-done.1, bf16[3,6,4,512]{3,2,1,0:T(4,128)(2,1)} %copy-done.2, ...), custom_call_target="tpu_custom_call" | custom-call | tf_op jit(solution)/shard_map/attention/pallas_call | solution.py:251
  86.9 2.3 %collective-permute-start.5 = (bf16[3,6,4,512]{3,2,1,0:T(4,128)(2,1)}, bf16[3,6,4,512]{3,2,1,0:T(4,128)(2,1)S(1)}, u32[]{:S(2)}, u32[]{:S(2)}) collective-permute-start(bf16[3,6,4,512]{3,2,1,0:T(4,128)(2,1)} %get-tuple-element.20), channel_id=1, source_target_pairs={{0,31},{1,0},{2,1},{3,2},{4,3},{5,4},{6,5},{7,6},{8,7},{9,8},{10,9... | collective-permute-start | bytes 221192 | tf_op jit(solution)/shard_map/ppermute | solution.py:307
  89.1 3.2 %collective-permute-start.6 = (bf16[3,6,4,512]{3,2,1,0:T(4,128)(2,1)}, bf16[3,6,4,512]{3,2,1,0:T(4,128)(2,1)S(1)}, u32[]{:S(2)}, u32[]{:S(2)}) collective-permute-start(bf16[3,6,4,512]{3,2,1,0:T(4,128)(2,1)} %get-tuple-element.21), channel_id=1, source_target_pairs={{0,480},{1,481},{2,482},{3,483},{4,484},{5,485},{6,486},{7,487},{8... | collective-permute-start | bytes 221192 | tf_op jit(solution)/shard_map/ppermute | solution.py:308
  92.3 6.5 %collective-permute-start.7 = (bf16[3,6,4,512]{3,2,1,0:T(4,128)(2,1)}, bf16[3,6,4,512]{3,2,1,0:T(4,128)(2,1)S(1)}, u32[]{:S(2)}, u32[]{:S(2)}) collective-permute-start(bf16[3,6,4,512]{3,2,1,0:T(4,128)(2,1)} %get-tuple-element.22), channel_id=1, source_target_pairs={{0,511},{1,480},{2,481},{3,482},{4,483},{5,484},{6,485},{7,486},{8... | collective-permute-start | bytes 221192 | tf_op jit(solution)/shard_map/ppermute | solution.py:309
  98.9 0.0 collective-permute-done.5.m1
  98.9 0.0 copy-start.4
  98.9 0.0 collective-permute-done.6.m2
  98.9 2.1 %collective-permute-done.7.m3 = bf16[3,6,4,512]{3,2,1,0:T(4,128)(2,1)S(1)} collective-permute-done((bf16[3,6,4,512]{3,2,1,0:T(4,128)(2,1)}, bf16[3,6,4,512]{3,2,1,0:T(4,128)(2,1)S(1)}, u32[]{:S(2)}, u32[]{:S(2)}) %collective-permute-start.7) | collective-permute-done | bytes 73760 | tf_op jit(solution)/shard_map/ppermute | solution.py:309
  101.1 0.6 copy-done.6
  101.7 5.9 %tokens.1 = bf16[6,12,4,512]{3,2,1,0:T(4,128)(2,1)} custom-call(bf16[3,6,4,512]{3,2,1,0:T(4,128)(2,1)} %get-tuple-element.19.m0, bf16[3,6,4,512]{3,2,1,0:T(4,128)(2,1)} %copy-done.4, bf16[3,6,4,512]{3,2,1,0:T(4,128)(2,1)} %copy-done.5, bf16[3,6,4,512]{3,2,1,0:T(4,128)(2,1)} %copy-done.6, bf16[6,12,4,512]{3,2,1,0:T(4,128)(2,1)} %bitcast.23, ...), custom_call_target="tpu_custom_call" | custom-call | tf_op jit(solution)/shard_map/tokens/pallas_call | solution.py:268
  (11 shorter events, 0.0 us)
Async XLA Ops:
  6.5 94.5 %all-gather.5.cloned.1.call-start = ((), (), s32[]{:S(2)}) async-start(), calls=%async_computation | async-start | bytes 5013504 | tf_op jit(solution)/shard_map/all_gather | solution.py:288
  8.1 8.0 %collective-permute-start = (bf16[144,512]{1,0:T(8,128)(2,1)}, bf16[144,512]{1,0:T(8,128)(2,1)S(1)}, u32[]{:S(2)}, u32[]{:S(2)}) collective-permute-start(bf16[144,512]{1,0:T(8,128)(2,1)} %pack.1), channel_id=1, source_target_pairs={{0,272},{1,273},{2,274},{3,275},{4,276},{5,277},{6,278},{7,279},{8... | collective-permute-start | bytes 442376 | tf_op jit(solution)/shard_map/ppermute | solution.py:285
  19.5 12.5 %collective-permute-start.1 = (bf16[3,6,4,512]{3,2,1,0:T(4,128)(2,1)S(1)}, bf16[3,6,4,512]{3,2,1,0:T(4,128)(2,1)S(1)}, u32[]{:S(2)}, u32[]{:S(2)}) collective-permute-start(bf16[3,6,4,512]{3,2,1,0:T(4,128)(2,1)S(1)} %get-tuple-element.26), channel_id=1, source_target_pairs={{0,33},{1,34},{2,35},{3,36},{4,37},{5,38},{6,39},{7,40},{8,41},{9,... | collective-permute-start | bytes 221192 | tf_op jit(solution)/shard_map/ppermute | solution.py:292
  26.8 7.2 %collective-permute-start.2 = (bf16[3,6,4,512]{3,2,1,0:T(4,128)(2,1)S(1)}, bf16[3,6,4,512]{3,2,1,0:T(4,128)(2,1)S(1)}, u32[]{:S(2)}, u32[]{:S(2)}) collective-permute-start(bf16[3,6,4,512]{3,2,1,0:T(4,128)(2,1)S(1)} %get-tuple-element.25), channel_id=1, source_target_pairs={{0,32},{1,33},{2,34},{3,35},{4,36},{5,37},{6,38},{7,39},{8,40},{9,... | collective-permute-start | bytes 221192 | tf_op jit(solution)/shard_map/ppermute | solution.py:293
  30.1 4.0 %collective-permute-start.3 = (bf16[3,6,4,512]{3,2,1,0:T(4,128)(2,1)S(1)}, bf16[3,6,4,512]{3,2,1,0:T(4,128)(2,1)S(1)}, u32[]{:S(2)}, u32[]{:S(2)}) collective-permute-start(bf16[3,6,4,512]{3,2,1,0:T(4,128)(2,1)S(1)} %get-tuple-element.24), channel_id=1, source_target_pairs={{0,1},{1,2},{2,3},{3,4},{4,5},{5,6},{6,7},{7,8},{8,9},{9,10},{10,1... | collective-permute-start | bytes 221192 | tf_op jit(solution)/shard_map/ppermute | solution.py:294
  32.0 46.8 %copy-start.1 = (bf16[3,6,4,512]{3,2,1,0:T(4,128)(2,1)}, bf16[3,6,4,512]{3,2,1,0:T(4,128)(2,1)S(1)}, u32[]{:S(2)}) copy-start(bf16[3,6,4,512]{3,2,1,0:T(4,128)(2,1)S(1)} %collective-permute-done.1.r0) | copy-start | bytes 221188
  34.0 44.7 %copy-start.2 = (bf16[3,6,4,512]{3,2,1,0:T(4,128)(2,1)}, bf16[3,6,4,512]{3,2,1,0:T(4,128)(2,1)S(1)}, u32[]{:S(2)}) copy-start(bf16[3,6,4,512]{3,2,1,0:T(4,128)(2,1)S(1)} %collective-permute-done.2.r1) | copy-start | bytes 221188
  34.1 44.7 %copy-start.3 = (bf16[3,6,4,512]{3,2,1,0:T(4,128)(2,1)}, bf16[3,6,4,512]{3,2,1,0:T(4,128)(2,1)S(1)}, u32[]{:S(2)}) copy-start(bf16[3,6,4,512]{3,2,1,0:T(4,128)(2,1)S(1)} %collective-permute-done.3.r2) | copy-start | bytes 221188
  62.0 16.8 %copy-start = (bf16[256,1536]{1,0:T(8,128)(2,1)}, bf16[256,1536]{1,0:T(8,128)(2,1)S(1)}, u32[]{:S(2)}) copy-start(bf16[256,1536]{1,0:T(8,128)(2,1)S(1)} %all-gather) | copy-start | bytes 2359300
  62.0 13.7 %collective-permute-start.4 = (bf16[8,16,1536]{2,1,0:T(8,128)(2,1)S(1)}, bf16[8,16,1536]{2,1,0:T(8,128)(2,1)S(1)}, u32[]{:S(2)}, u32[]{:S(2)}) collective-permute-start(bf16[8,16,1536]{2,1,0:T(8,128)(2,1)S(1)} %dynamic-slice_bitcast_fusion), channel_id=1, source_target_pairs={{0,272},{1,273},{2,274},{3,275},{4,276},{5,277},{6,278},{7,279},{8... | collective-permute-start | bytes 1179656 | tf_op jit(solution)/shard_map/ppermute | solution.py:301
  86.9 12.0 %collective-permute-start.5 = (bf16[3,6,4,512]{3,2,1,0:T(4,128)(2,1)}, bf16[3,6,4,512]{3,2,1,0:T(4,128)(2,1)S(1)}, u32[]{:S(2)}, u32[]{:S(2)}) collective-permute-start(bf16[3,6,4,512]{3,2,1,0:T(4,128)(2,1)} %get-tuple-element.20), channel_id=1, source_target_pairs={{0,31},{1,0},{2,1},{3,2},{4,3},{5,4},{6,5},{7,6},{8,7},{9,8},{10,9... | collective-permute-start | bytes 221192 | tf_op jit(solution)/shard_map/ppermute | solution.py:307
  89.1 9.7 %collective-permute-start.6 = (bf16[3,6,4,512]{3,2,1,0:T(4,128)(2,1)}, bf16[3,6,4,512]{3,2,1,0:T(4,128)(2,1)S(1)}, u32[]{:S(2)}, u32[]{:S(2)}) collective-permute-start(bf16[3,6,4,512]{3,2,1,0:T(4,128)(2,1)} %get-tuple-element.21), channel_id=1, source_target_pairs={{0,480},{1,481},{2,482},{3,483},{4,484},{5,485},{6,486},{7,487},{8... | collective-permute-start | bytes 221192 | tf_op jit(solution)/shard_map/ppermute | solution.py:308
  92.3 8.7 %collective-permute-start.7 = (bf16[3,6,4,512]{3,2,1,0:T(4,128)(2,1)}, bf16[3,6,4,512]{3,2,1,0:T(4,128)(2,1)S(1)}, u32[]{:S(2)}, u32[]{:S(2)}) collective-permute-start(bf16[3,6,4,512]{3,2,1,0:T(4,128)(2,1)} %get-tuple-element.22), channel_id=1, source_target_pairs={{0,511},{1,480},{2,481},{3,482},{4,483},{5,484},{6,485},{7,486},{8... | collective-permute-start | bytes 221192 | tf_op jit(solution)/shard_map/ppermute | solution.py:309
  98.9 2.2 %copy-start.4 = (bf16[3,6,4,512]{3,2,1,0:T(4,128)(2,1)}, bf16[3,6,4,512]{3,2,1,0:T(4,128)(2,1)S(1)}, u32[]{:S(2)}) copy-start(bf16[3,6,4,512]{3,2,1,0:T(4,128)(2,1)S(1)} %collective-permute-done.5.m1) | copy-start | bytes 221188
  98.9 2.2 %copy-start.5 = (bf16[3,6,4,512]{3,2,1,0:T(4,128)(2,1)}, bf16[3,6,4,512]{3,2,1,0:T(4,128)(2,1)S(1)}, u32[]{:S(2)}) copy-start(bf16[3,6,4,512]{3,2,1,0:T(4,128)(2,1)S(1)} %collective-permute-done.6.m2) | copy-start | bytes 221188
  101.0 0.6 copy-start.6
Sparse Core Ops, SparseCore 0:
  17.9 54.7 all-gather.4

commit v4 on v3

--- a/solution.py
+++ b/solution.py
@@ -27,6 +27,8 @@
 F32 = jnp.float32
 BF16 = jnp.bfloat16
 VMEM_LIMIT = 60 * 1024 * 1024
+STAGE_LIMIT = 48 * 1024 * 1024
+TOKENS_LIMIT = 40 * 1024 * 1024
 
 AXES = ("xl", "y", "xh", "z", "c")
 SIZES = (2, 8, 2, 8, 2)
@@ -167,41 +169,35 @@
         out[...] = attended[i * QUARTER : (i + 1) * QUARTER].reshape(CORNER).astype(BF16)
 
 
+def stage_kernel(gathered_ref, wp_ref, wu_ref, wd_ref, sems):
+    copies = [
+        pltpu.make_async_copy(gathered_ref.at[:, :, start:stop], target, sems.at[i])
+        for i, (start, stop, target) in enumerate(
+            ((128, 144, wp_ref), (0, 64, wu_ref), (64, 128, wd_ref))
+        )
+    ]
+    for copy in copies:
+        copy.start()
+    for copy in copies:
+        copy.wait()
+
+
 def token_kernel(
-    m0, m1, m2, m3, cells_ref, attn_gain_ref, mlp_gain_ref, weights_hbm, out_ref, wp, wu, wd, sems
+    spot_ref, m0, m1, m2, m3, cells_ref, wp, wu, wd, attn_gain_ref, mlp_gain_ref, out_ref
 ):
-    fetch_proj = pltpu.make_async_copy(weights_hbm.at[:, :, 128:144], wp, sems.at[0])
-    fetch_proj.start()
-    fetches = []
-    step = 16 // PIECES
-    for i in range(PIECES):
-        shards_of = slice(i * step, (i + 1) * step)
-        fetches.append(
-            [
-                pltpu.make_async_copy(
-                    weights_hbm.at[shards_of, :, 64 * k : 64 * (k + 1)],
-                    target.at[shards_of],
-                    sems.at[1 + 2 * i + k],
-                )
-                for k, target in enumerate((wu, wd))
-            ]
-        )
-        for fetch in fetches[-1]:
-            fetch.start()
     attended = stacked([m[...] for m in (m0, m1, m2, m3)]).astype(BF16)
     cells = stacked([corner(cells_ref, i, j) for i in range(2) for j in range(2)])
-    fetch_proj.wait()
-    projected = dot(attended[:, : D // 2], wp[:, 0].reshape(D // 2, D)) + dot(
-        attended[:, D // 2 :], wp[:, 1].reshape(D // 2, D)
-    )
+    low_half = spot_ref[0] == 0
+    low, high = attended[:, : D // 2], attended[:, D // 2 :]
+    ours, theirs = jnp.where(low_half, low, high), jnp.where(low_half, high, low)
+    projected = dot(ours, wp[:, 0].reshape(D // 2, D)) + dot(theirs, wp[:, 1].reshape(D // 2, D))
     rows = (cells + normed(projected, attn_gain_ref[...])).astype(BF16)
     lowered = None
+    step = 16 // PIECES
     units = FF // PIECES
-    for i in range(PIECES):
-        for fetch in fetches[i]:
-            fetch.wait()
-        up = wu[i * step : (i + 1) * step].reshape(units, D)
-        down = wd[i * step : (i + 1) * step].reshape(units, D)
+    for i in range(0, 16, step):
+        up = wu[i : i + step].reshape(units, D)
+        down = wd[i : i + step].reshape(units, D)
         raised = dot_t(rows, up)
         hidden = 0.5 * raised * (1.0 + lax.erf(raised * (0.5**0.5)))
         part = dot(hidden.astype(BF16), down)
@@ -263,19 +259,37 @@
     )(spot, *quarters, mine, other, *constants, bias)
 
 
-def tokens(quarters, cells, gathered, attn_gain, mlp_gain):
+def staged(gathered):
+    sizes = [(16, 2, rows, D) for rows in (16, 64, 64)]
+    return pl.pallas_call(
+        stage_kernel,
+        in_specs=[fetched()],
+        out_specs=[pl.BlockSpec(memory_space=pltpu.VMEM)] * 3,
+        out_shape=[jax.ShapeDtypeStruct(size, BF16) for size in sizes],
+        scratch_shapes=[pltpu.SemaphoreType.DMA((3,))],
+        compiler_params=pltpu.CompilerParams(vmem_limit_bytes=STAGE_LIMIT),
+        cost_estimate=pl.CostEstimate(flops=0, bytes_accessed=2 * 144 * 32 * D * 2, transcendentals=0),
+        name="stage",
+    )(gathered)
+
+
+def tokens(spot, quarters, cells, weights, attn_gain, mlp_gain):
     out = (WLAT, WLON, LEVELS, D)
     return pl.pallas_call(
         token_kernel,
         grid=(1,),
-        in_specs=[whole(CORNER)] * 4 + [whole(out)] + [whole((1, D))] * 2 + [fetched()],
+        in_specs=[scalars()]
+        + [whole(CORNER)] * 4
+        + [whole(a.shape) for a in (cells, *weights)]
+        + [whole((1, D))] * 2,
         out_specs=whole(out),
         out_shape=jax.ShapeDtypeStruct(out, BF16),
-        scratch_shapes=[pltpu.VMEM((16, 2, rows, D), BF16) for rows in (16, 64, 64)]
-        + [pltpu.SemaphoreType.DMA((1 + 2 * PIECES,))],
-        compiler_params=params(),
+        compiler_params=pltpu.CompilerParams(vmem_limit_bytes=TOKENS_LIMIT),
         name="tokens",
-    )(*quarters, cells, attn_gain.reshape(1, D), mlp_gain.reshape(1, D), gathered)
+    )(
+        spot, *quarters, cells, *weights,
+        attn_gain.reshape(1, D), mlp_gain.reshape(1, D),
+    )
 
 
 def shards(
@@ -283,32 +297,33 @@
 ):
     own = packed(up_weight, down_weight, proj_weight)
     other = lax.ppermute(own, AXES, mirrored())
-    low_half = lax.axis_index("xh") == 0
-    both = jnp.stack([jnp.where(low_half, own, other), jnp.where(low_half, other, own)])
+    both = jnp.stack([own, other])
     gathered = lax.all_gather(both, ("z", "c"), axis=0, tiled=False)
 
+    qkv_weight, _ = lax.optimization_barrier((qkv_weight, both))
+    mine = lax.all_gather(qkv_weight, ("z", "c"), axis=0, tiled=False)
     cells = latent.transpose(1, 2, 0, 3)
+    cells_after, mine = lax.optimization_barrier((cells, mine))
     rolled = [
-        lax.ppermute(corner(cells, 1, 1), AXES, shifted(1, 1)),
-        lax.ppermute(corner(cells, 1, 0), AXES, shifted(1, 0)),
-        lax.ppermute(corner(cells, 0, 1), AXES, shifted(0, 1)),
-        corner(cells, 0, 0),
-    ]
-    qkv_weight, _, rolled = lax.optimization_barrier((qkv_weight, both, rolled))
-    mine = lax.all_gather(qkv_weight, ("z", "c"), axis=0, tiled=False)
+        lax.ppermute(corner(cells_after, 1, 1), AXES, shifted(1, 1)),
+        lax.ppermute(corner(cells_after, 1, 0), AXES, shifted(1, 0)),
+        lax.ppermute(corner(cells_after, 0, 1), AXES, shifted(0, 1)),
+        corner(cells_after, 0, 0),
+    ]
     core = lax.axis_index("c")
     sent = lax.dynamic_index_in_dim(mine.reshape(8, 2, 16, 3 * D), core, 1, keepdims=False)
     theirs = lax.all_gather(lax.ppermute(sent, AXES, mirrored()), "c", axis=0, tiled=False)
 
     spot = jnp.stack([lax.axis_index("xh"), (lax.axis_index(LAT) == 0).astype(jnp.int32)])
     attended = attention(spot, rolled, mine, theirs, position_bias)
+    attended, gathered = lax.optimization_barrier((attended, gathered))
     restored = [
         attended[3],
         lax.ppermute(attended[2], AXES, shifted(0, -1)),
         lax.ppermute(attended[1], AXES, shifted(-1, 0)),
         lax.ppermute(attended[0], AXES, shifted(-1, -1)),
     ]
-    return tokens(restored, cells, gathered, attn_gain, mlp_gain).transpose(2, 0, 1, 3)
+    return tokens(spot, restored, cells, staged(gathered), attn_gain, mlp_gain).transpose(2, 0, 1, 3)
 
 
 def solution(mesh):

time: 115 us -> 104 us (0.904)
  waiting for transfers between devices: 15.6 us -> 7.1 us
  starting transfers between devices: 34 us -> 29.8 us
  blocking collectives: 31 us -> 32.7 us
    ppermute x1, waiting for transfers between devices: 8.65 us -> 0.17 us  [shards(): lax.ppermute(sent, AXES, mirrored())]
    ppermute x3, starting transfers between devices: 12.5 us -> 6.91 us  [the longest x1 3.08 us: shards(): lax.ppermute(corner(cells_after, 1, 0), AXES, shifted(1, 0))]
    ppermute x1, starting transfers between devices: 6.53 us -> 2.28 us  [shards(): lax.ppermute(attended[0], AXES, shifted(-1, -1))]
    ppermute x1, starting transfers between devices: 2.28 us -> 6.21 us  [shards(): lax.ppermute(attended[2], AXES, shifted(0, -1))]
    all_gather x1, blocking collectives: 27.9 us -> 29.1 us  [shards(): mine = lax.all_gather(qkv_weight, ('z', 'c'), axis=0, tiled=False)]
    pallas_call x1 -> x2, Pallas kernels: 5.93 us -> 6.13 us  [the longest x1 3.7 us: tokens(): pl.pallas_call(token_kernel, grid=(1,), in_specs=[scalars()] + [whole(COR...]
  transfers between devices with their start and end apart: 9 -> 9, of which waited for: 4 -> 4; matrix products, arithmetic and copies ran while one was open for 2% -> 2% of each run, Pallas kernels for 7% -> 10%
where the time goes in v4:
time: 104 us
  blocking collectives  32.7 us (31%)
  starting transfers between devices  29.8 us (29%)
  Pallas kernels  15.7 us (15%)
  between operations  13.6 us (13%)
  waiting for transfers between devices  7.1 us (7%)
  local copies, waits for them, and re-layouts  2.43 us (2%)
  other arithmetic  2.21 us (2%)
    all_gather x1, blocking collectives, shards(): mine = lax.all_gather(qkv_weight, ('z', 'c'), axis=0, tiled=False)  29.1 us
    pallas_call x1, Pallas kernels, attention(): pl.pallas_call(attention_kernel, grid=(1,), in_specs=[scalars()] + [quart...  8.05 us
    ppermute x1, starting transfers between devices, shards(): lax.ppermute(attended[2], AXES, shifted(0, -1))  6.21 us
    ppermute x1, starting transfers between devices, shards(): other = lax.ppermute(own, AXES, mirrored())  5.22 us
    ppermute x1, starting transfers between devices, shards(): lax.ppermute(sent, AXES, mirrored())  5.15 us
    ppermute x1, starting transfers between devices, shards(): lax.ppermute(attended[1], AXES, shifted(-1, 0))  4.01 us
    pallas_call x1, Pallas kernels, tokens(): pl.pallas_call(token_kernel, grid=(1,), in_specs=[scalars()] + [whole(COR...  3.7 us
    all_gather x1, blocking collectives, shards(): lax.all_gather(lax.ppermute(sent, AXES, mirrored()), 'c', axis=0, tiled=F...  3.55 us
  transfers between devices with their start and end apart: 9, of which 4 were waited for; matrix products, arithmetic and copies ran while one was open for 2% of the time, Pallas kernels for 10%

profile of v4, /device:TPU:1, one launch (start us, length us, event | category | flops | bytes accessed | tf_op | source)
XLA Modules:
  0.0 103.5 jit_solution(58386235844353222)
XLA Ops:
  6.5 1.6 %pack.1 = bf16[144,512]{1,0:T(8,128)(2,1)} custom-call(bf16[64,512]{1,0:T(8,128)(2,1)} %up_ref.1, bf16[64,512]{1,0:T(8,128)(2,1)} %down_ref.1, bf16[16,512]{1,0:T(8,128)(2,1)} %proj_ref.1), custom_call_target="tpu_custom_call" | custom-call | tf_op jit(solution)/shard_map/pack/pallas_call | solution.py:232
  8.1 5.2 %collective-permute-start = (bf16[144,512]{1,0:T(8,128)(2,1)}, bf16[144,512]{1,0:T(8,128)(2,1)S(1)}, u32[]{:S(2)}, u32[]{:S(2)}) collective-permute-start(bf16[144,512]{1,0:T(8,128)(2,1)} %pack.1), channel_id=1, source_target_pairs={{0,272},{1,273},{2,274},{3,275},{4,276},{5,277},{6,278},{7,279},{8... | collective-permute-start | bytes 442376 | tf_op jit(solution)/shard_map/ppermute | solution.py:299
  13.3 2.7 %collective-permute-done = bf16[144,512]{1,0:T(8,128)(2,1)S(1)} collective-permute-done((bf16[144,512]{1,0:T(8,128)(2,1)}, bf16[144,512]{1,0:T(8,128)(2,1)S(1)}, u32[]{:S(2)}, u32[]{:S(2)}) %collective-permute-start) | collective-permute-done | bytes 147488 | tf_op jit(solution)/shard_map/ppermute | solution.py:299
  16.1 1.7 %pad_maximum_fusion = bf16[2,144,512]{2,1,0:T(8,128)(2,1)} fusion(bf16[1,144,512]{2,1,0:T(8,128)(2,1)S(1)} %bitcast.23, bf16[1,144,512]{2,1,0:T(8,128)(2,1)} %bitcast.22), kind=kLoop, calls=%fused_computation.1 | loop fusion | flops 147456 | bytes 589824 | tf_op jit(solution)/shard_map/stack | solution.py:300
  17.7 0.0 all-gather.5.cloned.1.call-update
  17.7 29.1 %all-gather = bf16[256,1536]{1,0:T(8,128)(2,1)S(1)} all-gather(bf16[16,1536]{1,0:T(8,128)(2,1)} %param.11), channel_id=2, replica_groups=mesh['xl'=2,'y'=8,'xh'=2,'z'=8,'c'=2] {'z','c'}, dimensions={0}, use_global_device_ids=true | all-gather | bytes 835584 | tf_op jit(solution)/shard_map/all_gather | solution.py:304
  46.9 5.2 %collective-permute-start.4 = (bf16[8,16,1536]{2,1,0:T(8,128)(2,1)S(1)}, bf16[8,16,1536]{2,1,0:T(8,128)(2,1)S(1)}, u32[]{:S(2)}, u32[]{:S(2)}) collective-permute-start(bf16[8,16,1536]{2,1,0:T(8,128)(2,1)S(1)} %dynamic-slice_bitcast_fusion), channel_id=1, source_target_pairs={{0,272},{1,273},{2,274},{3,275},{4,276},{5,277},{6,278},{7,279},{8... | collective-permute-start | bytes 1179656 | tf_op jit(solution)/shard_map/ppermute | solution.py:315
  52.0 0.6 pad_add_fusion.spot_ref
  52.6 1.8 %fusion = (bf16[3,6,4,512]{3,2,1,0:T(4,128)(2,1)}, bf16[3,6,4,512]{3,2,1,0:T(4,128)(2,1)S(1)}, bf16[3,6,4,512]{3,2,1,0:T(4,128)(2,1)S(1)}, bf16[3,6,4,512]{3,2,1,0:T(4,128)(2,1)S(1)}) fusion(bf16[6,12,4,512]{3,2,1,0:T(4,128)(2,1)} %bitcast.14), kind=kLoop, calls=%fused_computation.3 | loop fusion | bytes 589824 | tf_op jit(solution)/shard_map/slice | solution.py:101
  54.4 1.9 %collective-permute-start.3 = (bf16[3,6,4,512]{3,2,1,0:T(4,128)(2,1)S(1)}, bf16[3,6,4,512]{3,2,1,0:T(4,128)(2,1)S(1)}, u32[]{:S(2)}, u32[]{:S(2)}) collective-permute-start(bf16[3,6,4,512]{3,2,1,0:T(4,128)(2,1)S(1)} %get-tuple-element.36), channel_id=1, source_target_pairs={{0,1},{1,2},{2,3},{3,4},{4,5},{5,6},{6,7},{7,8},{8,9},{9,10},{10,1... | collective-permute-start | bytes 221192 | tf_op jit(solution)/shard_map/ppermute | solution.py:310
  56.3 3.1 %collective-permute-start.2 = (bf16[3,6,4,512]{3,2,1,0:T(4,128)(2,1)S(1)}, bf16[3,6,4,512]{3,2,1,0:T(4,128)(2,1)S(1)}, u32[]{:S(2)}, u32[]{:S(2)}) collective-permute-start(bf16[3,6,4,512]{3,2,1,0:T(4,128)(2,1)S(1)} %get-tuple-element.37), channel_id=1, source_target_pairs={{0,32},{1,33},{2,34},{3,35},{4,36},{5,37},{6,38},{7,39},{8,40},{9,... | collective-permute-start | bytes 221192 | tf_op jit(solution)/shard_map/ppermute | solution.py:309
  59.4 1.9 %collective-permute-start.1 = (bf16[3,6,4,512]{3,2,1,0:T(4,128)(2,1)S(1)}, bf16[3,6,4,512]{3,2,1,0:T(4,128)(2,1)S(1)}, u32[]{:S(2)}, u32[]{:S(2)}) collective-permute-start(bf16[3,6,4,512]{3,2,1,0:T(4,128)(2,1)S(1)} %get-tuple-element.38), channel_id=1, source_target_pairs={{0,33},{1,34},{2,35},{3,36},{4,37},{5,38},{6,39},{7,40},{8,41},{9,... | collective-permute-start | bytes 221192 | tf_op jit(solution)/shard_map/ppermute | solution.py:308
  61.3 0.2 collective-permute-done.4
  61.5 3.5 %all-gather.1 = bf16[16,16,1536]{2,1,0:T(8,128)(2,1)} all-gather(bf16[8,16,1536]{2,1,0:T(8,128)(2,1)S(1)} %collective-permute-done.4), channel_id=3, replica_groups=mesh['xl'=2,'y'=8,'xh'=2,'z'=8,'c'=2] {'c'}, dimensions={0}, use_global_device_ids=true | all-gather | bytes 1179648 | tf_op jit(solution)/shard_map/all_gather | solution.py:315
  65.0 0.0 collective-permute-done.3.r2
  65.0 0.0 collective-permute-done.2.r1
  65.0 2.1 %collective-permute-done.1.r0 = bf16[3,6,4,512]{3,2,1,0:T(4,128)(2,1)S(1)} collective-permute-done((bf16[3,6,4,512]{3,2,1,0:T(4,128)(2,1)S(1)}, bf16[3,6,4,512]{3,2,1,0:T(4,128)(2,1)S(1)}, u32[]{:S(2)}, u32[]{:S(2)}) %collective-permute-start.1) | collective-permute-done | bytes 73760 | tf_op jit(solution)/shard_map/ppermute | solution.py:308
  67.2 0.0 copy-done.6
  67.2 0.6 copy-done.8
  67.8 8.1 %attention.1 = (bf16[3,6,4,512]{3,2,1,0:T(4,128)(2,1)}, bf16[3,6,4,512]{3,2,1,0:T(4,128)(2,1)}, bf16[3,6,4,512]{3,2,1,0:T(4,128)(2,1)}, bf16[3,6,4,512]{3,2,1,0:T(4,128)(2,1)}) custom-call(s32[2]{0:T(128)} %pad_add_fusion.spot_ref, bf16[3,6,4,512]{3,2,1,0:T(4,128)(2,1)} %copy-done.8, bf16[3,6,4,512]{3,2,1,0:T(4,128)(2,1)} %copy-done.7, ...), custom_call_target="tpu_custom_call" | custom-call | tf_op jit(solution)/shard_map/attention/pallas_call | solution.py:247
  75.8 0.0 copy-start
  75.9 0.0 copy-start.2
  75.9 0.0 copy-start.3
  75.9 0.0 all-gather.5.cloned.1.call-done
  75.9 6.2 %collective-permute-start.5 = (bf16[3,6,4,512]{3,2,1,0:T(4,128)(2,1)}, bf16[3,6,4,512]{3,2,1,0:T(4,128)(2,1)S(1)}, u32[]{:S(2)}, u32[]{:S(2)}) collective-permute-start(bf16[3,6,4,512]{3,2,1,0:T(4,128)(2,1)} %get-tuple-element.28), channel_id=1, source_target_pairs={{0,31},{1,0},{2,1},{3,2},{4,3},{5,4},{6,5},{7,6},{8,7},{9,8},{10,9... | collective-permute-start | bytes 221192 | tf_op jit(solution)/shard_map/ppermute | solution.py:322
  82.1 4.0 %collective-permute-start.6 = (bf16[3,6,4,512]{3,2,1,0:T(4,128)(2,1)}, bf16[3,6,4,512]{3,2,1,0:T(4,128)(2,1)S(1)}, u32[]{:S(2)}, u32[]{:S(2)}) collective-permute-start(bf16[3,6,4,512]{3,2,1,0:T(4,128)(2,1)} %get-tuple-element.29), channel_id=1, source_target_pairs={{0,480},{1,481},{2,482},{3,483},{4,484},{5,485},{6,486},{7,487},{8... | collective-permute-start | bytes 221192 | tf_op jit(solution)/shard_map/ppermute | solution.py:323
  86.2 2.3 %collective-permute-start.7 = (bf16[3,6,4,512]{3,2,1,0:T(4,128)(2,1)}, bf16[3,6,4,512]{3,2,1,0:T(4,128)(2,1)S(1)}, u32[]{:S(2)}, u32[]{:S(2)}) collective-permute-start(bf16[3,6,4,512]{3,2,1,0:T(4,128)(2,1)} %get-tuple-element.30), channel_id=1, source_target_pairs={{0,511},{1,480},{2,481},{3,482},{4,483},{5,484},{6,485},{7,486},{8... | collective-permute-start | bytes 221192 | tf_op jit(solution)/shard_map/ppermute | solution.py:324
  88.4 2.4 %stage.1 = (bf16[16,2,16,512]{3,2,1,0:T(8,128)(2,1)S(1)}, bf16[16,2,64,512]{3,2,1,0:T(8,128)(2,1)S(1)}, bf16[16,2,64,512]{3,2,1,0:T(8,128)(2,1)S(1)}) custom-call(bf16[16,2,144,512]{3,2,1,0:T(8,128)(2,1)} %bitcast.20), custom_call_target="tpu_custom_call" | custom-call | bytes 9437184 | tf_op jit(solution)/shard_map/stage/pallas_call | solution.py:264
  90.9 0.0 collective-permute-done.5.m1
  90.9 0.0 collective-permute-done.6.m2
  90.9 2.0 %collective-permute-done.7.m3 = bf16[3,6,4,512]{3,2,1,0:T(4,128)(2,1)S(1)} collective-permute-done((bf16[3,6,4,512]{3,2,1,0:T(4,128)(2,1)}, bf16[3,6,4,512]{3,2,1,0:T(4,128)(2,1)S(1)}, u32[]{:S(2)}, u32[]{:S(2)}) %collective-permute-start.7) | collective-permute-done | bytes 73760 | tf_op jit(solution)/shard_map/ppermute | solution.py:324
  93.0 3.7 %tokens.1 = bf16[6,12,4,512]{3,2,1,0:T(4,128)(2,1)} custom-call(s32[2]{0:T(128)S(1)} %copy-done.4, bf16[3,6,4,512]{3,2,1,0:T(4,128)(2,1)S(1)} %copy-done.1, bf16[3,6,4,512]{3,2,1,0:T(4,128)(2,1)S(1)} %collective-permute-done.5.m1, bf16[3,6,4,512]{3,2,1,0:T(4,128)(2,1)S(1)} %collective-permute-done.6.m2, ...), custom_call_target="tpu_custom_call" | custom-call | tf_op jit(solution)/shard_map/tokens/pallas_call | solution.py:278
  (15 shorter events, 0.1 us)
Async XLA Ops:
  6.5 69.4 %all-gather.5.cloned.1.call-start = ((), (), s32[]{:S(2)}) async-start(), calls=%async_computation | async-start | bytes 5013504 | tf_op jit(solution)/shard_map/all_gather | solution.py:301
  8.1 8.0 %collective-permute-start = (bf16[144,512]{1,0:T(8,128)(2,1)}, bf16[144,512]{1,0:T(8,128)(2,1)S(1)}, u32[]{:S(2)}, u32[]{:S(2)}) collective-permute-start(bf16[144,512]{1,0:T(8,128)(2,1)} %pack.1), channel_id=1, source_target_pairs={{0,272},{1,273},{2,274},{3,275},{4,276},{5,277},{6,278},{7,279},{8... | collective-permute-start | bytes 442376 | tf_op jit(solution)/shard_map/ppermute | solution.py:299
  46.8 20.3 %copy-start.5 = (bf16[256,1536]{1,0:T(8,128)(2,1)}, bf16[256,1536]{1,0:T(8,128)(2,1)S(1)}, u32[]{:S(2)}) copy-start(bf16[256,1536]{1,0:T(8,128)(2,1)S(1)} %all-gather) | copy-start | bytes 2359300
  46.9 14.6 %collective-permute-start.4 = (bf16[8,16,1536]{2,1,0:T(8,128)(2,1)S(1)}, bf16[8,16,1536]{2,1,0:T(8,128)(2,1)S(1)}, u32[]{:S(2)}, u32[]{:S(2)}) collective-permute-start(bf16[8,16,1536]{2,1,0:T(8,128)(2,1)S(1)} %dynamic-slice_bitcast_fusion), channel_id=1, source_target_pairs={{0,272},{1,273},{2,274},{3,275},{4,276},{5,277},{6,278},{7,279},{8... | collective-permute-start | bytes 1179656 | tf_op jit(solution)/shard_map/ppermute | solution.py:315
  54.4 10.7 %collective-permute-start.3 = (bf16[3,6,4,512]{3,2,1,0:T(4,128)(2,1)S(1)}, bf16[3,6,4,512]{3,2,1,0:T(4,128)(2,1)S(1)}, u32[]{:S(2)}, u32[]{:S(2)}) collective-permute-start(bf16[3,6,4,512]{3,2,1,0:T(4,128)(2,1)S(1)} %get-tuple-element.36), channel_id=1, source_target_pairs={{0,1},{1,2},{2,3},{3,4},{4,5},{5,6},{6,7},{7,8},{8,9},{9,10},{10,1... | collective-permute-start | bytes 221192 | tf_op jit(solution)/shard_map/ppermute | solution.py:310
  56.3 8.7 %collective-permute-start.2 = (bf16[3,6,4,512]{3,2,1,0:T(4,128)(2,1)S(1)}, bf16[3,6,4,512]{3,2,1,0:T(4,128)(2,1)S(1)}, u32[]{:S(2)}, u32[]{:S(2)}) collective-permute-start(bf16[3,6,4,512]{3,2,1,0:T(4,128)(2,1)S(1)} %get-tuple-element.37), channel_id=1, source_target_pairs={{0,32},{1,33},{2,34},{3,35},{4,36},{5,37},{6,38},{7,39},{8,40},{9,... | collective-permute-start | bytes 221192 | tf_op jit(solution)/shard_map/ppermute | solution.py:309
  59.4 7.8 %collective-permute-start.1 = (bf16[3,6,4,512]{3,2,1,0:T(4,128)(2,1)S(1)}, bf16[3,6,4,512]{3,2,1,0:T(4,128)(2,1)S(1)}, u32[]{:S(2)}, u32[]{:S(2)}) collective-permute-start(bf16[3,6,4,512]{3,2,1,0:T(4,128)(2,1)S(1)} %get-tuple-element.38), channel_id=1, source_target_pairs={{0,33},{1,34},{2,35},{3,36},{4,37},{5,38},{6,39},{7,40},{8,41},{9,... | collective-permute-start | bytes 221192 | tf_op jit(solution)/shard_map/ppermute | solution.py:308
  65.0 2.1 %copy-start.6 = (bf16[3,6,4,512]{3,2,1,0:T(4,128)(2,1)}, bf16[3,6,4,512]{3,2,1,0:T(4,128)(2,1)S(1)}, u32[]{:S(2)}) copy-start(bf16[3,6,4,512]{3,2,1,0:T(4,128)(2,1)S(1)} %collective-permute-done.3.r2) | copy-start | bytes 221188
  65.0 2.1 %copy-start.7 = (bf16[3,6,4,512]{3,2,1,0:T(4,128)(2,1)}, bf16[3,6,4,512]{3,2,1,0:T(4,128)(2,1)S(1)}, u32[]{:S(2)}) copy-start(bf16[3,6,4,512]{3,2,1,0:T(4,128)(2,1)S(1)} %collective-permute-done.2.r1) | copy-start | bytes 221188
  67.1 0.6 copy-start.8
  75.8 17.1 %copy-start = (bf16[4,6,12,512]{3,0,2,1:T(4,128)(2,1)S(1)}, bf16[4,6,12,512]{3,0,2,1:T(4,128)(2,1)}, u32[]{:S(2)}) copy-start(bf16[4,6,12,512]{3,0,2,1:T(4,128)(2,1)} %param.10) | copy-start | bytes 884740
  75.8 17.1 %copy-start.1 = (bf16[3,6,4,512]{3,2,1,0:T(4,128)(2,1)S(1)}, bf16[3,6,4,512]{3,2,1,0:T(4,128)(2,1)}, u32[]{:S(2)}) copy-start(bf16[3,6,4,512]{3,2,1,0:T(4,128)(2,1)} %get-tuple-element.27.m0) | copy-start | bytes 221188
  75.9 17.1 %copy-start.2 = (f32[512]{0:T(512)S(1)}, f32[512]{0:T(512)}, u32[]{:S(2)}) copy-start(f32[512]{0:T(512)} %param.14) | copy-start | bytes 6148
  75.9 17.1 %copy-start.3 = (f32[512]{0:T(512)S(1)}, f32[512]{0:T(512)}, u32[]{:S(2)}) copy-start(f32[512]{0:T(512)} %param.17) | copy-start | bytes 6148
  75.9 17.1 %copy-start.4 = (s32[2]{0:T(128)S(1)}, s32[2]{0:T(128)}, u32[]{:S(2)}) copy-start(s32[2]{0:T(128)} %pad_add_fusion.spot_ref) | copy-start | bytes 28
  75.9 15.0 %collective-permute-start.5 = (bf16[3,6,4,512]{3,2,1,0:T(4,128)(2,1)}, bf16[3,6,4,512]{3,2,1,0:T(4,128)(2,1)S(1)}, u32[]{:S(2)}, u32[]{:S(2)}) collective-permute-start(bf16[3,6,4,512]{3,2,1,0:T(4,128)(2,1)} %get-tuple-element.28), channel_id=1, source_target_pairs={{0,31},{1,0},{2,1},{3,2},{4,3},{5,4},{6,5},{7,6},{8,7},{9,8},{10,9... | collective-permute-start | bytes 221192 | tf_op jit(solution)/shard_map/ppermute | solution.py:322
  82.1 8.8 %collective-permute-start.6 = (bf16[3,6,4,512]{3,2,1,0:T(4,128)(2,1)}, bf16[3,6,4,512]{3,2,1,0:T(4,128)(2,1)S(1)}, u32[]{:S(2)}, u32[]{:S(2)}) collective-permute-start(bf16[3,6,4,512]{3,2,1,0:T(4,128)(2,1)} %get-tuple-element.29), channel_id=1, source_target_pairs={{0,480},{1,481},{2,482},{3,483},{4,484},{5,485},{6,486},{7,487},{8... | collective-permute-start | bytes 221192 | tf_op jit(solution)/shard_map/ppermute | solution.py:323
  86.2 6.8 %collective-permute-start.7 = (bf16[3,6,4,512]{3,2,1,0:T(4,128)(2,1)}, bf16[3,6,4,512]{3,2,1,0:T(4,128)(2,1)S(1)}, u32[]{:S(2)}, u32[]{:S(2)}) collective-permute-start(bf16[3,6,4,512]{3,2,1,0:T(4,128)(2,1)} %get-tuple-element.30), channel_id=1, source_target_pairs={{0,511},{1,480},{2,481},{3,482},{4,483},{5,484},{6,485},{7,486},{8... | collective-permute-start | bytes 221192 | tf_op jit(solution)/shard_map/ppermute | solution.py:324
Sparse Core Ops, SparseCore 0:
  17.9 53.4 all-gather.4

commit v5 on v4

--- a/solution.py
+++ b/solution.py
@@ -21,12 +21,14 @@
 LANES = 128
 PER_GROUP = LANES // HEAD_DIM
 GROUPS = HEADS // PER_GROUP
+PADDED = 3 * LANES
 PIECES = 4
 MASKED = -1e30
 EPSILON = 1e-05
 F32 = jnp.float32
 BF16 = jnp.bfloat16
-VMEM_LIMIT = 60 * 1024 * 1024
+VMEM_LIMIT = 48 * 1024 * 1024
+ATTENTION_LIMIT = 32 * 1024 * 1024
 STAGE_LIMIT = 48 * 1024 * 1024
 TOKENS_LIMIT = 40 * 1024 * 1024
 
@@ -101,15 +103,28 @@
     return cells[i * HALF_LAT : (i + 1) * HALF_LAT, j * HALF_LON : (j + 1) * HALF_LON]
 
 
-def pack_kernel(up_ref, down_ref, proj_ref, out_ref, sems):
+def copy_all(pairs, sems):
     copies = [
-        pltpu.make_async_copy(source, out_ref.at[start : start + source.shape[0]], sems.at[i])
-        for i, (source, start) in enumerate(((up_ref, 0), (down_ref, 64), (proj_ref, 128)))
+        pltpu.make_async_copy(source, target, sems.at[i]) for i, (source, target) in enumerate(pairs)
     ]
     for copy in copies:
         copy.start()
     for copy in copies:
         copy.wait()
+
+
+def pack_kernel(up_ref, down_ref, proj_ref, cells_ref, c0, c1, c2, c3, own_ref, both_ref, sems):
+    parts = ((up_ref, 0, 64), (down_ref, 64, 128), (proj_ref, 128, 144))
+    pairs = [(part, own_ref.at[start:stop]) for part, start, stop in parts]
+    pairs += [(part, both_ref.at[0, start:stop]) for part, start, stop in parts]
+    for i, target in enumerate((c0, c1, c2, c3)):
+        lat, lon = HALF_LAT * (i // 2), HALF_LON * (i % 2)
+        pairs.append((cells_ref.at[lat : lat + HALF_LAT, lon : lon + HALF_LON], target))
+    copy_all(pairs, sems)
+
+
+def merge_kernel(both_ref, other_ref, out_ref, sems):
+    copy_all([(other_ref, out_ref.at[1])], sems)
 
 
 def attention_kernel(
@@ -131,55 +146,51 @@
     rows = lax.dot_general(hot, rows, (((0,), (0,)), ((), ())), preferred_element_type=F32)
     rows = rows.astype(BF16)
     low_half = spot_ref[0] == 0
+    low, high = rows[:, : D // 2], rows[:, D // 2 :]
+    ours, theirs = jnp.where(low_half, low, high), jnp.where(low_half, high, low)
 
     def projected(which):
         columns = slice(which * D, (which + 1) * D)
         mine = mine_ref[:, :, columns].reshape(D // 2, D)
         other = jnp.stack([other_ref[0, :, :, columns], other_ref[1, :, :, columns]], 1)
-        other = other.reshape(D // 2, D)
-        low = dot(rows[:, : D // 2], jnp.where(low_half, mine, other))
-        return (low + dot(rows[:, D // 2 :], jnp.where(low_half, other, mine))).astype(BF16)
+        return (dot(ours, mine) + dot(theirs, other.reshape(D // 2, D))).astype(BF16)
 
     queries, keys, values = projected(0), projected(1), projected(2)
     lane_head = lax.broadcasted_iota(jnp.int32, (1, LANES), 1) // HEAD_DIM
     zero = jnp.zeros((), BF16)
-    ones = jnp.ones((WN, LANES), BF16)
+    gap = jnp.zeros((PADDED - WN, 2 * LANES), BF16)
+    beyond = jnp.full((WN, PADDED - WN), MASKED, F32)
     query_tags = jnp.where(spot_ref[1] == 1, tags_ref[0], zero)
     key_tags = tags_ref[1]
     groups = []
     for group in range(GROUPS):
-        fetches[group].wait()
         lanes = slice(group * LANES, (group + 1) * LANES)
-        group_q, group_v = queries[:, lanes], values[:, lanes]
-        group_k = jnp.concatenate([keys[:, lanes], key_tags], 1)
-        total = None
+        group_q = jnp.concatenate([queries[:, lanes], query_tags], 1)
+        group_k, group_v = keys[:, lanes], values[:, lanes]
+        key_rows, value_rows = [], []
         for j in range(PER_GROUP):
             mine = lane_head == j
-            head_q = jnp.concatenate([jnp.where(mine, group_q, zero), query_tags], 1)
-            scores = dot_t(head_q, group_k) * HEAD_DIM ** (-0.5)
-            scores = scores + bias_ref[group * PER_GROUP + j].astype(F32)
-            weights = jnp.exp(scores - jnp.max(scores, -1, keepdims=True)).astype(BF16)
-            head_v = jnp.concatenate([jnp.where(mine, group_v, zero), ones], 1)
-            product = dot(weights, head_v)
-            part = product[:, :LANES] / product[:, LANES:]
-            total = part if total is None else total + part
-        groups.append(total.astype(BF16))
+            key_rows += [jnp.concatenate([jnp.where(mine, group_k, zero), key_tags], 1), gap]
+            sums = jnp.broadcast_to(jnp.where(mine, 1.0, 0.0).astype(BF16), (WN, LANES))
+            value_rows += [jnp.concatenate([jnp.where(mine, group_v, zero), sums], 1), gap]
+        scores = dot_t(group_q, jnp.concatenate(key_rows, 0))
+        fetches[group].wait()
+        weights = []
+        for j in range(PER_GROUP):
+            bias = bias_ref[group * PER_GROUP + j].astype(F32)
+            bias = jnp.concatenate([bias, beyond], 1)
+            head = scores[:, j * PADDED : (j + 1) * PADDED] * HEAD_DIM ** (-0.5) + bias
+            weights.append(jnp.exp(head - jnp.max(head, -1, keepdims=True)).astype(BF16))
+        product = dot(jnp.concatenate(weights, 1), jnp.concatenate(value_rows, 0))
+        groups.append((product[:, :LANES] / product[:, LANES:]).astype(BF16))
     attended = dot(hot, jnp.concatenate(groups, 1))
     for i, out in enumerate((o0, o1, o2, o3)):
         out[...] = attended[i * QUARTER : (i + 1) * QUARTER].reshape(CORNER).astype(BF16)
 
 
 def stage_kernel(gathered_ref, wp_ref, wu_ref, wd_ref, sems):
-    copies = [
-        pltpu.make_async_copy(gathered_ref.at[:, :, start:stop], target, sems.at[i])
-        for i, (start, stop, target) in enumerate(
-            ((128, 144, wp_ref), (0, 64, wu_ref), (64, 128, wd_ref))
-        )
-    ]
-    for copy in copies:
-        copy.start()
-    for copy in copies:
-        copy.wait()
+    parts = ((wp_ref, 128, 144), (wu_ref, 0, 64), (wd_ref, 64, 128))
+    copy_all([(gathered_ref.at[:, :, start:stop], target) for target, start, stop in parts], sems)
 
 
 def token_kernel(
@@ -220,43 +231,60 @@
     return pl.BlockSpec(memory_space=pltpu.SMEM)
 
 
+def held():
+    return pl.BlockSpec(memory_space=pltpu.VMEM)
+
+
 def fetched():
-    return pl.BlockSpec(memory_space=pl.ANY)
+    return pl.BlockSpec(memory_space=pltpu.HBM)
+
+
+def off_chip(*arrays):
+    return [pltpu.with_memory_space_constraint(a, pltpu.HBM) for a in arrays]
 
 
 def params():
     return pltpu.CompilerParams(vmem_limit_bytes=VMEM_LIMIT)
 
 
-def packed(up_weight, down_weight, proj_weight):
-    return pl.pallas_call(
+def packed(up_weight, down_weight, proj_weight, cells):
+    out = pl.pallas_call(
         pack_kernel,
-        grid=(1,),
-        in_specs=[fetched()] * 3,
-        out_specs=whole((144, D)),
-        out_shape=jax.ShapeDtypeStruct((144, D), BF16),
-        scratch_shapes=[pltpu.SemaphoreType.DMA((3,))],
+        in_specs=[fetched()] * 4,
+        out_specs=[held()] * 5 + [fetched()],
+        out_shape=[jax.ShapeDtypeStruct(CORNER, BF16)] * 4
+        + [jax.ShapeDtypeStruct(shape, BF16) for shape in ((144, D), (2, 144, D))],
+        scratch_shapes=[pltpu.SemaphoreType.DMA((10,))],
         compiler_params=params(),
         name="pack",
-    )(up_weight, down_weight, proj_weight)
+    )(*off_chip(up_weight, down_weight, proj_weight, cells))
+    return out[:4], out[4], out[5]
+
+
+def merged(both, other):
+    return pl.pallas_call(
+        merge_kernel,
+        in_specs=[fetched(), fetched()],
+        out_specs=fetched(),
+        out_shape=jax.ShapeDtypeStruct(both.shape, BF16),
+        scratch_shapes=[pltpu.SemaphoreType.DMA((1,))],
+        input_output_aliases={0: 0},
+        compiler_params=params(),
+        name="merge",
+    )(both, other)
 
 
 def attention(spot, quarters, mine, other, bias):
-    quarter = whole(CORNER)
     constants = (jnp.asarray(to_quarters(), BF16), jnp.asarray(tags(), BF16))
     return pl.pallas_call(
         attention_kernel,
-        grid=(1,),
-        in_specs=[scalars()]
-        + [quarter] * 4
-        + [whole(a.shape) for a in (mine, other, *constants)]
-        + [fetched()],
-        out_specs=[quarter] * 4,
+        in_specs=[scalars()] + [held()] * (len(quarters) + 4) + [fetched()],
+        out_specs=[held()] * 4,
         out_shape=[jax.ShapeDtypeStruct(CORNER, BF16)] * 4,
         scratch_shapes=[pltpu.VMEM(bias.shape, BF16), pltpu.SemaphoreType.DMA((GROUPS,))],
-        compiler_params=params(),
+        compiler_params=pltpu.CompilerParams(vmem_limit_bytes=ATTENTION_LIMIT),
         name="attention",
-    )(spot, *quarters, mine, other, *constants, bias)
+    )(spot, *quarters, mine, other, *constants, *off_chip(bias))
 
 
 def staged(gathered):
@@ -270,7 +298,7 @@
         compiler_params=pltpu.CompilerParams(vmem_limit_bytes=STAGE_LIMIT),
         cost_estimate=pl.CostEstimate(flops=0, bytes_accessed=2 * 144 * 32 * D * 2, transcendentals=0),
         name="stage",
-    )(gathered)
+    )(*off_chip(gathered))
 
 
 def tokens(spot, quarters, cells, weights, attn_gain, mlp_gain):
@@ -295,20 +323,18 @@
 def shards(
     latent, qkv_weight, proj_weight, position_bias, attn_gain, up_weight, down_weight, mlp_gain
 ):
-    own = packed(up_weight, down_weight, proj_weight)
-    other = lax.ppermute(own, AXES, mirrored())
-    both = jnp.stack([own, other])
+    cells = latent.transpose(1, 2, 0, 3)
+    corners, own, both = packed(up_weight, down_weight, proj_weight, cells)
+    both = merged(both, lax.ppermute(own, AXES, mirrored()))
     gathered = lax.all_gather(both, ("z", "c"), axis=0, tiled=False)
-
     qkv_weight, _ = lax.optimization_barrier((qkv_weight, both))
     mine = lax.all_gather(qkv_weight, ("z", "c"), axis=0, tiled=False)
-    cells = latent.transpose(1, 2, 0, 3)
-    cells_after, mine = lax.optimization_barrier((cells, mine))
+    corners, mine = lax.optimization_barrier((corners, mine))
     rolled = [
-        lax.ppermute(corner(cells_after, 1, 1), AXES, shifted(1, 1)),
-        lax.ppermute(corner(cells_after, 1, 0), AXES, shifted(1, 0)),
-        lax.ppermute(corner(cells_after, 0, 1), AXES, shifted(0, 1)),
-        corner(cells_after, 0, 0),
+        lax.ppermute(corners[3], AXES, shifted(1, 1)),
+        lax.ppermute(corners[2], AXES, shifted(1, 0)),
+        lax.ppermute(corners[1], AXES, shifted(0, 1)),
+        corners[0],
     ]
     core = lax.axis_index("c")
     sent = lax.dynamic_index_in_dim(mine.reshape(8, 2, 16, 3 * D), core, 1, keepdims=False)
@@ -316,7 +342,6 @@
 
     spot = jnp.stack([lax.axis_index("xh"), (lax.axis_index(LAT) == 0).astype(jnp.int32)])
     attended = attention(spot, rolled, mine, theirs, position_bias)
-    attended, gathered = lax.optimization_barrier((attended, gathered))
     restored = [
         attended[3],
         lax.ppermute(attended[2], AXES, shifted(0, -1)),

time: 104 us -> 102 us (0.981)
  Pallas kernels: 15.7 us -> 18.4 us
  local copies, waits for them, and re-layouts: 2.43 us -> 0.05 us
  other arithmetic: 2.21 us -> 0.08 us
  starting transfers between devices: 29.8 us -> 31.1 us
    pallas_call x2 -> x3, Pallas kernels: 9.61 us -> 12.3 us  [the longest x1 5.92 us: attention(): pl.pallas_call(attention_kernel, in_specs=[scalars()] + [held()] * (len(q...]
    ppermute x4, waiting for transfers between devices: 4.85 us -> 2.53 us  [the longest x1 2.52 us: shards(): both = merged(both, lax.ppermute(own, AXES, mirrored()))]
    ppermute x1, waiting for transfers between devices: 0.17 us -> 2.37 us  [shards(): lax.ppermute(sent, AXES, mirrored())]
    slice x1 -> x0, local copies, waits for them, and re-layouts: 1.75 us -> none  [corner(): cells[i * HALF_LAT:(i + 1) * HALF_LAT, j * HALF_LON:(j + 1) * HALF_LON]]
    another operation x1 -> x0, other arithmetic: 1.65 us -> none  [shards(): both = jnp.stack([own, other])]
  transfers between devices with their start and end apart: 9 -> 9, of which waited for: 4 -> 3; matrix products, arithmetic and copies ran while one was open for 2% -> 0% of each run, Pallas kernels for 10% -> 8%
where the time goes in v5:
time: 102 us
  blocking collectives  31.8 us (31%)
  starting transfers between devices  31.1 us (30%)
  Pallas kernels  18.4 us (18%)
  between operations  13.6 us (13%)
  waiting for transfers between devices  6.87 us (7%)
    all_gather x1, blocking collectives, shards(): mine = lax.all_gather(qkv_weight, ('z', 'c'), axis=0, tiled=False)  29.1 us
    ppermute x1, starting transfers between devices, shards(): lax.ppermute(attended[2], AXES, shifted(0, -1))  7.2 us
    pallas_call x1, Pallas kernels, attention(): pl.pallas_call(attention_kernel, in_specs=[scalars()] + [held()] * (len(q...  5.92 us
    pallas_call x1, Pallas kernels, packed(): pl.pallas_call(pack_kernel, in_specs=[fetched()] * 4, out_specs=[held()]...  5.66 us
    ppermute x1, starting transfers between devices, shards(): both = merged(both, lax.ppermute(own, AXES, mirrored()))  5.22 us
    ppermute x1, starting transfers between devices, shards(): lax.ppermute(sent, AXES, mirrored())  5.15 us
    ppermute x1, starting transfers between devices, shards(): lax.ppermute(attended[1], AXES, shifted(-1, 0))  4.48 us
    pallas_call x1, Pallas kernels, tokens(): pl.pallas_call(token_kernel, grid=(1,), in_specs=[scalars()] + [whole(COR...  3.69 us
  transfers between devices with their start and end apart: 9, of which 3 were waited for; matrix products, arithmetic and copies ran while one was open for 0% of the time, Pallas kernels for 8%

profile of v5, /device:TPU:1, one launch (start us, length us, event | category | flops | bytes accessed | tf_op | source)
XLA Modules:
  0.0 101.9 jit_solution(10929412844434221834)
XLA Ops:
  6.5 0.0 all-gather.5.cloned.1.call-start
  6.5 5.7 %pack.1 = (bf16[3,6,4,512]{3,2,1,0:T(4,128)(2,1)S(1)}, bf16[3,6,4,512]{3,2,1,0:T(4,128)(2,1)S(1)}, bf16[3,6,4,512]{3,2,1,0:T(4,128)(2,1)S(1)}, bf16[3,6,4,512]{3...) custom-call(bf16[64,512]{1,0:T(8,128)(2,1)} %up_ref.1, bf16[64,512]{1,0:T(8,128)(2,1)} %down_ref.1, ...), custom_call_target="tpu_custom_call" | custom-call | tf_op jit(solution)/shard_map/pack/pallas_call | solution.py:251
  12.2 5.2 %collective-permute-start = (bf16[144,512]{1,0:T(8,128)(2,1)S(1)}, bf16[144,512]{1,0:T(8,128)(2,1)S(1)}, u32[]{:S(2)}, u32[]{:S(2)}) collective-permute-start(bf16[144,512]{1,0:T(8,128)(2,1)S(1)} %get-tuple-element.29), channel_id=1, source_target_pairs={{0,272},{1,273},{2,274},{3,275},{4,276},{5,277},{6,278},{7,279},{8... | collective-permute-start | bytes 442376 | tf_op jit(solution)/shard_map/ppermute | solution.py:328
  17.4 2.5 %collective-permute-done.other_ref = bf16[144,512]{1,0:T(8,128)(2,1)S(1)} collective-permute-done((bf16[144,512]{1,0:T(8,128)(2,1)S(1)}, bf16[144,512]{1,0:T(8,128)(2,1)S(1)}, u32[]{:S(2)}, u32[]{:S(2)}) %collective-permute-start) | collective-permute-done | bytes 147488 | tf_op jit(solution)/shard_map/ppermute | solution.py:328
  20.0 0.7 merge.1
  20.6 0.0 all-gather.5.cloned.1.call-update
  20.7 29.1 %all-gather = bf16[256,1536]{1,0:T(8,128)(2,1)S(1)} all-gather(bf16[16,1536]{1,0:T(8,128)(2,1)} %param.11), channel_id=2, replica_groups=mesh['xl'=2,'y'=8,'xh'=2,'z'=8,'c'=2] {'z','c'}, dimensions={0}, use_global_device_ids=true | all-gather | bytes 835584 | tf_op jit(solution)/shard_map/all_gather | solution.py:331
  49.8 5.2 %collective-permute-start.4 = (bf16[8,16,1536]{2,1,0:T(8,128)(2,1)S(1)}, bf16[8,16,1536]{2,1,0:T(8,128)(2,1)S(1)}, u32[]{:S(2)}, u32[]{:S(2)}) collective-permute-start(bf16[8,16,1536]{2,1,0:T(8,128)(2,1)S(1)} %dynamic-slice_bitcast_fusion), channel_id=1, source_target_pairs={{0,272},{1,273},{2,274},{3,275},{4,276},{5,277},{6,278},{7,279},{8... | collective-permute-start | bytes 1179656 | tf_op jit(solution)/shard_map/ppermute | solution.py:341
  55.0 0.1 pad_add_fusion.spot_ref
  55.1 1.9 %collective-permute-start.1 = (bf16[3,6,4,512]{3,2,1,0:T(4,128)(2,1)S(1)}, bf16[3,6,4,512]{3,2,1,0:T(4,128)(2,1)S(1)}, u32[]{:S(2)}, u32[]{:S(2)}) collective-permute-start(bf16[3,6,4,512]{3,2,1,0:T(4,128)(2,1)S(1)} %get-tuple-element.31), channel_id=1, source_target_pairs={{0,33},{1,34},{2,35},{3,36},{4,37},{5,38},{6,39},{7,40},{8,41},{9,... | collective-permute-start | bytes 221192 | tf_op jit(solution)/shard_map/ppermute | solution.py:334
  57.0 3.1 %collective-permute-start.2 = (bf16[3,6,4,512]{3,2,1,0:T(4,128)(2,1)S(1)}, bf16[3,6,4,512]{3,2,1,0:T(4,128)(2,1)S(1)}, u32[]{:S(2)}, u32[]{:S(2)}) collective-permute-start(bf16[3,6,4,512]{3,2,1,0:T(4,128)(2,1)S(1)} %get-tuple-element.32), channel_id=1, source_target_pairs={{0,32},{1,33},{2,34},{3,35},{4,36},{5,37},{6,38},{7,39},{8,40},{9,... | collective-permute-start | bytes 221192 | tf_op jit(solution)/shard_map/ppermute | solution.py:335
  60.1 1.9 %collective-permute-start.3 = (bf16[3,6,4,512]{3,2,1,0:T(4,128)(2,1)S(1)}, bf16[3,6,4,512]{3,2,1,0:T(4,128)(2,1)S(1)}, u32[]{:S(2)}, u32[]{:S(2)}) collective-permute-start(bf16[3,6,4,512]{3,2,1,0:T(4,128)(2,1)S(1)} %get-tuple-element.33), channel_id=1, source_target_pairs={{0,1},{1,2},{2,3},{3,4},{4,5},{5,6},{6,7},{7,8},{8,9},{9,10},{10,1... | collective-permute-start | bytes 221192 | tf_op jit(solution)/shard_map/ppermute | solution.py:336
  62.0 2.4 %collective-permute-done.4 = bf16[8,16,1536]{2,1,0:T(8,128)(2,1)S(1)} collective-permute-done((bf16[8,16,1536]{2,1,0:T(8,128)(2,1)S(1)}, bf16[8,16,1536]{2,1,0:T(8,128)(2,1)S(1)}, u32[]{:S(2)}, u32[]{:S(2)}) %collective-permute-start.4) | collective-permute-done | bytes 393248 | tf_op jit(solution)/shard_map/ppermute | solution.py:341
  64.4 2.7 %all-gather.1 = bf16[16,16,1536]{2,1,0:T(8,128)(2,1)S(1)} all-gather(bf16[8,16,1536]{2,1,0:T(8,128)(2,1)S(1)} %collective-permute-done.4), channel_id=3, replica_groups=mesh['xl'=2,'y'=8,'xh'=2,'z'=8,'c'=2] {'c'}, dimensions={0}, use_global_device_ids=true | all-gather | bytes 1179648 | tf_op jit(solution)/shard_map/all_gather | solution.py:341
  67.0 0.0 collective-permute-done.1.r0
  67.0 0.0 collective-permute-done.2.r1
  67.1 0.0 collective-permute-done.3.r2
  67.1 0.0 copy-done.1
  67.1 0.0 copy-done.2
  67.1 5.9 %attention.1 = (bf16[3,6,4,512]{3,2,1,0:T(4,128)(2,1)S(1)}, bf16[3,6,4,512]{3,2,1,0:T(4,128)(2,1)S(1)}, bf16[3,6,4,512]{3,2,1,0:T(4,128)(2,1)S(1)}, bf16[3,6,4,512]{3,2,1,0:T(4,128)(2,1)S(1)}) custom-call(s32[2]{0:T(128)S(1)} %pad_add_fusion.spot_ref, bf16[3,6,4,512]{3,2,1,0:T(4,128)(2,1)S(1)} %collective-permute-done.1.r0, ...), custom_call_target="tpu_custom_call" | custom-call | tf_op jit(solution)/shard_map/attention/pallas_call | solution.py:279
  73.0 0.0 copy-start
  73.0 0.0 copy-start.3
  73.0 0.0 copy-start.4
  73.0 7.2 %collective-permute-start.5 = (bf16[3,6,4,512]{3,2,1,0:T(4,128)(2,1)S(1)}, bf16[3,6,4,512]{3,2,1,0:T(4,128)(2,1)S(1)}, u32[]{:S(2)}, u32[]{:S(2)}) collective-permute-start(bf16[3,6,4,512]{3,2,1,0:T(4,128)(2,1)S(1)} %get-tuple-element.37), channel_id=1, source_target_pairs={{0,31},{1,0},{2,1},{3,2},{4,3},{5,4},{6,5},{7,6},{8,7},{9,8},{10,9... | collective-permute-start | bytes 221192 | tf_op jit(solution)/shard_map/ppermute | solution.py:347
  80.2 4.5 %collective-permute-start.6 = (bf16[3,6,4,512]{3,2,1,0:T(4,128)(2,1)S(1)}, bf16[3,6,4,512]{3,2,1,0:T(4,128)(2,1)S(1)}, u32[]{:S(2)}, u32[]{:S(2)}) collective-permute-start(bf16[3,6,4,512]{3,2,1,0:T(4,128)(2,1)S(1)} %get-tuple-element.38), channel_id=1, source_target_pairs={{0,480},{1,481},{2,482},{3,483},{4,484},{5,485},{6,486},{7,487},{8... | collective-permute-start | bytes 221192 | tf_op jit(solution)/shard_map/ppermute | solution.py:348
  84.7 2.1 %collective-permute-start.7 = (bf16[3,6,4,512]{3,2,1,0:T(4,128)(2,1)S(1)}, bf16[3,6,4,512]{3,2,1,0:T(4,128)(2,1)S(1)}, u32[]{:S(2)}, u32[]{:S(2)}) collective-permute-start(bf16[3,6,4,512]{3,2,1,0:T(4,128)(2,1)S(1)} %get-tuple-element.39), channel_id=1, source_target_pairs={{0,511},{1,480},{2,481},{3,482},{4,483},{5,484},{6,485},{7,486},{8... | collective-permute-start | bytes 221192 | tf_op jit(solution)/shard_map/ppermute | solution.py:349
  86.9 0.0 all-gather.5.cloned.1.call-done
  86.9 2.4 %stage.1 = (bf16[16,2,16,512]{3,2,1,0:T(8,128)(2,1)S(1)}, bf16[16,2,64,512]{3,2,1,0:T(8,128)(2,1)S(1)}, bf16[16,2,64,512]{3,2,1,0:T(8,128)(2,1)S(1)}) custom-call(bf16[16,2,144,512]{3,2,1,0:T(8,128)(2,1)} %bitcast.19), custom_call_target="tpu_custom_call" | custom-call | bytes 9437184 | tf_op jit(solution)/shard_map/stage/pallas_call | solution.py:292
  89.4 0.0 collective-permute-done.5.m1
  89.4 0.0 collective-permute-done.6.m2
  89.4 1.9 %collective-permute-done.7.m3 = bf16[3,6,4,512]{3,2,1,0:T(4,128)(2,1)S(1)} collective-permute-done((bf16[3,6,4,512]{3,2,1,0:T(4,128)(2,1)S(1)}, bf16[3,6,4,512]{3,2,1,0:T(4,128)(2,1)S(1)}, u32[]{:S(2)}, u32[]{:S(2)}) %collective-permute-start.7) | collective-permute-done | bytes 73760 | tf_op jit(solution)/shard_map/ppermute | solution.py:349
  91.3 3.7 %tokens.1 = bf16[6,12,4,512]{3,2,1,0:T(4,128)(2,1)} custom-call(s32[2]{0:T(128)S(1)} %pad_add_fusion.spot_ref, bf16[3,6,4,512]{3,2,1,0:T(4,128)(2,1)S(1)} %get-tuple-element.36.m0, bf16[3,6,4,512]{3,2,1,0:T(4,128)(2,1)S(1)} %collective-permute-done.5.m1, bf16[3,6,4,512]{3,2,1,0:T(4,128)(2,1)S(1)} %collective-permute-done.6.m2, ...), custom_call_target="tpu_custom_call" | custom-call | tf_op jit(solution)/shard_map/tokens/pallas_call | solution.py:306
  (6 shorter events, 0.0 us)
Async XLA Ops:
  6.5 60.5 %copy-start.1 = (bf16[288,288]{1,0:T(8,128)(2,1)S(1)}, bf16[288,288]{1,0:T(8,128)(2,1)}, u32[]{:S(2)}) copy-start(bf16[288,288]{1,0:T(8,128)(2,1)} %constant.31.clone.hot_ref) | copy-start | bytes 497668
  6.5 60.5 %copy-start.2 = (bf16[2,288,128]{2,1,0:T(8,128)(2,1)S(1)}, bf16[2,288,128]{2,1,0:T(8,128)(2,1)}, u32[]{:S(2)}) copy-start(bf16[2,288,128]{2,1,0:T(8,128)(2,1)} %constant.32.clone.tags_ref) | copy-start | bytes 442372
  6.5 80.4 %all-gather.5.cloned.1.call-start = ((), (), s32[]{:S(2)}) async-start(), calls=%async_computation | async-start | bytes 5013504 | tf_op jit(solution)/shard_map/all_gather | solution.py:329
  12.2 7.7 %collective-permute-start = (bf16[144,512]{1,0:T(8,128)(2,1)S(1)}, bf16[144,512]{1,0:T(8,128)(2,1)S(1)}, u32[]{:S(2)}, u32[]{:S(2)}) collective-permute-start(bf16[144,512]{1,0:T(8,128)(2,1)S(1)} %get-tuple-element.29), channel_id=1, source_target_pairs={{0,272},{1,273},{2,274},{3,275},{4,276},{5,277},{6,278},{7,279},{8... | collective-permute-start | bytes 442376 | tf_op jit(solution)/shard_map/ppermute | solution.py:328
  49.8 14.6 %collective-permute-start.4 = (bf16[8,16,1536]{2,1,0:T(8,128)(2,1)S(1)}, bf16[8,16,1536]{2,1,0:T(8,128)(2,1)S(1)}, u32[]{:S(2)}, u32[]{:S(2)}) collective-permute-start(bf16[8,16,1536]{2,1,0:T(8,128)(2,1)S(1)} %dynamic-slice_bitcast_fusion), channel_id=1, source_target_pairs={{0,272},{1,273},{2,274},{3,275},{4,276},{5,277},{6,278},{7,279},{8... | collective-permute-start | bytes 1179656 | tf_op jit(solution)/shard_map/ppermute | solution.py:341
  55.1 12.0 %collective-permute-start.1 = (bf16[3,6,4,512]{3,2,1,0:T(4,128)(2,1)S(1)}, bf16[3,6,4,512]{3,2,1,0:T(4,128)(2,1)S(1)}, u32[]{:S(2)}, u32[]{:S(2)}) collective-permute-start(bf16[3,6,4,512]{3,2,1,0:T(4,128)(2,1)S(1)} %get-tuple-element.31), channel_id=1, source_target_pairs={{0,33},{1,34},{2,35},{3,36},{4,37},{5,38},{6,39},{7,40},{8,41},{9,... | collective-permute-start | bytes 221192 | tf_op jit(solution)/shard_map/ppermute | solution.py:334
  57.0 10.1 %collective-permute-start.2 = (bf16[3,6,4,512]{3,2,1,0:T(4,128)(2,1)S(1)}, bf16[3,6,4,512]{3,2,1,0:T(4,128)(2,1)S(1)}, u32[]{:S(2)}, u32[]{:S(2)}) collective-permute-start(bf16[3,6,4,512]{3,2,1,0:T(4,128)(2,1)S(1)} %get-tuple-element.32), channel_id=1, source_target_pairs={{0,32},{1,33},{2,34},{3,35},{4,36},{5,37},{6,38},{7,39},{8,40},{9,... | collective-permute-start | bytes 221192 | tf_op jit(solution)/shard_map/ppermute | solution.py:335
  60.1 7.0 %collective-permute-start.3 = (bf16[3,6,4,512]{3,2,1,0:T(4,128)(2,1)S(1)}, bf16[3,6,4,512]{3,2,1,0:T(4,128)(2,1)S(1)}, u32[]{:S(2)}, u32[]{:S(2)}) collective-permute-start(bf16[3,6,4,512]{3,2,1,0:T(4,128)(2,1)S(1)} %get-tuple-element.33), channel_id=1, source_target_pairs={{0,1},{1,2},{2,3},{3,4},{4,5},{5,6},{6,7},{7,8},{8,9},{9,10},{10,1... | collective-permute-start | bytes 221192 | tf_op jit(solution)/shard_map/ppermute | solution.py:336
  73.0 18.3 %copy-start = (bf16[4,6,12,512]{3,0,2,1:T(4,128)(2,1)S(1)}, bf16[4,6,12,512]{3,0,2,1:T(4,128)(2,1)}, u32[]{:S(2)}) copy-start(bf16[4,6,12,512]{3,0,2,1:T(4,128)(2,1)} %param.10) | copy-start | bytes 884740
  73.0 18.3 %copy-start.3 = (f32[512]{0:T(512)S(1)}, f32[512]{0:T(512)}, u32[]{:S(2)}) copy-start(f32[512]{0:T(512)} %param.14) | copy-start | bytes 6148
  73.0 18.3 %copy-start.4 = (f32[512]{0:T(512)S(1)}, f32[512]{0:T(512)}, u32[]{:S(2)}) copy-start(f32[512]{0:T(512)} %param.17) | copy-start | bytes 6148
  73.0 16.3 %collective-permute-start.5 = (bf16[3,6,4,512]{3,2,1,0:T(4,128)(2,1)S(1)}, bf16[3,6,4,512]{3,2,1,0:T(4,128)(2,1)S(1)}, u32[]{:S(2)}, u32[]{:S(2)}) collective-permute-start(bf16[3,6,4,512]{3,2,1,0:T(4,128)(2,1)S(1)} %get-tuple-element.37), channel_id=1, source_target_pairs={{0,31},{1,0},{2,1},{3,2},{4,3},{5,4},{6,5},{7,6},{8,7},{9,8},{10,9... | collective-permute-start | bytes 221192 | tf_op jit(solution)/shard_map/ppermute | solution.py:347
  80.2 9.1 %collective-permute-start.6 = (bf16[3,6,4,512]{3,2,1,0:T(4,128)(2,1)S(1)}, bf16[3,6,4,512]{3,2,1,0:T(4,128)(2,1)S(1)}, u32[]{:S(2)}, u32[]{:S(2)}) collective-permute-start(bf16[3,6,4,512]{3,2,1,0:T(4,128)(2,1)S(1)} %get-tuple-element.38), channel_id=1, source_target_pairs={{0,480},{1,481},{2,482},{3,483},{4,484},{5,485},{6,486},{7,487},{8... | collective-permute-start | bytes 221192 | tf_op jit(solution)/shard_map/ppermute | solution.py:348
  84.7 6.6 %collective-permute-start.7 = (bf16[3,6,4,512]{3,2,1,0:T(4,128)(2,1)S(1)}, bf16[3,6,4,512]{3,2,1,0:T(4,128)(2,1)S(1)}, u32[]{:S(2)}, u32[]{:S(2)}) collective-permute-start(bf16[3,6,4,512]{3,2,1,0:T(4,128)(2,1)S(1)} %get-tuple-element.39), channel_id=1, source_target_pairs={{0,511},{1,480},{2,481},{3,482},{4,483},{5,484},{6,485},{7,486},{8... | collective-permute-start | bytes 221192 | tf_op jit(solution)/shard_map/ppermute | solution.py:349
Sparse Core Ops, SparseCore 0:
  20.8 53.4 all-gather.4

commit v6 on v5

--- a/solution.py
+++ b/solution.py
@@ -46,17 +46,21 @@
     return [(place(a, o), place(a + dlat, o + dlon)) for a in range(16) for o in range(32)]
 
 
-def mirrored():
+def mirrored_pairs():
     def at(x, y, z, c):
         return (((x % 2) * 8 + y) * 2 + x // 2) * 16 + z * 2 + c
 
     return [
-        (at(x, y, z, c), at(3 - x, y, z, c))
-        for x in range(4)
+        [at(x, y, z, c), at(3 - x, y, z, c)]
+        for x in range(2)
         for y in range(8)
         for z in range(8)
         for c in range(2)
     ]
+
+
+def mirrored():
+    return [pair for a, b in mirrored_pairs() for pair in ((a, b), (b, a))]
 
 
 def to_quarters():
@@ -113,18 +117,9 @@
         copy.wait()
 
 
-def pack_kernel(up_ref, down_ref, proj_ref, cells_ref, c0, c1, c2, c3, own_ref, both_ref, sems):
+def pack_kernel(up_ref, down_ref, proj_ref, own_ref, sems):
     parts = ((up_ref, 0, 64), (down_ref, 64, 128), (proj_ref, 128, 144))
-    pairs = [(part, own_ref.at[start:stop]) for part, start, stop in parts]
-    pairs += [(part, both_ref.at[0, start:stop]) for part, start, stop in parts]
-    for i, target in enumerate((c0, c1, c2, c3)):
-        lat, lon = HALF_LAT * (i // 2), HALF_LON * (i % 2)
-        pairs.append((cells_ref.at[lat : lat + HALF_LAT, lon : lon + HALF_LON], target))
-    copy_all(pairs, sems)
-
-
-def merge_kernel(both_ref, other_ref, out_ref, sems):
-    copy_all([(other_ref, out_ref.at[1])], sems)
+    copy_all([(part, own_ref.at[start:stop]) for part, start, stop in parts], sems)
 
 
 def attention_kernel(
@@ -194,14 +189,12 @@
 
 
 def token_kernel(
-    spot_ref, m0, m1, m2, m3, cells_ref, wp, wu, wd, attn_gain_ref, mlp_gain_ref, out_ref
+    m0, m1, m2, m3, cells_ref, wp, wu, wd, attn_gain_ref, mlp_gain_ref, out_ref
 ):
     attended = stacked([m[...] for m in (m0, m1, m2, m3)]).astype(BF16)
     cells = stacked([corner(cells_ref, i, j) for i in range(2) for j in range(2)])
-    low_half = spot_ref[0] == 0
-    low, high = attended[:, : D // 2], attended[:, D // 2 :]
-    ours, theirs = jnp.where(low_half, low, high), jnp.where(low_half, high, low)
-    projected = dot(ours, wp[:, 0].reshape(D // 2, D)) + dot(theirs, wp[:, 1].reshape(D // 2, D))
+    low = dot(attended[:, : D // 2], wp[:, 0].reshape(D // 2, D))
+    projected = low + dot(attended[:, D // 2 :], wp[:, 1].reshape(D // 2, D))
     rows = (cells + normed(projected, attn_gain_ref[...])).astype(BF16)
     lowered = None
     step = 16 // PIECES
@@ -247,31 +240,16 @@
     return pltpu.CompilerParams(vmem_limit_bytes=VMEM_LIMIT)
 
 
-def packed(up_weight, down_weight, proj_weight, cells):
-    out = pl.pallas_call(
+def packed(up_weight, down_weight, proj_weight):
+    return pl.pallas_call(
         pack_kernel,
-        in_specs=[fetched()] * 4,
-        out_specs=[held()] * 5 + [fetched()],
-        out_shape=[jax.ShapeDtypeStruct(CORNER, BF16)] * 4
-        + [jax.ShapeDtypeStruct(shape, BF16) for shape in ((144, D), (2, 144, D))],
-        scratch_shapes=[pltpu.SemaphoreType.DMA((10,))],
+        in_specs=[fetched()] * 3,
+        out_specs=held(),
+        out_shape=jax.ShapeDtypeStruct((144, D), BF16),
+        scratch_shapes=[pltpu.SemaphoreType.DMA((3,))],
         compiler_params=params(),
         name="pack",
-    )(*off_chip(up_weight, down_weight, proj_weight, cells))
-    return out[:4], out[4], out[5]
-
-
-def merged(both, other):
-    return pl.pallas_call(
-        merge_kernel,
-        in_specs=[fetched(), fetched()],
-        out_specs=fetched(),
-        out_shape=jax.ShapeDtypeStruct(both.shape, BF16),
-        scratch_shapes=[pltpu.SemaphoreType.DMA((1,))],
-        input_output_aliases={0: 0},
-        compiler_params=params(),
-        name="merge",
-    )(both, other)
+    )(*off_chip(up_weight, down_weight, proj_weight))
 
 
 def attention(spot, quarters, mine, other, bias):
@@ -301,40 +279,36 @@
     )(*off_chip(gathered))
 
 
-def tokens(spot, quarters, cells, weights, attn_gain, mlp_gain):
+def tokens(quarters, cells, weights, attn_gain, mlp_gain):
     out = (WLAT, WLON, LEVELS, D)
     return pl.pallas_call(
         token_kernel,
         grid=(1,),
-        in_specs=[scalars()]
-        + [whole(CORNER)] * 4
+        in_specs=[whole(CORNER)] * 4
         + [whole(a.shape) for a in (cells, *weights)]
         + [whole((1, D))] * 2,
         out_specs=whole(out),
         out_shape=jax.ShapeDtypeStruct(out, BF16),
         compiler_params=pltpu.CompilerParams(vmem_limit_bytes=TOKENS_LIMIT),
         name="tokens",
-    )(
-        spot, *quarters, cells, *weights,
-        attn_gain.reshape(1, D), mlp_gain.reshape(1, D),
-    )
+    )(*quarters, cells, *weights, attn_gain.reshape(1, D), mlp_gain.reshape(1, D))
 
 
 def shards(
     latent, qkv_weight, proj_weight, position_bias, attn_gain, up_weight, down_weight, mlp_gain
 ):
-    cells = latent.transpose(1, 2, 0, 3)
-    corners, own, both = packed(up_weight, down_weight, proj_weight, cells)
-    both = merged(both, lax.ppermute(own, AXES, mirrored()))
+    own = packed(up_weight, down_weight, proj_weight)
+    both = lax.all_gather(own, AXES, axis=0, tiled=False, axis_index_groups=mirrored_pairs())
     gathered = lax.all_gather(both, ("z", "c"), axis=0, tiled=False)
     qkv_weight, _ = lax.optimization_barrier((qkv_weight, both))
     mine = lax.all_gather(qkv_weight, ("z", "c"), axis=0, tiled=False)
-    corners, mine = lax.optimization_barrier((corners, mine))
+    cells = latent.transpose(1, 2, 0, 3)
+    cells_after, mine = lax.optimization_barrier((cells, mine))
     rolled = [
-        lax.ppermute(corners[3], AXES, shifted(1, 1)),
-        lax.ppermute(corners[2], AXES, shifted(1, 0)),
-        lax.ppermute(corners[1], AXES, shifted(0, 1)),
-        corners[0],
+        lax.ppermute(corner(cells_after, 1, 1), AXES, shifted(1, 1)),
+        lax.ppermute(corner(cells_after, 1, 0), AXES, shifted(1, 0)),
+        lax.ppermute(corner(cells_after, 0, 1), AXES, shifted(0, 1)),
+        corner(cells_after, 0, 0),
     ]
     core = lax.axis_index("c")
     sent = lax.dynamic_index_in_dim(mine.reshape(8, 2, 16, 3 * D), core, 1, keepdims=False)
@@ -348,7 +322,7 @@
         lax.ppermute(attended[1], AXES, shifted(-1, 0)),
         lax.ppermute(attended[0], AXES, shifted(-1, -1)),
     ]
-    return tokens(spot, restored, cells, staged(gathered), attn_gain, mlp_gain).transpose(2, 0, 1, 3)
+    return tokens(restored, cells, staged(gathered), attn_gain, mlp_gain).transpose(2, 0, 1, 3)
 
 
 def solution(mesh):

time: 102 us -> 95.7 us (0.938)
  blocking collectives: 31.8 us -> 38.6 us
  starting transfers between devices: 31.1 us -> 24.5 us
  Pallas kernels: 18.4 us -> 12.4 us
  waiting for transfers between devices: 6.87 us -> 5 us
  local copies, waits for them, and re-layouts: 0.05 us -> 1.17 us
    all_gather x0 -> x1, blocking collectives: none -> 6.6 us  [shards(): lax.all_gather(own, AXES, axis=0, tiled=False, axis_index_groups=mirrored...]
    pallas_call x3 -> x2, Pallas kernels: 10 us -> 4.11 us  [the longest x1 3.17 us: tokens(): pl.pallas_call(token_kernel, grid=(1,), in_specs=[whole(CORNER)] * 4 + [w...]
    ppermute x4 -> x3, starting transfers between devices: 12.2 us -> 6.95 us  [the longest x1 3.11 us: shards(): lax.ppermute(corner(cells_after, 1, 0), AXES, shifted(1, 0))]
    ppermute x1, waiting for transfers between devices: 2.37 us -> 1.24 us  [shards(): lax.ppermute(sent, AXES, mirrored())]
    slice x0 -> x1, local copies, waits for them, and re-layouts: none -> 1.11 us  [corner(): cells[i * HALF_LAT:(i + 1) * HALF_LAT, j * HALF_LON:(j + 1) * HALF_LON]]
    ppermute x4 -> x3, waiting for transfers between devices: 2.53 us -> 1.71 us  [the longest x1 1.7 us: shards(): lax.ppermute(corner(cells_after, 1, 1), AXES, shifted(1, 1))]
  transfers between devices with their start and end apart: 9 -> 8, of which waited for: 3 -> 3; matrix products, arithmetic and copies ran while one was open for 0% -> 1% of each run, Pallas kernels for 8% -> 9%
where the time goes in v6:
time: 95.7 us; the launch traced here: 95.3 us
  blocking collectives  38.6 us (40%)
  starting transfers between devices  24.5 us (26%)
  between operations  13.5 us (14%)
  Pallas kernels  12.4 us (13%)
  waiting for transfers between devices  5 us (5%)
  local copies, waits for them, and re-layouts  1.17 us (1%)
    all_gather x1, blocking collectives, shards(): mine = lax.all_gather(qkv_weight, ('z', 'c'), axis=0, tiled=False)  29.1 us
    all_gather x1, blocking collectives, shards(): lax.all_gather(own, AXES, axis=0, tiled=False, axis_index_groups=mirrored...  6.6 us
    ppermute x1, starting transfers between devices, shards(): lax.ppermute(attended[2], AXES, shifted(0, -1))  6.18 us
    pallas_call x1, Pallas kernels, attention(): pl.pallas_call(attention_kernel, in_specs=[scalars()] + [held()] * (len(q...  5.9 us
    ppermute x1, starting transfers between devices, shards(): lax.ppermute(sent, AXES, mirrored())  5.15 us
    ppermute x1, starting transfers between devices, shards(): lax.ppermute(attended[1], AXES, shifted(-1, 0))  4.13 us
    pallas_call x1, Pallas kernels, tokens(): pl.pallas_call(token_kernel, grid=(1,), in_specs=[whole(CORNER)] * 4 + [w...  3.17 us
    ppermute x1, starting transfers between devices, shards(): lax.ppermute(corner(cells_after, 1, 0), AXES, shifted(1, 0))  3.11 us
  transfers between devices with their start and end apart: 8, of which 3 were waited for; matrix products, arithmetic and copies ran while one was open for 1% of the time, Pallas kernels for 9%

profile of v6, /device:TPU:1, one launch (start us, length us, event | category | flops | bytes accessed | tf_op | source)
XLA Modules:
  0.0 95.3 jit_solution(919519534021460136)
XLA Ops:
  6.5 0.0 all-gather.6.cloned.1.call-start
  6.5 0.9 pack.1
  7.5 6.6 %all-gather = bf16[288,512]{1,0:T(8,128)(2,1)} all-gather(bf16[144,512]{1,0:T(8,128)(2,1)S(1)} %pack.1), channel_id=2, replica_groups={{0,272},{1,273},{2,274},{3,275},{4,276},{5,277},{6,278},{7,279},{8,280}..., dimensions={0}, use_global_device_ids=true | all-gather | bytes 442368 | tf_op jit(solution)/shard_map/all_gather | solution.py:301
  14.1 0.0 all-gather.6.cloned.1.call-update
  14.1 29.1 %all-gather.1 = bf16[256,1536]{1,0:T(8,128)(2,1)S(1)} all-gather(bf16[16,1536]{1,0:T(8,128)(2,1)} %param.11), channel_id=3, replica_groups=mesh['xl'=2,'y'=8,'xh'=2,'z'=8,'c'=2] {'z','c'}, dimensions={0}, use_global_device_ids=true | all-gather | bytes 835584 | tf_op jit(solution)/shard_map/all_gather | solution.py:304
  43.3 5.2 %collective-permute-start.3 = (bf16[8,16,1536]{2,1,0:T(8,128)(2,1)S(1)}, bf16[8,16,1536]{2,1,0:T(8,128)(2,1)S(1)}, u32[]{:S(2)}, u32[]{:S(2)}) collective-permute-start(bf16[8,16,1536]{2,1,0:T(8,128)(2,1)S(1)} %dynamic-slice_bitcast_fusion), channel_id=1, source_target_pairs={{0,272},{272,0},{1,273},{273,1},{2,274},{274,2},{3,275},{275,3},{4... | collective-permute-start | bytes 1179656 | tf_op jit(solution)/shard_map/ppermute | solution.py:315
  48.5 1.1 %fusion = (bf16[3,6,4,512]{3,2,1,0:T(4,128)(2,1)S(1)}, bf16[3,6,4,512]{3,2,1,0:T(4,128)(2,1)S(1)}, bf16[3,6,4,512]{3,2,1,0:T(4,128)(2,1)S(1)}, bf16[3,6,4,512]{3,2,1,0:T(4,128)(2,1)S(1)}) fusion(bf16[6,12,4,512]{3,2,1,0:T(4,128)(2,1)} %bitcast.16), kind=kLoop, calls=%fused_computation.2 | loop fusion | bytes 589824 | tf_op jit(solution)/shard_map/slice | solution.py:107
  49.6 1.9 %collective-permute-start.2 = (bf16[3,6,4,512]{3,2,1,0:T(4,128)(2,1)S(1)}, bf16[3,6,4,512]{3,2,1,0:T(4,128)(2,1)S(1)}, u32[]{:S(2)}, u32[]{:S(2)}) collective-permute-start(bf16[3,6,4,512]{3,2,1,0:T(4,128)(2,1)S(1)} %get-tuple-element.26), channel_id=1, source_target_pairs={{0,1},{1,2},{2,3},{3,4},{4,5},{5,6},{6,7},{7,8},{8,9},{9,10},{10,1... | collective-permute-start | bytes 221192 | tf_op jit(solution)/shard_map/ppermute | solution.py:310
  51.5 3.1 %collective-permute-start.1 = (bf16[3,6,4,512]{3,2,1,0:T(4,128)(2,1)S(1)}, bf16[3,6,4,512]{3,2,1,0:T(4,128)(2,1)S(1)}, u32[]{:S(2)}, u32[]{:S(2)}) collective-permute-start(bf16[3,6,4,512]{3,2,1,0:T(4,128)(2,1)S(1)} %get-tuple-element.27), channel_id=1, source_target_pairs={{0,32},{1,33},{2,34},{3,35},{4,36},{5,37},{6,38},{7,39},{8,40},{9,... | collective-permute-start | bytes 221192 | tf_op jit(solution)/shard_map/ppermute | solution.py:309
  54.6 1.9 %collective-permute-start = (bf16[3,6,4,512]{3,2,1,0:T(4,128)(2,1)S(1)}, bf16[3,6,4,512]{3,2,1,0:T(4,128)(2,1)S(1)}, u32[]{:S(2)}, u32[]{:S(2)}) collective-permute-start(bf16[3,6,4,512]{3,2,1,0:T(4,128)(2,1)S(1)} %get-tuple-element.28), channel_id=1, source_target_pairs={{0,33},{1,34},{2,35},{3,36},{4,37},{5,38},{6,39},{7,40},{8,41},{9,... | collective-permute-start | bytes 221192 | tf_op jit(solution)/shard_map/ppermute | solution.py:308
  56.6 0.1 pad_add_fusion.spot_ref
  56.6 1.2 %collective-permute-done.3 = bf16[8,16,1536]{2,1,0:T(8,128)(2,1)S(1)} collective-permute-done((bf16[8,16,1536]{2,1,0:T(8,128)(2,1)S(1)}, bf16[8,16,1536]{2,1,0:T(8,128)(2,1)S(1)}, u32[]{:S(2)}, u32[]{:S(2)}) %collective-permute-start.3) | collective-permute-done | bytes 393248 | tf_op jit(solution)/shard_map/ppermute | solution.py:315
  57.9 2.8 %all-gather.2 = bf16[16,16,1536]{2,1,0:T(8,128)(2,1)S(1)} all-gather(bf16[8,16,1536]{2,1,0:T(8,128)(2,1)S(1)} %collective-permute-done.3), channel_id=4, replica_groups=mesh['xl'=2,'y'=8,'xh'=2,'z'=8,'c'=2] {'c'}, dimensions={0}, use_global_device_ids=true | all-gather | bytes 1179648 | tf_op jit(solution)/shard_map/all_gather | solution.py:315
  60.7 0.0 collective-permute-done.2.r2
  60.7 0.0 collective-permute-done.1.r1
  60.7 1.7 %collective-permute-done.r0 = bf16[3,6,4,512]{3,2,1,0:T(4,128)(2,1)S(1)} collective-permute-done((bf16[3,6,4,512]{3,2,1,0:T(4,128)(2,1)S(1)}, bf16[3,6,4,512]{3,2,1,0:T(4,128)(2,1)S(1)}, u32[]{:S(2)}, u32[]{:S(2)}) %collective-permute-start) | collective-permute-done | bytes 73760 | tf_op jit(solution)/shard_map/ppermute | solution.py:308
  62.4 0.0 copy-done.1
  62.4 5.9 %attention.1 = (bf16[3,6,4,512]{3,2,1,0:T(4,128)(2,1)S(1)}, bf16[3,6,4,512]{3,2,1,0:T(4,128)(2,1)S(1)}, bf16[3,6,4,512]{3,2,1,0:T(4,128)(2,1)S(1)}, bf16[3,6,4,512]{3,2,1,0:T(4,128)(2,1)S(1)}) custom-call(s32[2]{0:T(128)S(1)} %pad_add_fusion.spot_ref, bf16[3,6,4,512]{3,2,1,0:T(4,128)(2,1)S(1)} %collective-permute-done.r0, ...), custom_call_target="tpu_custom_call" | custom-call | tf_op jit(solution)/shard_map/attention/pallas_call | solution.py:257
  68.3 0.0 copy-start
  68.3 0.0 copy-start.3
  68.4 0.0 copy-start.4
  68.4 6.2 %collective-permute-start.4 = (bf16[3,6,4,512]{3,2,1,0:T(4,128)(2,1)S(1)}, bf16[3,6,4,512]{3,2,1,0:T(4,128)(2,1)S(1)}, u32[]{:S(2)}, u32[]{:S(2)}) collective-permute-start(bf16[3,6,4,512]{3,2,1,0:T(4,128)(2,1)S(1)} %get-tuple-element.19), channel_id=1, source_target_pairs={{0,31},{1,0},{2,1},{3,2},{4,3},{5,4},{6,5},{7,6},{8,7},{9,8},{10,9... | collective-permute-start | bytes 221192 | tf_op jit(solution)/shard_map/ppermute | solution.py:321
  74.6 4.1 %collective-permute-start.5 = (bf16[3,6,4,512]{3,2,1,0:T(4,128)(2,1)S(1)}, bf16[3,6,4,512]{3,2,1,0:T(4,128)(2,1)S(1)}, u32[]{:S(2)}, u32[]{:S(2)}) collective-permute-start(bf16[3,6,4,512]{3,2,1,0:T(4,128)(2,1)S(1)} %get-tuple-element.20), channel_id=1, source_target_pairs={{0,480},{1,481},{2,482},{3,483},{4,484},{5,485},{6,486},{7,487},{8... | collective-permute-start | bytes 221192 | tf_op jit(solution)/shard_map/ppermute | solution.py:322
  78.7 2.1 %collective-permute-start.6 = (bf16[3,6,4,512]{3,2,1,0:T(4,128)(2,1)S(1)}, bf16[3,6,4,512]{3,2,1,0:T(4,128)(2,1)S(1)}, u32[]{:S(2)}, u32[]{:S(2)}) collective-permute-start(bf16[3,6,4,512]{3,2,1,0:T(4,128)(2,1)S(1)} %get-tuple-element.21), channel_id=1, source_target_pairs={{0,511},{1,480},{2,481},{3,482},{4,483},{5,484},{6,485},{7,486},{8... | collective-permute-start | bytes 221192 | tf_op jit(solution)/shard_map/ppermute | solution.py:323
  80.8 0.0 all-gather.6.cloned.1.call-done
  80.8 2.4 %stage.1 = (bf16[16,2,16,512]{3,2,1,0:T(8,128)(2,1)S(1)}, bf16[16,2,64,512]{3,2,1,0:T(8,128)(2,1)S(1)}, bf16[16,2,64,512]{3,2,1,0:T(8,128)(2,1)S(1)}) custom-call(bf16[16,2,144,512]{3,2,1,0:T(8,128)(2,1)} %bitcast.20), custom_call_target="tpu_custom_call" | custom-call | bytes 9437184 | tf_op jit(solution)/shard_map/stage/pallas_call | solution.py:270
  83.2 0.0 collective-permute-done.4.m1
  83.2 0.0 collective-permute-done.5.m2
  83.3 2.0 %collective-permute-done.6.m3 = bf16[3,6,4,512]{3,2,1,0:T(4,128)(2,1)S(1)} collective-permute-done((bf16[3,6,4,512]{3,2,1,0:T(4,128)(2,1)S(1)}, bf16[3,6,4,512]{3,2,1,0:T(4,128)(2,1)S(1)}, u32[]{:S(2)}, u32[]{:S(2)}) %collective-permute-start.6) | collective-permute-done | bytes 73760 | tf_op jit(solution)/shard_map/ppermute | solution.py:323
  85.3 0.0 copy-done
  85.3 0.0 copy-done.4
  85.3 3.2 %tokens.1 = bf16[6,12,4,512]{3,2,1,0:T(4,128)(2,1)} custom-call(bf16[3,6,4,512]{3,2,1,0:T(4,128)(2,1)S(1)} %get-tuple-element.18.m0, bf16[3,6,4,512]{3,2,1,0:T(4,128)(2,1)S(1)} %collective-permute-done.4.m1, bf16[3,6,4,512]{3,2,1,0:T(4,128)(2,1)S(1)} %collective-permute-done.5.m2, bf16[3,6,4,512]{3,2,1,0:T(4,128)(2,1)S(1)} %collective-permute-done.6.m3, ...), custom_call_target="tpu_custom_call" | custom-call | tf_op jit(solution)/shard_map/tokens/pallas_call | solution.py:284
  (5 shorter events, 0.0 us)
Async XLA Ops:
  6.5 55.9 %copy-start.2 = (bf16[2,288,128]{2,1,0:T(8,128)(2,1)S(1)}, bf16[2,288,128]{2,1,0:T(8,128)(2,1)}, u32[]{:S(2)}) copy-start(bf16[2,288,128]{2,1,0:T(8,128)(2,1)} %constant.32.clone.tags_ref) | copy-start | bytes 442372
  6.5 55.9 %copy-start.1 = (bf16[288,288]{1,0:T(8,128)(2,1)S(1)}, bf16[288,288]{1,0:T(8,128)(2,1)}, u32[]{:S(2)}) copy-start(bf16[288,288]{1,0:T(8,128)(2,1)} %constant.31.clone.hot_ref) | copy-start | bytes 497668
  6.5 74.3 %all-gather.6.cloned.1.call-start = ((), (), s32[]{:S(2)}) async-start(), calls=%async_computation | async-start | bytes 5013504 | tf_op jit(solution)/shard_map/all_gather | solution.py:302
  43.3 14.6 %collective-permute-start.3 = (bf16[8,16,1536]{2,1,0:T(8,128)(2,1)S(1)}, bf16[8,16,1536]{2,1,0:T(8,128)(2,1)S(1)}, u32[]{:S(2)}, u32[]{:S(2)}) collective-permute-start(bf16[8,16,1536]{2,1,0:T(8,128)(2,1)S(1)} %dynamic-slice_bitcast_fusion), channel_id=1, source_target_pairs={{0,272},{272,0},{1,273},{273,1},{2,274},{274,2},{3,275},{275,3},{4... | collective-permute-start | bytes 1179656 | tf_op jit(solution)/shard_map/ppermute | solution.py:315
  49.6 11.1 %collective-permute-start.2 = (bf16[3,6,4,512]{3,2,1,0:T(4,128)(2,1)S(1)}, bf16[3,6,4,512]{3,2,1,0:T(4,128)(2,1)S(1)}, u32[]{:S(2)}, u32[]{:S(2)}) collective-permute-start(bf16[3,6,4,512]{3,2,1,0:T(4,128)(2,1)S(1)} %get-tuple-element.26), channel_id=1, source_target_pairs={{0,1},{1,2},{2,3},{3,4},{4,5},{5,6},{6,7},{7,8},{8,9},{9,10},{10,1... | collective-permute-start | bytes 221192 | tf_op jit(solution)/shard_map/ppermute | solution.py:310
  51.5 9.2 %collective-permute-start.1 = (bf16[3,6,4,512]{3,2,1,0:T(4,128)(2,1)S(1)}, bf16[3,6,4,512]{3,2,1,0:T(4,128)(2,1)S(1)}, u32[]{:S(2)}, u32[]{:S(2)}) collective-permute-start(bf16[3,6,4,512]{3,2,1,0:T(4,128)(2,1)S(1)} %get-tuple-element.27), channel_id=1, source_target_pairs={{0,32},{1,33},{2,34},{3,35},{4,36},{5,37},{6,38},{7,39},{8,40},{9,... | collective-permute-start | bytes 221192 | tf_op jit(solution)/shard_map/ppermute | solution.py:309
  54.6 7.8 %collective-permute-start = (bf16[3,6,4,512]{3,2,1,0:T(4,128)(2,1)S(1)}, bf16[3,6,4,512]{3,2,1,0:T(4,128)(2,1)S(1)}, u32[]{:S(2)}, u32[]{:S(2)}) collective-permute-start(bf16[3,6,4,512]{3,2,1,0:T(4,128)(2,1)S(1)} %get-tuple-element.28), channel_id=1, source_target_pairs={{0,33},{1,34},{2,35},{3,36},{4,37},{5,38},{6,39},{7,40},{8,41},{9,... | collective-permute-start | bytes 221192 | tf_op jit(solution)/shard_map/ppermute | solution.py:308
  68.3 16.9 %copy-start = (bf16[4,6,12,512]{3,0,2,1:T(4,128)(2,1)S(1)}, bf16[4,6,12,512]{3,0,2,1:T(4,128)(2,1)}, u32[]{:S(2)}) copy-start(bf16[4,6,12,512]{3,0,2,1:T(4,128)(2,1)} %param.10) | copy-start | bytes 884740
  68.3 16.9 %copy-start.3 = (f32[512]{0:T(512)S(1)}, f32[512]{0:T(512)}, u32[]{:S(2)}) copy-start(f32[512]{0:T(512)} %param.14) | copy-start | bytes 6148
  68.4 16.9 %copy-start.4 = (f32[512]{0:T(512)S(1)}, f32[512]{0:T(512)}, u32[]{:S(2)}) copy-start(f32[512]{0:T(512)} %param.17) | copy-start | bytes 6148
  68.4 14.9 %collective-permute-start.4 = (bf16[3,6,4,512]{3,2,1,0:T(4,128)(2,1)S(1)}, bf16[3,6,4,512]{3,2,1,0:T(4,128)(2,1)S(1)}, u32[]{:S(2)}, u32[]{:S(2)}) collective-permute-start(bf16[3,6,4,512]{3,2,1,0:T(4,128)(2,1)S(1)} %get-tuple-element.19), channel_id=1, source_target_pairs={{0,31},{1,0},{2,1},{3,2},{4,3},{5,4},{6,5},{7,6},{8,7},{9,8},{10,9... | collective-permute-start | bytes 221192 | tf_op jit(solution)/shard_map/ppermute | solution.py:321
  74.6 8.7 %collective-permute-start.5 = (bf16[3,6,4,512]{3,2,1,0:T(4,128)(2,1)S(1)}, bf16[3,6,4,512]{3,2,1,0:T(4,128)(2,1)S(1)}, u32[]{:S(2)}, u32[]{:S(2)}) collective-permute-start(bf16[3,6,4,512]{3,2,1,0:T(4,128)(2,1)S(1)} %get-tuple-element.20), channel_id=1, source_target_pairs={{0,480},{1,481},{2,482},{3,483},{4,484},{5,485},{6,486},{7,487},{8... | collective-permute-start | bytes 221192 | tf_op jit(solution)/shard_map/ppermute | solution.py:322
  78.7 6.6 %collective-permute-start.6 = (bf16[3,6,4,512]{3,2,1,0:T(4,128)(2,1)S(1)}, bf16[3,6,4,512]{3,2,1,0:T(4,128)(2,1)S(1)}, u32[]{:S(2)}, u32[]{:S(2)}) collective-permute-start(bf16[3,6,4,512]{3,2,1,0:T(4,128)(2,1)S(1)} %get-tuple-element.21), channel_id=1, source_target_pairs={{0,511},{1,480},{2,481},{3,482},{4,483},{5,484},{6,485},{7,486},{8... | collective-permute-start | bytes 221192 | tf_op jit(solution)/shard_map/ppermute | solution.py:323
Sparse Core Ops, SparseCore 0:
  14.2 53.2 all-gather.5

commit v7 on v6

--- a/solution.py
+++ b/solution.py
@@ -27,7 +27,7 @@
 EPSILON = 1e-05
 F32 = jnp.float32
 BF16 = jnp.bfloat16
-VMEM_LIMIT = 48 * 1024 * 1024
+VMEM_LIMIT = 8 * 1024 * 1024
 ATTENTION_LIMIT = 32 * 1024 * 1024
 STAGE_LIMIT = 48 * 1024 * 1024
 TOKENS_LIMIT = 40 * 1024 * 1024
@@ -122,20 +122,13 @@
     copy_all([(part, own_ref.at[start:stop]) for part, start, stop in parts], sems)
 
 
+def bias_kernel(bias_hbm, bias_ref, sems):
+    copy_all([(bias_hbm, bias_ref)], sems)
+
+
 def attention_kernel(
-    spot_ref, r0, r1, r2, r3, mine_ref, other_ref, hot_ref, tags_ref, bias_hbm,
-    o0, o1, o2, o3, bias_ref, sems,
+    spot_ref, r0, r1, r2, r3, mine_ref, other_ref, hot_ref, tags_ref, bias_ref, o0, o1, o2, o3
 ):
-    fetches = [
-        pltpu.make_async_copy(
-            bias_hbm.at[g * PER_GROUP : (g + 1) * PER_GROUP],
-            bias_ref.at[g * PER_GROUP : (g + 1) * PER_GROUP],
-            sems.at[g],
-        )
-        for g in range(GROUPS)
-    ]
-    for fetch in fetches:
-        fetch.start()
     hot = hot_ref[...]
     rows = stacked([r[...] for r in (r0, r1, r2, r3)]).astype(BF16)
     rows = lax.dot_general(hot, rows, (((0,), (0,)), ((), ())), preferred_element_type=F32)
@@ -169,7 +162,6 @@
             sums = jnp.broadcast_to(jnp.where(mine, 1.0, 0.0).astype(BF16), (WN, LANES))
             value_rows += [jnp.concatenate([jnp.where(mine, group_v, zero), sums], 1), gap]
         scores = dot_t(group_q, jnp.concatenate(key_rows, 0))
-        fetches[group].wait()
         weights = []
         for j in range(PER_GROUP):
             bias = bias_ref[group * PER_GROUP + j].astype(F32)
@@ -252,17 +244,29 @@
     )(*off_chip(up_weight, down_weight, proj_weight))
 
 
+def held_bias(bias):
+    return pl.pallas_call(
+        bias_kernel,
+        in_specs=[fetched()],
+        out_specs=held(),
+        out_shape=jax.ShapeDtypeStruct(bias.shape, BF16),
+        scratch_shapes=[pltpu.SemaphoreType.DMA((1,))],
+        compiler_params=params(),
+        cost_estimate=pl.CostEstimate(flops=0, bytes_accessed=2 * bias.size * 2, transcendentals=0),
+        name="bias",
+    )(*off_chip(bias))
+
+
 def attention(spot, quarters, mine, other, bias):
     constants = (jnp.asarray(to_quarters(), BF16), jnp.asarray(tags(), BF16))
     return pl.pallas_call(
         attention_kernel,
-        in_specs=[scalars()] + [held()] * (len(quarters) + 4) + [fetched()],
+        in_specs=[scalars()] + [held()] * (len(quarters) + 5),
         out_specs=[held()] * 4,
         out_shape=[jax.ShapeDtypeStruct(CORNER, BF16)] * 4,
-        scratch_shapes=[pltpu.VMEM(bias.shape, BF16), pltpu.SemaphoreType.DMA((GROUPS,))],
         compiler_params=pltpu.CompilerParams(vmem_limit_bytes=ATTENTION_LIMIT),
         name="attention",
-    )(spot, *quarters, mine, other, *constants, *off_chip(bias))
+    )(spot, *quarters, mine, other, *constants, bias)
 
 
 def staged(gathered):
@@ -303,7 +307,7 @@
     qkv_weight, _ = lax.optimization_barrier((qkv_weight, both))
     mine = lax.all_gather(qkv_weight, ("z", "c"), axis=0, tiled=False)
     cells = latent.transpose(1, 2, 0, 3)
-    cells_after, mine = lax.optimization_barrier((cells, mine))
+    cells_after, bias, mine = lax.optimization_barrier((cells, position_bias, mine))
     rolled = [
         lax.ppermute(corner(cells_after, 1, 1), AXES, shifted(1, 1)),
         lax.ppermute(corner(cells_after, 1, 0), AXES, shifted(1, 0)),
@@ -315,7 +319,7 @@
     theirs = lax.all_gather(lax.ppermute(sent, AXES, mirrored()), "c", axis=0, tiled=False)
 
     spot = jnp.stack([lax.axis_index("xh"), (lax.axis_index(LAT) == 0).astype(jnp.int32)])
-    attended = attention(spot, rolled, mine, theirs, position_bias)
+    attended = attention(spot, rolled, mine, theirs, held_bias(bias))
     restored = [
         attended[3],
         lax.ppermute(attended[2], AXES, shifted(0, -1)),

time: 95.7 us -> 94.4 us (0.986)
  waiting for transfers between devices: 5 us -> 0.17 us
  starting transfers between devices: 24.5 us -> 26.7 us
    pallas_call x0 -> x1, Pallas kernels: none -> 2.11 us  [held_bias(): pl.pallas_call(bias_kernel, in_specs=[fetched()], out_specs=held(), out_s...]
    ppermute x1, starting transfers between devices: 2.07 us -> 3.96 us  [shards(): lax.ppermute(attended[0], AXES, shifted(-1, -1))]
    ppermute x1, waiting for transfers between devices: 2.01 us -> 0.12 us  [shards(): lax.ppermute(attended[0], AXES, shifted(-1, -1))]
    ppermute x1, waiting for transfers between devices: 1.7 us -> 0.01 us  [shards(): lax.ppermute(corner(cells_after, 1, 1), AXES, shifted(1, 1))]
    pallas_call x1, Pallas kernels: 5.9 us -> 4.21 us  [attention(): pl.pallas_call(attention_kernel, in_specs=[scalars()] + [held()] * (len(q...]
    ppermute x1, waiting for transfers between devices: 1.24 us -> 0.01 us  [shards(): lax.ppermute(sent, AXES, mirrored())]
  transfers between devices with their start and end apart: 8 -> 8, of which waited for: 3 -> 1; matrix products, arithmetic and copies ran while one was open for 1% -> 1% of each run, Pallas kernels for 9% -> 9%
where the time goes in v7:
time: 94.4 us; the launch traced here: 94 us
  blocking collectives  39.5 us (42%)
  starting transfers between devices  26.7 us (28%)
  between operations  13.6 us (14%)
  Pallas kernels  12.8 us (14%)
  local copies, waits for them, and re-layouts  1.17 us (1%)
    all_gather x1, blocking collectives, shards(): mine = lax.all_gather(qkv_weight, ('z', 'c'), axis=0, tiled=False)  29.1 us
    all_gather x1, blocking collectives, shards(): lax.all_gather(own, AXES, axis=0, tiled=False, axis_index_groups=mirrored...  6.6 us
    ppermute x1, starting transfers between devices, shards(): lax.ppermute(attended[2], AXES, shifted(0, -1))  6.14 us
    ppermute x1, starting transfers between devices, shards(): lax.ppermute(sent, AXES, mirrored())  5.15 us
    ppermute x1, starting transfers between devices, shards(): lax.ppermute(attended[1], AXES, shifted(-1, 0))  4.49 us
    pallas_call x1, Pallas kernels, attention(): pl.pallas_call(attention_kernel, in_specs=[scalars()] + [held()] * (len(q...  4.21 us
    ppermute x1, starting transfers between devices, shards(): lax.ppermute(attended[0], AXES, shifted(-1, -1))  3.96 us
    all_gather x1, blocking collectives, shards(): lax.all_gather(lax.ppermute(sent, AXES, mirrored()), 'c', axis=0, tiled=F...  3.74 us
  transfers between devices with their start and end apart: 8, of which 1 were waited for; matrix products, arithmetic and copies ran while one was open for 1% of the time, Pallas kernels for 9%

profile of v7, /device:TPU:1, one launch (start us, length us, event | category | flops | bytes accessed | tf_op | source)
XLA Modules:
  0.0 94.0 jit_solution(410875578856493228)
XLA Ops:
  6.5 0.9 pack.1
  7.4 6.6 %all-gather = bf16[288,512]{1,0:T(8,128)(2,1)} all-gather(bf16[144,512]{1,0:T(8,128)(2,1)S(1)} %pack.1), channel_id=2, replica_groups={{0,272},{1,273},{2,274},{3,275},{4,276},{5,277},{6,278},{7,279},{8,280}..., dimensions={0}, use_global_device_ids=true | all-gather | bytes 442368 | tf_op jit(solution)/shard_map/all_gather | solution.py:305
  14.0 0.0 all-gather.6.cloned.1.call-update
  14.1 29.1 %all-gather.1 = bf16[256,1536]{1,0:T(8,128)(2,1)S(1)} all-gather(bf16[16,1536]{1,0:T(8,128)(2,1)} %param.11), channel_id=3, replica_groups=mesh['xl'=2,'y'=8,'xh'=2,'z'=8,'c'=2] {'z','c'}, dimensions={0}, use_global_device_ids=true | all-gather | bytes 835584 | tf_op jit(solution)/shard_map/all_gather | solution.py:308
  43.2 5.2 %collective-permute-start.3 = (bf16[8,16,1536]{2,1,0:T(8,128)(2,1)S(1)}, bf16[8,16,1536]{2,1,0:T(8,128)(2,1)S(1)}, u32[]{:S(2)}, u32[]{:S(2)}) collective-permute-start(bf16[8,16,1536]{2,1,0:T(8,128)(2,1)S(1)} %dynamic-slice_bitcast_fusion), channel_id=1, source_target_pairs={{0,272},{272,0},{1,273},{273,1},{2,274},{274,2},{3,275},{275,3},{4... | collective-permute-start | bytes 1179656 | tf_op jit(solution)/shard_map/ppermute | solution.py:319
  48.4 1.1 %fusion = (bf16[3,6,4,512]{3,2,1,0:T(4,128)(2,1)S(1)}, bf16[3,6,4,512]{3,2,1,0:T(4,128)(2,1)S(1)}, bf16[3,6,4,512]{3,2,1,0:T(4,128)(2,1)S(1)}, bf16[3,6,4,512]{3,2,1,0:T(4,128)(2,1)S(1)}) fusion(bf16[6,12,4,512]{3,2,1,0:T(4,128)(2,1)} %bitcast.16), kind=kLoop, calls=%fused_computation.2 | loop fusion | bytes 589824 | tf_op jit(solution)/shard_map/slice | solution.py:107
  49.5 1.9 %collective-permute-start = (bf16[3,6,4,512]{3,2,1,0:T(4,128)(2,1)S(1)}, bf16[3,6,4,512]{3,2,1,0:T(4,128)(2,1)S(1)}, u32[]{:S(2)}, u32[]{:S(2)}) collective-permute-start(bf16[3,6,4,512]{3,2,1,0:T(4,128)(2,1)S(1)} %get-tuple-element.30), channel_id=1, source_target_pairs={{0,33},{1,34},{2,35},{3,36},{4,37},{5,38},{6,39},{7,40},{8,41},{9,... | collective-permute-start | bytes 221192 | tf_op jit(solution)/shard_map/ppermute | solution.py:312
  51.5 3.1 %collective-permute-start.1 = (bf16[3,6,4,512]{3,2,1,0:T(4,128)(2,1)S(1)}, bf16[3,6,4,512]{3,2,1,0:T(4,128)(2,1)S(1)}, u32[]{:S(2)}, u32[]{:S(2)}) collective-permute-start(bf16[3,6,4,512]{3,2,1,0:T(4,128)(2,1)S(1)} %get-tuple-element.29), channel_id=1, source_target_pairs={{0,32},{1,33},{2,34},{3,35},{4,36},{5,37},{6,38},{7,39},{8,40},{9,... | collective-permute-start | bytes 221192 | tf_op jit(solution)/shard_map/ppermute | solution.py:313
  54.6 1.9 %collective-permute-start.2 = (bf16[3,6,4,512]{3,2,1,0:T(4,128)(2,1)S(1)}, bf16[3,6,4,512]{3,2,1,0:T(4,128)(2,1)S(1)}, u32[]{:S(2)}, u32[]{:S(2)}) collective-permute-start(bf16[3,6,4,512]{3,2,1,0:T(4,128)(2,1)S(1)} %get-tuple-element.28), channel_id=1, source_target_pairs={{0,1},{1,2},{2,3},{3,4},{4,5},{5,6},{6,7},{7,8},{8,9},{9,10},{10,1... | collective-permute-start | bytes 221192 | tf_op jit(solution)/shard_map/ppermute | solution.py:314
  56.5 0.0 copy-start.1
  56.5 0.0 copy-start.2
  56.5 2.1 %bias.1.bias_ref = bf16[16,288,288]{2,1,0:T(8,128)(2,1)S(1)} custom-call(bf16[16,288,288]{2,1,0:T(8,128)(2,1)} %bias_hbm), custom_call_target="tpu_custom_call" | custom-call | bytes 5308416 | tf_op jit(solution)/shard_map/bias/pallas_call | solution.py:248
  58.7 0.1 pad_add_fusion.spot_ref
  58.7 0.0 collective-permute-done.3
  58.7 3.7 %all-gather.2 = bf16[16,16,1536]{2,1,0:T(8,128)(2,1)S(1)} all-gather(bf16[8,16,1536]{2,1,0:T(8,128)(2,1)S(1)} %collective-permute-done.3), channel_id=4, replica_groups=mesh['xl'=2,'y'=8,'xh'=2,'z'=8,'c'=2] {'c'}, dimensions={0}, use_global_device_ids=true | all-gather | bytes 1179648 | tf_op jit(solution)/shard_map/all_gather | solution.py:319
  62.5 0.0 collective-permute-done.r0
  62.5 0.0 collective-permute-done.1.r1
  62.5 0.0 collective-permute-done.2.r2
  62.5 0.0 copy-done.1
  62.5 4.2 %attention.1 = (bf16[3,6,4,512]{3,2,1,0:T(4,128)(2,1)S(1)}, bf16[3,6,4,512]{3,2,1,0:T(4,128)(2,1)S(1)}, bf16[3,6,4,512]{3,2,1,0:T(4,128)(2,1)S(1)}, bf16[3,6,4,512]{3,2,1,0:T(4,128)(2,1)S(1)}) custom-call(s32[2]{0:T(128)S(1)} %pad_add_fusion.spot_ref, bf16[3,6,4,512]{3,2,1,0:T(4,128)(2,1)S(1)} %collective-permute-done.r0, ...), custom_call_target="tpu_custom_call" | custom-call | tf_op jit(solution)/shard_map/attention/pallas_call | solution.py:262
  66.7 0.0 copy-start
  66.7 0.0 copy-start.3
  66.8 0.0 copy-start.4
  66.8 6.1 %collective-permute-start.4 = (bf16[3,6,4,512]{3,2,1,0:T(4,128)(2,1)S(1)}, bf16[3,6,4,512]{3,2,1,0:T(4,128)(2,1)S(1)}, u32[]{:S(2)}, u32[]{:S(2)}) collective-permute-start(bf16[3,6,4,512]{3,2,1,0:T(4,128)(2,1)S(1)} %get-tuple-element.21), channel_id=1, source_target_pairs={{0,31},{1,0},{2,1},{3,2},{4,3},{5,4},{6,5},{7,6},{8,7},{9,8},{10,9... | collective-permute-start | bytes 221192 | tf_op jit(solution)/shard_map/ppermute | solution.py:325
  72.9 4.5 %collective-permute-start.5 = (bf16[3,6,4,512]{3,2,1,0:T(4,128)(2,1)S(1)}, bf16[3,6,4,512]{3,2,1,0:T(4,128)(2,1)S(1)}, u32[]{:S(2)}, u32[]{:S(2)}) collective-permute-start(bf16[3,6,4,512]{3,2,1,0:T(4,128)(2,1)S(1)} %get-tuple-element.22), channel_id=1, source_target_pairs={{0,480},{1,481},{2,482},{3,483},{4,484},{5,485},{6,486},{7,487},{8... | collective-permute-start | bytes 221192 | tf_op jit(solution)/shard_map/ppermute | solution.py:326
  77.4 4.0 %collective-permute-start.6 = (bf16[3,6,4,512]{3,2,1,0:T(4,128)(2,1)S(1)}, bf16[3,6,4,512]{3,2,1,0:T(4,128)(2,1)S(1)}, u32[]{:S(2)}, u32[]{:S(2)}) collective-permute-start(bf16[3,6,4,512]{3,2,1,0:T(4,128)(2,1)S(1)} %get-tuple-element.23), channel_id=1, source_target_pairs={{0,511},{1,480},{2,481},{3,482},{4,483},{5,484},{6,485},{7,486},{8... | collective-permute-start | bytes 221192 | tf_op jit(solution)/shard_map/ppermute | solution.py:327
  81.4 0.0 all-gather.6.cloned.1.call-done
  81.4 2.4 %stage.1 = (bf16[16,2,16,512]{3,2,1,0:T(8,128)(2,1)S(1)}, bf16[16,2,64,512]{3,2,1,0:T(8,128)(2,1)S(1)}, bf16[16,2,64,512]{3,2,1,0:T(8,128)(2,1)S(1)}) custom-call(bf16[16,2,144,512]{3,2,1,0:T(8,128)(2,1)} %bitcast.20), custom_call_target="tpu_custom_call" | custom-call | bytes 9437184 | tf_op jit(solution)/shard_map/stage/pallas_call | solution.py:274
  83.8 0.0 collective-permute-done.4.m1
  83.9 0.0 collective-permute-done.5.m2
  83.9 0.1 collective-permute-done.6.m3
  84.0 3.2 %tokens.1 = bf16[6,12,4,512]{3,2,1,0:T(4,128)(2,1)} custom-call(bf16[3,6,4,512]{3,2,1,0:T(4,128)(2,1)S(1)} %get-tuple-element.20.m0, bf16[3,6,4,512]{3,2,1,0:T(4,128)(2,1)S(1)} %collective-permute-done.4.m1, bf16[3,6,4,512]{3,2,1,0:T(4,128)(2,1)S(1)} %collective-permute-done.5.m2, bf16[3,6,4,512]{3,2,1,0:T(4,128)(2,1)S(1)} %collective-permute-done.6.m3, ...), custom_call_target="tpu_custom_call" | custom-call | tf_op jit(solution)/shard_map/tokens/pallas_call | solution.py:288
  (6 shorter events, 0.0 us)
Async XLA Ops:
  6.5 74.9 %all-gather.6.cloned.1.call-start = ((), (), s32[]{:S(2)}) async-start(), calls=%async_computation | async-start | bytes 5013504 | tf_op jit(solution)/shard_map/all_gather | solution.py:306
  43.2 15.5 %collective-permute-start.3 = (bf16[8,16,1536]{2,1,0:T(8,128)(2,1)S(1)}, bf16[8,16,1536]{2,1,0:T(8,128)(2,1)S(1)}, u32[]{:S(2)}, u32[]{:S(2)}) collective-permute-start(bf16[8,16,1536]{2,1,0:T(8,128)(2,1)S(1)} %dynamic-slice_bitcast_fusion), channel_id=1, source_target_pairs={{0,272},{272,0},{1,273},{273,1},{2,274},{274,2},{3,275},{275,3},{4... | collective-permute-start | bytes 1179656 | tf_op jit(solution)/shard_map/ppermute | solution.py:319
  49.5 13.0 %collective-permute-start = (bf16[3,6,4,512]{3,2,1,0:T(4,128)(2,1)S(1)}, bf16[3,6,4,512]{3,2,1,0:T(4,128)(2,1)S(1)}, u32[]{:S(2)}, u32[]{:S(2)}) collective-permute-start(bf16[3,6,4,512]{3,2,1,0:T(4,128)(2,1)S(1)} %get-tuple-element.30), channel_id=1, source_target_pairs={{0,33},{1,34},{2,35},{3,36},{4,37},{5,38},{6,39},{7,40},{8,41},{9,... | collective-permute-start | bytes 221192 | tf_op jit(solution)/shard_map/ppermute | solution.py:312
  51.5 11.0 %collective-permute-start.1 = (bf16[3,6,4,512]{3,2,1,0:T(4,128)(2,1)S(1)}, bf16[3,6,4,512]{3,2,1,0:T(4,128)(2,1)S(1)}, u32[]{:S(2)}, u32[]{:S(2)}) collective-permute-start(bf16[3,6,4,512]{3,2,1,0:T(4,128)(2,1)S(1)} %get-tuple-element.29), channel_id=1, source_target_pairs={{0,32},{1,33},{2,34},{3,35},{4,36},{5,37},{6,38},{7,39},{8,40},{9,... | collective-permute-start | bytes 221192 | tf_op jit(solution)/shard_map/ppermute | solution.py:313
  54.6 7.9 %collective-permute-start.2 = (bf16[3,6,4,512]{3,2,1,0:T(4,128)(2,1)S(1)}, bf16[3,6,4,512]{3,2,1,0:T(4,128)(2,1)S(1)}, u32[]{:S(2)}, u32[]{:S(2)}) collective-permute-start(bf16[3,6,4,512]{3,2,1,0:T(4,128)(2,1)S(1)} %get-tuple-element.28), channel_id=1, source_target_pairs={{0,1},{1,2},{2,3},{3,4},{4,5},{5,6},{6,7},{7,8},{8,9},{9,10},{10,1... | collective-permute-start | bytes 221192 | tf_op jit(solution)/shard_map/ppermute | solution.py:314
  56.5 6.0 %copy-start.1 = (bf16[288,288]{1,0:T(8,128)(2,1)S(1)}, bf16[288,288]{1,0:T(8,128)(2,1)}, u32[]{:S(2)}) copy-start(bf16[288,288]{1,0:T(8,128)(2,1)} %constant.31.clone.hot_ref) | copy-start | bytes 497668
  56.5 6.0 %copy-start.2 = (bf16[2,288,128]{2,1,0:T(8,128)(2,1)S(1)}, bf16[2,288,128]{2,1,0:T(8,128)(2,1)}, u32[]{:S(2)}) copy-start(bf16[2,288,128]{2,1,0:T(8,128)(2,1)} %constant.32.clone.tags_ref) | copy-start | bytes 442372
  66.7 17.3 %copy-start = (bf16[4,6,12,512]{3,0,2,1:T(4,128)(2,1)S(1)}, bf16[4,6,12,512]{3,0,2,1:T(4,128)(2,1)}, u32[]{:S(2)}) copy-start(bf16[4,6,12,512]{3,0,2,1:T(4,128)(2,1)} %param.10) | copy-start | bytes 884740
  66.7 17.3 %copy-start.3 = (f32[512]{0:T(512)S(1)}, f32[512]{0:T(512)}, u32[]{:S(2)}) copy-start(f32[512]{0:T(512)} %param.14) | copy-start | bytes 6148
  66.8 17.2 %copy-start.4 = (f32[512]{0:T(512)S(1)}, f32[512]{0:T(512)}, u32[]{:S(2)}) copy-start(f32[512]{0:T(512)} %param.17) | copy-start | bytes 6148
  66.8 17.1 %collective-permute-start.4 = (bf16[3,6,4,512]{3,2,1,0:T(4,128)(2,1)S(1)}, bf16[3,6,4,512]{3,2,1,0:T(4,128)(2,1)S(1)}, u32[]{:S(2)}, u32[]{:S(2)}) collective-permute-start(bf16[3,6,4,512]{3,2,1,0:T(4,128)(2,1)S(1)} %get-tuple-element.21), channel_id=1, source_target_pairs={{0,31},{1,0},{2,1},{3,2},{4,3},{5,4},{6,5},{7,6},{8,7},{9,8},{10,9... | collective-permute-start | bytes 221192 | tf_op jit(solution)/shard_map/ppermute | solution.py:325
  72.9 10.9 %collective-permute-start.5 = (bf16[3,6,4,512]{3,2,1,0:T(4,128)(2,1)S(1)}, bf16[3,6,4,512]{3,2,1,0:T(4,128)(2,1)S(1)}, u32[]{:S(2)}, u32[]{:S(2)}) collective-permute-start(bf16[3,6,4,512]{3,2,1,0:T(4,128)(2,1)S(1)} %get-tuple-element.22), channel_id=1, source_target_pairs={{0,480},{1,481},{2,482},{3,483},{4,484},{5,485},{6,486},{7,487},{8... | collective-permute-start | bytes 221192 | tf_op jit(solution)/shard_map/ppermute | solution.py:326
  77.4 6.6 %collective-permute-start.6 = (bf16[3,6,4,512]{3,2,1,0:T(4,128)(2,1)S(1)}, bf16[3,6,4,512]{3,2,1,0:T(4,128)(2,1)S(1)}, u32[]{:S(2)}, u32[]{:S(2)}) collective-permute-start(bf16[3,6,4,512]{3,2,1,0:T(4,128)(2,1)S(1)} %get-tuple-element.23), channel_id=1, source_target_pairs={{0,511},{1,480},{2,481},{3,482},{4,483},{5,484},{6,485},{7,486},{8... | collective-permute-start | bytes 221192 | tf_op jit(solution)/shard_map/ppermute | solution.py:327
Sparse Core Ops, SparseCore 0:
  14.2 53.4 all-gather.5

commit v8 on v7

--- a/solution.py
+++ b/solution.py
@@ -181,7 +181,7 @@
 
 
 def token_kernel(
-    m0, m1, m2, m3, cells_ref, wp, wu, wd, attn_gain_ref, mlp_gain_ref, out_ref
+    m3, m2, m1, m0, cells_ref, wp, wu, wd, attn_gain_ref, mlp_gain_ref, out_ref
 ):
     attended = stacked([m[...] for m in (m0, m1, m2, m3)]).astype(BF16)
     cells = stacked([corner(cells_ref, i, j) for i in range(2) for j in range(2)])
@@ -321,10 +321,10 @@
     spot = jnp.stack([lax.axis_index("xh"), (lax.axis_index(LAT) == 0).astype(jnp.int32)])
     attended = attention(spot, rolled, mine, theirs, held_bias(bias))
     restored = [
+        lax.ppermute(attended[0], AXES, shifted(-1, -1)),
+        lax.ppermute(attended[1], AXES, shifted(-1, 0)),
+        lax.ppermute(attended[2], AXES, shifted(0, -1)),
         attended[3],
-        lax.ppermute(attended[2], AXES, shifted(0, -1)),
-        lax.ppermute(attended[1], AXES, shifted(-1, 0)),
-        lax.ppermute(attended[0], AXES, shifted(-1, -1)),
     ]
     return tokens(restored, cells, staged(gathered), attn_gain, mlp_gain).transpose(2, 0, 1, 3)
 

time: 94.4 us -> 94.2 us (level)
    ppermute x1, starting transfers between devices: 3.96 us -> 8.61 us  [shards(): lax.ppermute(attended[0], AXES, shifted(-1, -1))]
    ppermute x1, starting transfers between devices: 6.14 us -> 3.57 us  [shards(): lax.ppermute(attended[2], AXES, shifted(0, -1))]
    ppermute x1, starting transfers between devices: 4.49 us -> 2.24 us  [shards(): lax.ppermute(attended[1], AXES, shifted(-1, 0))]
  transfers between devices with their start and end apart: 8 -> 8, of which waited for: 1 -> 0; matrix products, arithmetic and copies ran while one was open for 1% -> 1% of each run, Pallas kernels for 9% -> 9%
where the time goes in v8:
time: 94.2 us; the launch traced here: 93.7 us
  blocking collectives  39.5 us (42%)
  starting transfers between devices  26.5 us (28%)
  between operations  13.6 us (14%)
  Pallas kernels  12.8 us (14%)
  local copies, waits for them, and re-layouts  1.17 us (1%)
    all_gather x1, blocking collectives, shards(): mine = lax.all_gather(qkv_weight, ('z', 'c'), axis=0, tiled=False)  29.1 us
    ppermute x1, starting transfers between devices, shards(): lax.ppermute(attended[0], AXES, shifted(-1, -1))  8.61 us
    all_gather x1, blocking collectives, shards(): lax.all_gather(own, AXES, axis=0, tiled=False, axis_index_groups=mirrored...  6.6 us
    ppermute x1, starting transfers between devices, shards(): lax.ppermute(sent, AXES, mirrored())  5.15 us
    pallas_call x1, Pallas kernels, attention(): pl.pallas_call(attention_kernel, in_specs=[scalars()] + [held()] * (len(q...  4.21 us
    all_gather x1, blocking collectives, shards(): lax.all_gather(lax.ppermute(sent, AXES, mirrored()), 'c', axis=0, tiled=F...  3.74 us
    ppermute x1, starting transfers between devices, shards(): lax.ppermute(attended[2], AXES, shifted(0, -1))  3.57 us
    pallas_call x1, Pallas kernels, tokens(): pl.pallas_call(token_kernel, grid=(1,), in_specs=[whole(CORNER)] * 4 + [w...  3.17 us
  transfers between devices with their start and end apart: 8, of which 0 were waited for; matrix products, arithmetic and copies ran while one was open for 1% of the time, Pallas kernels for 9%

profile of v8, /device:TPU:1, one launch (start us, length us, event | category | flops | bytes accessed | tf_op | source)
XLA Modules:
  0.0 93.7 jit_solution(4974416578247830028)
XLA Ops:
  6.5 0.9 pack.1
  7.4 6.6 %all-gather = bf16[288,512]{1,0:T(8,128)(2,1)} all-gather(bf16[144,512]{1,0:T(8,128)(2,1)S(1)} %pack.1), channel_id=2, replica_groups={{0,272},{1,273},{2,274},{3,275},{4,276},{5,277},{6,278},{7,279},{8,280}..., dimensions={0}, use_global_device_ids=true | all-gather | bytes 442368 | tf_op jit(solution)/shard_map/all_gather | solution.py:305
  14.0 0.0 all-gather.6.cloned.1.call-update
  14.1 29.1 %all-gather.1 = bf16[256,1536]{1,0:T(8,128)(2,1)S(1)} all-gather(bf16[16,1536]{1,0:T(8,128)(2,1)} %param.11), channel_id=3, replica_groups=mesh['xl'=2,'y'=8,'xh'=2,'z'=8,'c'=2] {'z','c'}, dimensions={0}, use_global_device_ids=true | all-gather | bytes 835584 | tf_op jit(solution)/shard_map/all_gather | solution.py:308
  43.2 5.2 %collective-permute-start.3 = (bf16[8,16,1536]{2,1,0:T(8,128)(2,1)S(1)}, bf16[8,16,1536]{2,1,0:T(8,128)(2,1)S(1)}, u32[]{:S(2)}, u32[]{:S(2)}) collective-permute-start(bf16[8,16,1536]{2,1,0:T(8,128)(2,1)S(1)} %dynamic-slice_bitcast_fusion), channel_id=1, source_target_pairs={{0,272},{272,0},{1,273},{273,1},{2,274},{274,2},{3,275},{275,3},{4... | collective-permute-start | bytes 1179656 | tf_op jit(solution)/shard_map/ppermute | solution.py:319
  48.4 1.1 %fusion = (bf16[3,6,4,512]{3,2,1,0:T(4,128)(2,1)S(1)}, bf16[3,6,4,512]{3,2,1,0:T(4,128)(2,1)S(1)}, bf16[3,6,4,512]{3,2,1,0:T(4,128)(2,1)S(1)}, bf16[3,6,4,512]{3,2,1,0:T(4,128)(2,1)S(1)}) fusion(bf16[6,12,4,512]{3,2,1,0:T(4,128)(2,1)} %bitcast.16), kind=kLoop, calls=%fused_computation.2 | loop fusion | bytes 589824 | tf_op jit(solution)/shard_map/slice | solution.py:107
  49.5 1.9 %collective-permute-start = (bf16[3,6,4,512]{3,2,1,0:T(4,128)(2,1)S(1)}, bf16[3,6,4,512]{3,2,1,0:T(4,128)(2,1)S(1)}, u32[]{:S(2)}, u32[]{:S(2)}) collective-permute-start(bf16[3,6,4,512]{3,2,1,0:T(4,128)(2,1)S(1)} %get-tuple-element.30), channel_id=1, source_target_pairs={{0,33},{1,34},{2,35},{3,36},{4,37},{5,38},{6,39},{7,40},{8,41},{9,... | collective-permute-start | bytes 221192 | tf_op jit(solution)/shard_map/ppermute | solution.py:312
  51.5 3.1 %collective-permute-start.1 = (bf16[3,6,4,512]{3,2,1,0:T(4,128)(2,1)S(1)}, bf16[3,6,4,512]{3,2,1,0:T(4,128)(2,1)S(1)}, u32[]{:S(2)}, u32[]{:S(2)}) collective-permute-start(bf16[3,6,4,512]{3,2,1,0:T(4,128)(2,1)S(1)} %get-tuple-element.29), channel_id=1, source_target_pairs={{0,32},{1,33},{2,34},{3,35},{4,36},{5,37},{6,38},{7,39},{8,40},{9,... | collective-permute-start | bytes 221192 | tf_op jit(solution)/shard_map/ppermute | solution.py:313
  54.6 1.9 %collective-permute-start.2 = (bf16[3,6,4,512]{3,2,1,0:T(4,128)(2,1)S(1)}, bf16[3,6,4,512]{3,2,1,0:T(4,128)(2,1)S(1)}, u32[]{:S(2)}, u32[]{:S(2)}) collective-permute-start(bf16[3,6,4,512]{3,2,1,0:T(4,128)(2,1)S(1)} %get-tuple-element.28), channel_id=1, source_target_pairs={{0,1},{1,2},{2,3},{3,4},{4,5},{5,6},{6,7},{7,8},{8,9},{9,10},{10,1... | collective-permute-start | bytes 221192 | tf_op jit(solution)/shard_map/ppermute | solution.py:314
  56.5 0.0 copy-start.1
  56.5 0.0 copy-start.2
  56.5 2.1 %bias.1.bias_ref = bf16[16,288,288]{2,1,0:T(8,128)(2,1)S(1)} custom-call(bf16[16,288,288]{2,1,0:T(8,128)(2,1)} %bias_hbm), custom_call_target="tpu_custom_call" | custom-call | bytes 5308416 | tf_op jit(solution)/shard_map/bias/pallas_call | solution.py:248
  58.7 0.1 pad_add_fusion.spot_ref
  58.7 0.0 collective-permute-done.3
  58.7 3.7 %all-gather.2 = bf16[16,16,1536]{2,1,0:T(8,128)(2,1)S(1)} all-gather(bf16[8,16,1536]{2,1,0:T(8,128)(2,1)S(1)} %collective-permute-done.3), channel_id=4, replica_groups=mesh['xl'=2,'y'=8,'xh'=2,'z'=8,'c'=2] {'c'}, dimensions={0}, use_global_device_ids=true | all-gather | bytes 1179648 | tf_op jit(solution)/shard_map/all_gather | solution.py:319
  62.5 0.0 collective-permute-done.r0
  62.5 0.0 collective-permute-done.1.r1
  62.5 0.0 collective-permute-done.2.r2
  62.5 0.0 copy-done.1
  62.5 4.2 %attention.1 = (bf16[3,6,4,512]{3,2,1,0:T(4,128)(2,1)S(1)}, bf16[3,6,4,512]{3,2,1,0:T(4,128)(2,1)S(1)}, bf16[3,6,4,512]{3,2,1,0:T(4,128)(2,1)S(1)}, bf16[3,6,4,512]{3,2,1,0:T(4,128)(2,1)S(1)}) custom-call(s32[2]{0:T(128)S(1)} %pad_add_fusion.spot_ref, bf16[3,6,4,512]{3,2,1,0:T(4,128)(2,1)S(1)} %collective-permute-done.r0, ...), custom_call_target="tpu_custom_call" | custom-call | tf_op jit(solution)/shard_map/attention/pallas_call | solution.py:262
  66.7 0.0 copy-start
  66.7 0.0 copy-start.3
  66.8 0.0 copy-start.4
  66.8 8.6 %collective-permute-start.4 = (bf16[3,6,4,512]{3,2,1,0:T(4,128)(2,1)S(1)}, bf16[3,6,4,512]{3,2,1,0:T(4,128)(2,1)S(1)}, u32[]{:S(2)}, u32[]{:S(2)}) collective-permute-start(bf16[3,6,4,512]{3,2,1,0:T(4,128)(2,1)S(1)} %get-tuple-element.20), channel_id=1, source_target_pairs={{0,511},{1,480},{2,481},{3,482},{4,483},{5,484},{6,485},{7,486},{8... | collective-permute-start | bytes 221192 | tf_op jit(solution)/shard_map/ppermute | solution.py:324
  75.4 2.2 %collective-permute-start.5 = (bf16[3,6,4,512]{3,2,1,0:T(4,128)(2,1)S(1)}, bf16[3,6,4,512]{3,2,1,0:T(4,128)(2,1)S(1)}, u32[]{:S(2)}, u32[]{:S(2)}) collective-permute-start(bf16[3,6,4,512]{3,2,1,0:T(4,128)(2,1)S(1)} %get-tuple-element.21), channel_id=1, source_target_pairs={{0,480},{1,481},{2,482},{3,483},{4,484},{5,485},{6,486},{7,487},{8... | collective-permute-start | bytes 221192 | tf_op jit(solution)/shard_map/ppermute | solution.py:325
  77.6 3.6 %collective-permute-start.6 = (bf16[3,6,4,512]{3,2,1,0:T(4,128)(2,1)S(1)}, bf16[3,6,4,512]{3,2,1,0:T(4,128)(2,1)S(1)}, u32[]{:S(2)}, u32[]{:S(2)}) collective-permute-start(bf16[3,6,4,512]{3,2,1,0:T(4,128)(2,1)S(1)} %get-tuple-element.22), channel_id=1, source_target_pairs={{0,31},{1,0},{2,1},{3,2},{4,3},{5,4},{6,5},{7,6},{8,7},{9,8},{10,9... | collective-permute-start | bytes 221192 | tf_op jit(solution)/shard_map/ppermute | solution.py:326
  81.2 0.0 all-gather.6.cloned.1.call-done
  81.2 2.4 %stage.1 = (bf16[16,2,16,512]{3,2,1,0:T(8,128)(2,1)S(1)}, bf16[16,2,64,512]{3,2,1,0:T(8,128)(2,1)S(1)}, bf16[16,2,64,512]{3,2,1,0:T(8,128)(2,1)S(1)}) custom-call(bf16[16,2,144,512]{3,2,1,0:T(8,128)(2,1)} %bitcast.20), custom_call_target="tpu_custom_call" | custom-call | bytes 9437184 | tf_op jit(solution)/shard_map/stage/pallas_call | solution.py:274
  83.7 0.0 collective-permute-done.4.m3
  83.7 0.0 collective-permute-done.5.m2
  83.7 0.0 collective-permute-done.6.m1
  83.7 3.2 %tokens.1 = bf16[6,12,4,512]{3,2,1,0:T(4,128)(2,1)} custom-call(bf16[3,6,4,512]{3,2,1,0:T(4,128)(2,1)S(1)} %collective-permute-done.4.m3, bf16[3,6,4,512]{3,2,1,0:T(4,128)(2,1)S(1)} %collective-permute-done.5.m2, bf16[3,6,4,512]{3,2,1,0:T(4,128)(2,1)S(1)} %collective-permute-done.6.m1, bf16[3,6,4,512]{3,2,1,0:T(4,128)(2,1)S(1)} %get-tuple-element.23.m0, ...), custom_call_target="tpu_custom_call" | custom-call | tf_op jit(solution)/shard_map/tokens/pallas_call | solution.py:288
  (6 shorter events, 0.0 us)
Async XLA Ops:
  6.5 74.7 %all-gather.6.cloned.1.call-start = ((), (), s32[]{:S(2)}) async-start(), calls=%async_computation | async-start | bytes 5013504 | tf_op jit(solution)/shard_map/all_gather | solution.py:306
  43.2 15.5 %collective-permute-start.3 = (bf16[8,16,1536]{2,1,0:T(8,128)(2,1)S(1)}, bf16[8,16,1536]{2,1,0:T(8,128)(2,1)S(1)}, u32[]{:S(2)}, u32[]{:S(2)}) collective-permute-start(bf16[8,16,1536]{2,1,0:T(8,128)(2,1)S(1)} %dynamic-slice_bitcast_fusion), channel_id=1, source_target_pairs={{0,272},{272,0},{1,273},{273,1},{2,274},{274,2},{3,275},{275,3},{4... | collective-permute-start | bytes 1179656 | tf_op jit(solution)/shard_map/ppermute | solution.py:319
  49.5 13.0 %collective-permute-start = (bf16[3,6,4,512]{3,2,1,0:T(4,128)(2,1)S(1)}, bf16[3,6,4,512]{3,2,1,0:T(4,128)(2,1)S(1)}, u32[]{:S(2)}, u32[]{:S(2)}) collective-permute-start(bf16[3,6,4,512]{3,2,1,0:T(4,128)(2,1)S(1)} %get-tuple-element.30), channel_id=1, source_target_pairs={{0,33},{1,34},{2,35},{3,36},{4,37},{5,38},{6,39},{7,40},{8,41},{9,... | collective-permute-start | bytes 221192 | tf_op jit(solution)/shard_map/ppermute | solution.py:312
  51.5 11.0 %collective-permute-start.1 = (bf16[3,6,4,512]{3,2,1,0:T(4,128)(2,1)S(1)}, bf16[3,6,4,512]{3,2,1,0:T(4,128)(2,1)S(1)}, u32[]{:S(2)}, u32[]{:S(2)}) collective-permute-start(bf16[3,6,4,512]{3,2,1,0:T(4,128)(2,1)S(1)} %get-tuple-element.29), channel_id=1, source_target_pairs={{0,32},{1,33},{2,34},{3,35},{4,36},{5,37},{6,38},{7,39},{8,40},{9,... | collective-permute-start | bytes 221192 | tf_op jit(solution)/shard_map/ppermute | solution.py:313
  54.6 7.9 %collective-permute-start.2 = (bf16[3,6,4,512]{3,2,1,0:T(4,128)(2,1)S(1)}, bf16[3,6,4,512]{3,2,1,0:T(4,128)(2,1)S(1)}, u32[]{:S(2)}, u32[]{:S(2)}) collective-permute-start(bf16[3,6,4,512]{3,2,1,0:T(4,128)(2,1)S(1)} %get-tuple-element.28), channel_id=1, source_target_pairs={{0,1},{1,2},{2,3},{3,4},{4,5},{5,6},{6,7},{7,8},{8,9},{9,10},{10,1... | collective-permute-start | bytes 221192 | tf_op jit(solution)/shard_map/ppermute | solution.py:314
  56.5 6.0 %copy-start.1 = (bf16[288,288]{1,0:T(8,128)(2,1)S(1)}, bf16[288,288]{1,0:T(8,128)(2,1)}, u32[]{:S(2)}) copy-start(bf16[288,288]{1,0:T(8,128)(2,1)} %constant.31.clone.hot_ref) | copy-start | bytes 497668
  56.5 6.0 %copy-start.2 = (bf16[2,288,128]{2,1,0:T(8,128)(2,1)S(1)}, bf16[2,288,128]{2,1,0:T(8,128)(2,1)}, u32[]{:S(2)}) copy-start(bf16[2,288,128]{2,1,0:T(8,128)(2,1)} %constant.32.clone.tags_ref) | copy-start | bytes 442372
  66.7 17.0 %copy-start = (bf16[4,6,12,512]{3,0,2,1:T(4,128)(2,1)S(1)}, bf16[4,6,12,512]{3,0,2,1:T(4,128)(2,1)}, u32[]{:S(2)}) copy-start(bf16[4,6,12,512]{3,0,2,1:T(4,128)(2,1)} %param.10) | copy-start | bytes 884740
  66.7 17.0 %copy-start.3 = (f32[512]{0:T(512)S(1)}, f32[512]{0:T(512)}, u32[]{:S(2)}) copy-start(f32[512]{0:T(512)} %param.14) | copy-start | bytes 6148
  66.8 17.0 %copy-start.4 = (f32[512]{0:T(512)S(1)}, f32[512]{0:T(512)}, u32[]{:S(2)}) copy-start(f32[512]{0:T(512)} %param.17) | copy-start | bytes 6148
  66.8 16.9 %collective-permute-start.4 = (bf16[3,6,4,512]{3,2,1,0:T(4,128)(2,1)S(1)}, bf16[3,6,4,512]{3,2,1,0:T(4,128)(2,1)S(1)}, u32[]{:S(2)}, u32[]{:S(2)}) collective-permute-start(bf16[3,6,4,512]{3,2,1,0:T(4,128)(2,1)S(1)} %get-tuple-element.20), channel_id=1, source_target_pairs={{0,511},{1,480},{2,481},{3,482},{4,483},{5,484},{6,485},{7,486},{8... | collective-permute-start | bytes 221192 | tf_op jit(solution)/shard_map/ppermute | solution.py:324
  75.4 8.3 %collective-permute-start.5 = (bf16[3,6,4,512]{3,2,1,0:T(4,128)(2,1)S(1)}, bf16[3,6,4,512]{3,2,1,0:T(4,128)(2,1)S(1)}, u32[]{:S(2)}, u32[]{:S(2)}) collective-permute-start(bf16[3,6,4,512]{3,2,1,0:T(4,128)(2,1)S(1)} %get-tuple-element.21), channel_id=1, source_target_pairs={{0,480},{1,481},{2,482},{3,483},{4,484},{5,485},{6,486},{7,487},{8... | collective-permute-start | bytes 221192 | tf_op jit(solution)/shard_map/ppermute | solution.py:325
  77.6 6.1 %collective-permute-start.6 = (bf16[3,6,4,512]{3,2,1,0:T(4,128)(2,1)S(1)}, bf16[3,6,4,512]{3,2,1,0:T(4,128)(2,1)S(1)}, u32[]{:S(2)}, u32[]{:S(2)}) collective-permute-start(bf16[3,6,4,512]{3,2,1,0:T(4,128)(2,1)S(1)} %get-tuple-element.22), channel_id=1, source_target_pairs={{0,31},{1,0},{2,1},{3,2},{4,3},{5,4},{6,5},{7,6},{8,7},{9,8},{10,9... | collective-permute-start | bytes 221192 | tf_op jit(solution)/shard_map/ppermute | solution.py:326
Sparse Core Ops, SparseCore 0:
  14.2 53.4 all-gather.5

commit v9 on v8

--- a/solution.py
+++ b/solution.py
@@ -127,7 +127,7 @@
 
 
 def attention_kernel(
-    spot_ref, r0, r1, r2, r3, mine_ref, other_ref, hot_ref, tags_ref, bias_ref, o0, o1, o2, o3
+    spot_ref, r1, r2, r0, r3, mine_ref, other_ref, hot_ref, tags_ref, bias_ref, o0, o1, o2, o3
 ):
     hot = hot_ref[...]
     rows = stacked([r[...] for r in (r0, r1, r2, r3)]).astype(BF16)
@@ -181,7 +181,7 @@
 
 
 def token_kernel(
-    m3, m2, m1, m0, cells_ref, wp, wu, wd, attn_gain_ref, mlp_gain_ref, out_ref
+    m2, m3, m1, m0, cells_ref, wp, wu, wd, attn_gain_ref, mlp_gain_ref, out_ref
 ):
     attended = stacked([m[...] for m in (m0, m1, m2, m3)]).astype(BF16)
     cells = stacked([corner(cells_ref, i, j) for i in range(2) for j in range(2)])
@@ -309,9 +309,9 @@
     cells = latent.transpose(1, 2, 0, 3)
     cells_after, bias, mine = lax.optimization_barrier((cells, position_bias, mine))
     rolled = [
-        lax.ppermute(corner(cells_after, 1, 1), AXES, shifted(1, 1)),
         lax.ppermute(corner(cells_after, 1, 0), AXES, shifted(1, 0)),
         lax.ppermute(corner(cells_after, 0, 1), AXES, shifted(0, 1)),
+        lax.ppermute(corner(cells_after, 1, 1), AXES, shifted(1, 1)),
         corner(cells_after, 0, 0),
     ]
     core = lax.axis_index("c")
@@ -321,8 +321,8 @@
     spot = jnp.stack([lax.axis_index("xh"), (lax.axis_index(LAT) == 0).astype(jnp.int32)])
     attended = attention(spot, rolled, mine, theirs, held_bias(bias))
     restored = [
+        lax.ppermute(attended[1], AXES, shifted(-1, 0)),
         lax.ppermute(attended[0], AXES, shifted(-1, -1)),
-        lax.ppermute(attended[1], AXES, shifted(-1, 0)),
         lax.ppermute(attended[2], AXES, shifted(0, -1)),
         attended[3],
     ]

time: 94.2 us -> 93.6 us (level)
    ppermute x1, starting transfers between devices: 8.61 us -> 5.05 us  [shards(): lax.ppermute(attended[0], AXES, shifted(-1, -1))]
    ppermute x1, starting transfers between devices: 2.24 us -> 4.1 us  [shards(): lax.ppermute(attended[1], AXES, shifted(-1, 0))]
    ppermute x1, starting transfers between devices: 3.57 us -> 4.62 us  [shards(): lax.ppermute(attended[2], AXES, shifted(0, -1))]
  transfers between devices with their start and end apart: 8 -> 8, of which waited for: 0 -> 1; matrix products, arithmetic and copies ran while one was open for 1% -> 1% of each run, Pallas kernels for 9% -> 9%
where the time goes in v9:
time: 93.6 us; the launch traced here: 93.2 us
  blocking collectives  39.3 us (42%)
  starting transfers between devices  25.9 us (28%)
  between operations  13.6 us (15%)
  Pallas kernels  12.8 us (14%)
  local copies, waits for them, and re-layouts  1.17 us (1%)
    all_gather x1, blocking collectives, shards(): mine = lax.all_gather(qkv_weight, ('z', 'c'), axis=0, tiled=False)  29.1 us
    all_gather x1, blocking collectives, shards(): lax.all_gather(own, AXES, axis=0, tiled=False, axis_index_groups=mirrored...  6.6 us
    ppermute x1, starting transfers between devices, shards(): lax.ppermute(sent, AXES, mirrored())  5.15 us
    ppermute x1, starting transfers between devices, shards(): lax.ppermute(attended[0], AXES, shifted(-1, -1))  5.05 us
    ppermute x1, starting transfers between devices, shards(): lax.ppermute(attended[2], AXES, shifted(0, -1))  4.62 us
    pallas_call x1, Pallas kernels, attention(): pl.pallas_call(attention_kernel, in_specs=[scalars()] + [held()] * (len(q...  4.2 us
    ppermute x1, starting transfers between devices, shards(): lax.ppermute(attended[1], AXES, shifted(-1, 0))  4.1 us
    all_gather x1, blocking collectives, shards(): lax.all_gather(lax.ppermute(sent, AXES, mirrored()), 'c', axis=0, tiled=F...  3.51 us
  transfers between devices with their start and end apart: 8, of which 1 were waited for; matrix products, arithmetic and copies ran while one was open for 1% of the time, Pallas kernels for 9%

profile of v9, /device:TPU:1, one launch (start us, length us, event | category | flops | bytes accessed | tf_op | source)
XLA Modules:
  0.0 93.2 jit_solution(5789519295944120779)
XLA Ops:
  6.5 0.9 pack.1
  7.4 6.6 %all-gather = bf16[288,512]{1,0:T(8,128)(2,1)} all-gather(bf16[144,512]{1,0:T(8,128)(2,1)S(1)} %pack.1), channel_id=2, replica_groups={{0,272},{1,273},{2,274},{3,275},{4,276},{5,277},{6,278},{7,279},{8,280}..., dimensions={0}, use_global_device_ids=true | all-gather | bytes 442368 | tf_op jit(solution)/shard_map/all_gather | solution.py:305
  14.0 0.0 all-gather.6.cloned.1.call-update
  14.1 29.1 %all-gather.1 = bf16[256,1536]{1,0:T(8,128)(2,1)S(1)} all-gather(bf16[16,1536]{1,0:T(8,128)(2,1)} %param.11), channel_id=3, replica_groups=mesh['xl'=2,'y'=8,'xh'=2,'z'=8,'c'=2] {'z','c'}, dimensions={0}, use_global_device_ids=true | all-gather | bytes 835584 | tf_op jit(solution)/shard_map/all_gather | solution.py:308
  43.2 5.2 %collective-permute-start.3 = (bf16[8,16,1536]{2,1,0:T(8,128)(2,1)S(1)}, bf16[8,16,1536]{2,1,0:T(8,128)(2,1)S(1)}, u32[]{:S(2)}, u32[]{:S(2)}) collective-permute-start(bf16[8,16,1536]{2,1,0:T(8,128)(2,1)S(1)} %dynamic-slice_bitcast_fusion), channel_id=1, source_target_pairs={{0,272},{272,0},{1,273},{273,1},{2,274},{274,2},{3,275},{275,3},{4... | collective-permute-start | bytes 1179656 | tf_op jit(solution)/shard_map/ppermute | solution.py:319
  48.4 1.1 %fusion = (bf16[3,6,4,512]{3,2,1,0:T(4,128)(2,1)S(1)}, bf16[3,6,4,512]{3,2,1,0:T(4,128)(2,1)S(1)}, bf16[3,6,4,512]{3,2,1,0:T(4,128)(2,1)S(1)}, bf16[3,6,4,512]{3,2,1,0:T(4,128)(2,1)S(1)}) fusion(bf16[6,12,4,512]{3,2,1,0:T(4,128)(2,1)} %bitcast.16), kind=kLoop, calls=%fused_computation.2 | loop fusion | bytes 589824 | tf_op jit(solution)/shard_map/slice | solution.py:107
  49.5 3.1 %collective-permute-start = (bf16[3,6,4,512]{3,2,1,0:T(4,128)(2,1)S(1)}, bf16[3,6,4,512]{3,2,1,0:T(4,128)(2,1)S(1)}, u32[]{:S(2)}, u32[]{:S(2)}) collective-permute-start(bf16[3,6,4,512]{3,2,1,0:T(4,128)(2,1)S(1)} %get-tuple-element.30), channel_id=1, source_target_pairs={{0,32},{1,33},{2,34},{3,35},{4,36},{5,37},{6,38},{7,39},{8,40},{9,... | collective-permute-start | bytes 221192 | tf_op jit(solution)/shard_map/ppermute | solution.py:312
  52.6 1.9 %collective-permute-start.1 = (bf16[3,6,4,512]{3,2,1,0:T(4,128)(2,1)S(1)}, bf16[3,6,4,512]{3,2,1,0:T(4,128)(2,1)S(1)}, u32[]{:S(2)}, u32[]{:S(2)}) collective-permute-start(bf16[3,6,4,512]{3,2,1,0:T(4,128)(2,1)S(1)} %get-tuple-element.29), channel_id=1, source_target_pairs={{0,1},{1,2},{2,3},{3,4},{4,5},{5,6},{6,7},{7,8},{8,9},{9,10},{10,1... | collective-permute-start | bytes 221192 | tf_op jit(solution)/shard_map/ppermute | solution.py:313
  54.6 1.9 %collective-permute-start.2 = (bf16[3,6,4,512]{3,2,1,0:T(4,128)(2,1)S(1)}, bf16[3,6,4,512]{3,2,1,0:T(4,128)(2,1)S(1)}, u32[]{:S(2)}, u32[]{:S(2)}) collective-permute-start(bf16[3,6,4,512]{3,2,1,0:T(4,128)(2,1)S(1)} %get-tuple-element.28), channel_id=1, source_target_pairs={{0,33},{1,34},{2,35},{3,36},{4,37},{5,38},{6,39},{7,40},{8,41},{9,... | collective-permute-start | bytes 221192 | tf_op jit(solution)/shard_map/ppermute | solution.py:314
  56.5 0.0 copy-start.1
  56.5 0.0 copy-start.2
  56.5 2.1 %bias.1.bias_ref = bf16[16,288,288]{2,1,0:T(8,128)(2,1)S(1)} custom-call(bf16[16,288,288]{2,1,0:T(8,128)(2,1)} %bias_hbm), custom_call_target="tpu_custom_call" | custom-call | bytes 5308416 | tf_op jit(solution)/shard_map/bias/pallas_call | solution.py:248
  58.7 0.1 pad_add_fusion.spot_ref
  58.7 0.0 collective-permute-done.3
  58.7 3.5 %all-gather.2 = bf16[16,16,1536]{2,1,0:T(8,128)(2,1)S(1)} all-gather(bf16[8,16,1536]{2,1,0:T(8,128)(2,1)S(1)} %collective-permute-done.3), channel_id=4, replica_groups=mesh['xl'=2,'y'=8,'xh'=2,'z'=8,'c'=2] {'c'}, dimensions={0}, use_global_device_ids=true | all-gather | bytes 1179648 | tf_op jit(solution)/shard_map/all_gather | solution.py:319
  62.2 0.0 collective-permute-done.r1
  62.3 0.0 collective-permute-done.1.r2
  62.3 0.4 collective-permute-done.2.r0
  62.7 0.0 copy-done.1
  62.7 4.2 %attention.1 = (bf16[3,6,4,512]{3,2,1,0:T(4,128)(2,1)S(1)}, bf16[3,6,4,512]{3,2,1,0:T(4,128)(2,1)S(1)}, bf16[3,6,4,512]{3,2,1,0:T(4,128)(2,1)S(1)}, bf16[3,6,4,512]{3,2,1,0:T(4,128)(2,1)S(1)}) custom-call(s32[2]{0:T(128)S(1)} %pad_add_fusion.spot_ref, bf16[3,6,4,512]{3,2,1,0:T(4,128)(2,1)S(1)} %collective-permute-done.r1, ...), custom_call_target="tpu_custom_call" | custom-call | tf_op jit(solution)/shard_map/attention/pallas_call | solution.py:262
  66.9 0.0 copy-start
  66.9 0.0 copy-start.3
  66.9 0.0 copy-start.4
  66.9 4.1 %collective-permute-start.4 = (bf16[3,6,4,512]{3,2,1,0:T(4,128)(2,1)S(1)}, bf16[3,6,4,512]{3,2,1,0:T(4,128)(2,1)S(1)}, u32[]{:S(2)}, u32[]{:S(2)}) collective-permute-start(bf16[3,6,4,512]{3,2,1,0:T(4,128)(2,1)S(1)} %get-tuple-element.20), channel_id=1, source_target_pairs={{0,480},{1,481},{2,482},{3,483},{4,484},{5,485},{6,486},{7,487},{8... | collective-permute-start | bytes 221192 | tf_op jit(solution)/shard_map/ppermute | solution.py:324
  71.0 5.0 %collective-permute-start.5 = (bf16[3,6,4,512]{3,2,1,0:T(4,128)(2,1)S(1)}, bf16[3,6,4,512]{3,2,1,0:T(4,128)(2,1)S(1)}, u32[]{:S(2)}, u32[]{:S(2)}) collective-permute-start(bf16[3,6,4,512]{3,2,1,0:T(4,128)(2,1)S(1)} %get-tuple-element.21), channel_id=1, source_target_pairs={{0,511},{1,480},{2,481},{3,482},{4,483},{5,484},{6,485},{7,486},{8... | collective-permute-start | bytes 221192 | tf_op jit(solution)/shard_map/ppermute | solution.py:325
  76.1 4.6 %collective-permute-start.6 = (bf16[3,6,4,512]{3,2,1,0:T(4,128)(2,1)S(1)}, bf16[3,6,4,512]{3,2,1,0:T(4,128)(2,1)S(1)}, u32[]{:S(2)}, u32[]{:S(2)}) collective-permute-start(bf16[3,6,4,512]{3,2,1,0:T(4,128)(2,1)S(1)} %get-tuple-element.22), channel_id=1, source_target_pairs={{0,31},{1,0},{2,1},{3,2},{4,3},{5,4},{6,5},{7,6},{8,7},{9,8},{10,9... | collective-permute-start | bytes 221192 | tf_op jit(solution)/shard_map/ppermute | solution.py:326
  80.7 0.0 all-gather.6.cloned.1.call-done
  80.7 2.4 %stage.1 = (bf16[16,2,16,512]{3,2,1,0:T(8,128)(2,1)S(1)}, bf16[16,2,64,512]{3,2,1,0:T(8,128)(2,1)S(1)}, bf16[16,2,64,512]{3,2,1,0:T(8,128)(2,1)S(1)}) custom-call(bf16[16,2,144,512]{3,2,1,0:T(8,128)(2,1)} %bitcast.20), custom_call_target="tpu_custom_call" | custom-call | bytes 9437184 | tf_op jit(solution)/shard_map/stage/pallas_call | solution.py:274
  83.2 0.0 collective-permute-done.4.m2
  83.2 0.0 collective-permute-done.5.m3
  83.2 0.0 collective-permute-done.6.m1
  83.2 3.2 %tokens.1 = bf16[6,12,4,512]{3,2,1,0:T(4,128)(2,1)} custom-call(bf16[3,6,4,512]{3,2,1,0:T(4,128)(2,1)S(1)} %collective-permute-done.4.m2, bf16[3,6,4,512]{3,2,1,0:T(4,128)(2,1)S(1)} %collective-permute-done.5.m3, bf16[3,6,4,512]{3,2,1,0:T(4,128)(2,1)S(1)} %collective-permute-done.6.m1, bf16[3,6,4,512]{3,2,1,0:T(4,128)(2,1)S(1)} %get-tuple-element.23.m0, ...), custom_call_target="tpu_custom_call" | custom-call | tf_op jit(solution)/shard_map/tokens/pallas_call | solution.py:288
  (6 shorter events, 0.0 us)
Async XLA Ops:
  6.5 74.2 %all-gather.6.cloned.1.call-start = ((), (), s32[]{:S(2)}) async-start(), calls=%async_computation | async-start | bytes 5013504 | tf_op jit(solution)/shard_map/all_gather | solution.py:306
  43.2 15.5 %collective-permute-start.3 = (bf16[8,16,1536]{2,1,0:T(8,128)(2,1)S(1)}, bf16[8,16,1536]{2,1,0:T(8,128)(2,1)S(1)}, u32[]{:S(2)}, u32[]{:S(2)}) collective-permute-start(bf16[8,16,1536]{2,1,0:T(8,128)(2,1)S(1)} %dynamic-slice_bitcast_fusion), channel_id=1, source_target_pairs={{0,272},{272,0},{1,273},{273,1},{2,274},{274,2},{3,275},{275,3},{4... | collective-permute-start | bytes 1179656 | tf_op jit(solution)/shard_map/ppermute | solution.py:319
  49.5 12.7 %collective-permute-start = (bf16[3,6,4,512]{3,2,1,0:T(4,128)(2,1)S(1)}, bf16[3,6,4,512]{3,2,1,0:T(4,128)(2,1)S(1)}, u32[]{:S(2)}, u32[]{:S(2)}) collective-permute-start(bf16[3,6,4,512]{3,2,1,0:T(4,128)(2,1)S(1)} %get-tuple-element.30), channel_id=1, source_target_pairs={{0,32},{1,33},{2,34},{3,35},{4,36},{5,37},{6,38},{7,39},{8,40},{9,... | collective-permute-start | bytes 221192 | tf_op jit(solution)/shard_map/ppermute | solution.py:312
  52.6 9.6 %collective-permute-start.1 = (bf16[3,6,4,512]{3,2,1,0:T(4,128)(2,1)S(1)}, bf16[3,6,4,512]{3,2,1,0:T(4,128)(2,1)S(1)}, u32[]{:S(2)}, u32[]{:S(2)}) collective-permute-start(bf16[3,6,4,512]{3,2,1,0:T(4,128)(2,1)S(1)} %get-tuple-element.29), channel_id=1, source_target_pairs={{0,1},{1,2},{2,3},{3,4},{4,5},{5,6},{6,7},{7,8},{8,9},{9,10},{10,1... | collective-permute-start | bytes 221192 | tf_op jit(solution)/shard_map/ppermute | solution.py:313
  54.6 8.1 %collective-permute-start.2 = (bf16[3,6,4,512]{3,2,1,0:T(4,128)(2,1)S(1)}, bf16[3,6,4,512]{3,2,1,0:T(4,128)(2,1)S(1)}, u32[]{:S(2)}, u32[]{:S(2)}) collective-permute-start(bf16[3,6,4,512]{3,2,1,0:T(4,128)(2,1)S(1)} %get-tuple-element.28), channel_id=1, source_target_pairs={{0,33},{1,34},{2,35},{3,36},{4,37},{5,38},{6,39},{7,40},{8,41},{9,... | collective-permute-start | bytes 221192 | tf_op jit(solution)/shard_map/ppermute | solution.py:314
  56.5 6.1 %copy-start.1 = (bf16[288,288]{1,0:T(8,128)(2,1)S(1)}, bf16[288,288]{1,0:T(8,128)(2,1)}, u32[]{:S(2)}) copy-start(bf16[288,288]{1,0:T(8,128)(2,1)} %constant.31.clone.hot_ref) | copy-start | bytes 497668
  56.5 6.1 %copy-start.2 = (bf16[2,288,128]{2,1,0:T(8,128)(2,1)S(1)}, bf16[2,288,128]{2,1,0:T(8,128)(2,1)}, u32[]{:S(2)}) copy-start(bf16[2,288,128]{2,1,0:T(8,128)(2,1)} %constant.32.clone.tags_ref) | copy-start | bytes 442372
  66.9 16.3 %copy-start = (bf16[4,6,12,512]{3,0,2,1:T(4,128)(2,1)S(1)}, bf16[4,6,12,512]{3,0,2,1:T(4,128)(2,1)}, u32[]{:S(2)}) copy-start(bf16[4,6,12,512]{3,0,2,1:T(4,128)(2,1)} %param.10) | copy-start | bytes 884740
  66.9 16.3 %copy-start.3 = (f32[512]{0:T(512)S(1)}, f32[512]{0:T(512)}, u32[]{:S(2)}) copy-start(f32[512]{0:T(512)} %param.14) | copy-start | bytes 6148
  66.9 16.3 %copy-start.4 = (f32[512]{0:T(512)S(1)}, f32[512]{0:T(512)}, u32[]{:S(2)}) copy-start(f32[512]{0:T(512)} %param.17) | copy-start | bytes 6148
  66.9 16.3 %collective-permute-start.4 = (bf16[3,6,4,512]{3,2,1,0:T(4,128)(2,1)S(1)}, bf16[3,6,4,512]{3,2,1,0:T(4,128)(2,1)S(1)}, u32[]{:S(2)}, u32[]{:S(2)}) collective-permute-start(bf16[3,6,4,512]{3,2,1,0:T(4,128)(2,1)S(1)} %get-tuple-element.20), channel_id=1, source_target_pairs={{0,480},{1,481},{2,482},{3,483},{4,484},{5,485},{6,486},{7,487},{8... | collective-permute-start | bytes 221192 | tf_op jit(solution)/shard_map/ppermute | solution.py:324
  71.0 12.2 %collective-permute-start.5 = (bf16[3,6,4,512]{3,2,1,0:T(4,128)(2,1)S(1)}, bf16[3,6,4,512]{3,2,1,0:T(4,128)(2,1)S(1)}, u32[]{:S(2)}, u32[]{:S(2)}) collective-permute-start(bf16[3,6,4,512]{3,2,1,0:T(4,128)(2,1)S(1)} %get-tuple-element.21), channel_id=1, source_target_pairs={{0,511},{1,480},{2,481},{3,482},{4,483},{5,484},{6,485},{7,486},{8... | collective-permute-start | bytes 221192 | tf_op jit(solution)/shard_map/ppermute | solution.py:325
  76.1 7.1 %collective-permute-start.6 = (bf16[3,6,4,512]{3,2,1,0:T(4,128)(2,1)S(1)}, bf16[3,6,4,512]{3,2,1,0:T(4,128)(2,1)S(1)}, u32[]{:S(2)}, u32[]{:S(2)}) collective-permute-start(bf16[3,6,4,512]{3,2,1,0:T(4,128)(2,1)S(1)} %get-tuple-element.22), channel_id=1, source_target_pairs={{0,31},{1,0},{2,1},{3,2},{4,3},{5,4},{6,5},{7,6},{8,7},{9,8},{10,9... | collective-permute-start | bytes 221192 | tf_op jit(solution)/shard_map/ppermute | solution.py:326
Sparse Core Ops, SparseCore 0:
  14.2 53.3 all-gather.5

commit v10 on v9

--- a/solution.py
+++ b/solution.py
@@ -22,7 +22,7 @@
 PER_GROUP = LANES // HEAD_DIM
 GROUPS = HEADS // PER_GROUP
 PADDED = 3 * LANES
-PIECES = 4
+PIECES = 2
 MASKED = -1e30
 EPSILON = 1e-05
 F32 = jnp.float32
@@ -181,7 +181,8 @@
 
 
 def token_kernel(
-    m2, m3, m1, m0, cells_ref, wp, wu, wd, attn_gain_ref, mlp_gain_ref, out_ref
+    m2, m3, m1, m0, cells_ref, wp, wu, wd, attn_gain_ref, mlp_gain_ref, out_hbm,
+    out_ref, sems,
 ):
     attended = stacked([m[...] for m in (m0, m1, m2, m3)]).astype(BF16)
     cells = stacked([corner(cells_ref, i, j) for i in range(2) for j in range(2)])
@@ -200,12 +201,18 @@
         lowered = part if lowered is None else lowered + part
     updated = rows.astype(F32) + normed(lowered, mlp_gain_ref[...])
     run = HALF_LON * LEVELS
+    copies = []
     for i in range(2):
         for j in range(2):
             for row in range(HALF_LAT):
                 start = (i * 2 + j) * QUARTER + row * run
                 piece = updated[start : start + run].reshape(HALF_LON, LEVELS, D)
                 out_ref[i * HALF_LAT + row, j * HALF_LON : (j + 1) * HALF_LON] = piece.astype(BF16)
+        half = slice(i * HALF_LAT, (i + 1) * HALF_LAT)
+        copies.append(pltpu.make_async_copy(out_ref.at[half], out_hbm.at[half], sems.at[i]))
+        copies[-1].start()
+    for copy in copies:
+        copy.wait()
 
 
 def whole(shape):
@@ -285,17 +292,16 @@
 
 def tokens(quarters, cells, weights, attn_gain, mlp_gain):
     out = (WLAT, WLON, LEVELS, D)
+    operands = (*quarters, cells, *weights, attn_gain.reshape(1, D), mlp_gain.reshape(1, D))
     return pl.pallas_call(
         token_kernel,
-        grid=(1,),
-        in_specs=[whole(CORNER)] * 4
-        + [whole(a.shape) for a in (cells, *weights)]
-        + [whole((1, D))] * 2,
-        out_specs=whole(out),
+        in_specs=[held()] * len(operands),
+        out_specs=fetched(),
         out_shape=jax.ShapeDtypeStruct(out, BF16),
+        scratch_shapes=[pltpu.VMEM(out, BF16), pltpu.SemaphoreType.DMA((2,))],
         compiler_params=pltpu.CompilerParams(vmem_limit_bytes=TOKENS_LIMIT),
         name="tokens",
-    )(*quarters, cells, *weights, attn_gain.reshape(1, D), mlp_gain.reshape(1, D))
+    )(*operands)
 
 
 def shards(

time: 93.6 us -> 93.3 us (level)
  no operation moved by 1% of the time
where the time goes in v10:
time: 93.3 us; the launch traced here: 92.9 us
  blocking collectives  39.3 us (42%)
  starting transfers between devices  25.9 us (28%)
  between operations  13.6 us (15%)
  Pallas kernels  12.4 us (13%)
  local copies, waits for them, and re-layouts  1.17 us (1%)
    all_gather x1, blocking collectives, shards(): mine = lax.all_gather(qkv_weight, ('z', 'c'), axis=0, tiled=False)  29.1 us
    all_gather x1, blocking collectives, shards(): lax.all_gather(own, AXES, axis=0, tiled=False, axis_index_groups=mirrored...  6.6 us
    ppermute x1, starting transfers between devices, shards(): lax.ppermute(sent, AXES, mirrored())  5.15 us
    ppermute x1, starting transfers between devices, shards(): lax.ppermute(attended[0], AXES, shifted(-1, -1))  5.05 us
    ppermute x1, starting transfers between devices, shards(): lax.ppermute(attended[2], AXES, shifted(0, -1))  4.62 us
    pallas_call x1, Pallas kernels, attention(): pl.pallas_call(attention_kernel, in_specs=[scalars()] + [held()] * (len(q...  4.2 us
    ppermute x1, starting transfers between devices, shards(): lax.ppermute(attended[1], AXES, shifted(-1, 0))  4.1 us
    all_gather x1, blocking collectives, shards(): lax.all_gather(lax.ppermute(sent, AXES, mirrored()), 'c', axis=0, tiled=F...  3.51 us
  transfers between devices with their start and end apart: 8, of which 1 were waited for; matrix products, arithmetic and copies ran while one was open for 1% of the time, Pallas kernels for 9%

profile of v10, /device:TPU:1, one launch (start us, length us, event | category | flops | bytes accessed | tf_op | source)
XLA Modules:
  0.0 92.9 jit_solution(5566933290857953938)
XLA Ops:
  6.5 0.9 pack.1
  7.4 6.6 %all-gather = bf16[288,512]{1,0:T(8,128)(2,1)} all-gather(bf16[144,512]{1,0:T(8,128)(2,1)S(1)} %pack.1), channel_id=2, replica_groups={{0,272},{1,273},{2,274},{3,275},{4,276},{5,277},{6,278},{7,279},{8,280}..., dimensions={0}, use_global_device_ids=true | all-gather | bytes 442368 | tf_op jit(solution)/shard_map/all_gather | solution.py:311
  14.0 0.0 all-gather.6.cloned.1.call-update
  14.1 29.1 %all-gather.1 = bf16[256,1536]{1,0:T(8,128)(2,1)S(1)} all-gather(bf16[16,1536]{1,0:T(8,128)(2,1)} %param.11), channel_id=3, replica_groups=mesh['xl'=2,'y'=8,'xh'=2,'z'=8,'c'=2] {'z','c'}, dimensions={0}, use_global_device_ids=true | all-gather | bytes 835584 | tf_op jit(solution)/shard_map/all_gather | solution.py:314
  43.2 5.2 %collective-permute-start.3 = (bf16[8,16,1536]{2,1,0:T(8,128)(2,1)S(1)}, bf16[8,16,1536]{2,1,0:T(8,128)(2,1)S(1)}, u32[]{:S(2)}, u32[]{:S(2)}) collective-permute-start(bf16[8,16,1536]{2,1,0:T(8,128)(2,1)S(1)} %dynamic-slice_bitcast_fusion), channel_id=1, source_target_pairs={{0,272},{272,0},{1,273},{273,1},{2,274},{274,2},{3,275},{275,3},{4... | collective-permute-start | bytes 1179656 | tf_op jit(solution)/shard_map/ppermute | solution.py:325
  48.4 1.1 %fusion = (bf16[3,6,4,512]{3,2,1,0:T(4,128)(2,1)S(1)}, bf16[3,6,4,512]{3,2,1,0:T(4,128)(2,1)S(1)}, bf16[3,6,4,512]{3,2,1,0:T(4,128)(2,1)S(1)}, bf16[3,6,4,512]{3,2,1,0:T(4,128)(2,1)S(1)}) fusion(bf16[6,12,4,512]{3,2,1,0:T(4,128)(2,1)} %bitcast.16), kind=kLoop, calls=%fused_computation.2 | loop fusion | bytes 589824 | tf_op jit(solution)/shard_map/slice | solution.py:107
  49.5 3.1 %collective-permute-start = (bf16[3,6,4,512]{3,2,1,0:T(4,128)(2,1)S(1)}, bf16[3,6,4,512]{3,2,1,0:T(4,128)(2,1)S(1)}, u32[]{:S(2)}, u32[]{:S(2)}) collective-permute-start(bf16[3,6,4,512]{3,2,1,0:T(4,128)(2,1)S(1)} %get-tuple-element.30), channel_id=1, source_target_pairs={{0,32},{1,33},{2,34},{3,35},{4,36},{5,37},{6,38},{7,39},{8,40},{9,... | collective-permute-start | bytes 221192 | tf_op jit(solution)/shard_map/ppermute | solution.py:318
  52.6 1.9 %collective-permute-start.1 = (bf16[3,6,4,512]{3,2,1,0:T(4,128)(2,1)S(1)}, bf16[3,6,4,512]{3,2,1,0:T(4,128)(2,1)S(1)}, u32[]{:S(2)}, u32[]{:S(2)}) collective-permute-start(bf16[3,6,4,512]{3,2,1,0:T(4,128)(2,1)S(1)} %get-tuple-element.29), channel_id=1, source_target_pairs={{0,1},{1,2},{2,3},{3,4},{4,5},{5,6},{6,7},{7,8},{8,9},{9,10},{10,1... | collective-permute-start | bytes 221192 | tf_op jit(solution)/shard_map/ppermute | solution.py:319
  54.6 1.9 %collective-permute-start.2 = (bf16[3,6,4,512]{3,2,1,0:T(4,128)(2,1)S(1)}, bf16[3,6,4,512]{3,2,1,0:T(4,128)(2,1)S(1)}, u32[]{:S(2)}, u32[]{:S(2)}) collective-permute-start(bf16[3,6,4,512]{3,2,1,0:T(4,128)(2,1)S(1)} %get-tuple-element.28), channel_id=1, source_target_pairs={{0,33},{1,34},{2,35},{3,36},{4,37},{5,38},{6,39},{7,40},{8,41},{9,... | collective-permute-start | bytes 221192 | tf_op jit(solution)/shard_map/ppermute | solution.py:320
  56.5 0.0 copy-start.1
  56.5 0.0 copy-start.2
  56.5 2.1 %bias.1.bias_ref = bf16[16,288,288]{2,1,0:T(8,128)(2,1)S(1)} custom-call(bf16[16,288,288]{2,1,0:T(8,128)(2,1)} %bias_hbm), custom_call_target="tpu_custom_call" | custom-call | bytes 5308416 | tf_op jit(solution)/shard_map/bias/pallas_call | solution.py:255
  58.7 0.1 pad_add_fusion.spot_ref
  58.7 0.0 collective-permute-done.3
  58.7 3.5 %all-gather.2 = bf16[16,16,1536]{2,1,0:T(8,128)(2,1)S(1)} all-gather(bf16[8,16,1536]{2,1,0:T(8,128)(2,1)S(1)} %collective-permute-done.3), channel_id=4, replica_groups=mesh['xl'=2,'y'=8,'xh'=2,'z'=8,'c'=2] {'c'}, dimensions={0}, use_global_device_ids=true | all-gather | bytes 1179648 | tf_op jit(solution)/shard_map/all_gather | solution.py:325
  62.2 0.0 collective-permute-done.r1
  62.3 0.0 collective-permute-done.1.r2
  62.3 0.4 collective-permute-done.2.r0
  62.7 0.0 copy-done.1
  62.7 4.2 %attention.1 = (bf16[3,6,4,512]{3,2,1,0:T(4,128)(2,1)S(1)}, bf16[3,6,4,512]{3,2,1,0:T(4,128)(2,1)S(1)}, bf16[3,6,4,512]{3,2,1,0:T(4,128)(2,1)S(1)}, bf16[3,6,4,512]{3,2,1,0:T(4,128)(2,1)S(1)}) custom-call(s32[2]{0:T(128)S(1)} %pad_add_fusion.spot_ref, bf16[3,6,4,512]{3,2,1,0:T(4,128)(2,1)S(1)} %collective-permute-done.r1, ...), custom_call_target="tpu_custom_call" | custom-call | tf_op jit(solution)/shard_map/attention/pallas_call | solution.py:269
  66.9 0.0 copy-start
  66.9 0.0 copy-start.3
  66.9 0.0 copy-start.4
  66.9 4.1 %collective-permute-start.4 = (bf16[3,6,4,512]{3,2,1,0:T(4,128)(2,1)S(1)}, bf16[3,6,4,512]{3,2,1,0:T(4,128)(2,1)S(1)}, u32[]{:S(2)}, u32[]{:S(2)}) collective-permute-start(bf16[3,6,4,512]{3,2,1,0:T(4,128)(2,1)S(1)} %get-tuple-element.20), channel_id=1, source_target_pairs={{0,480},{1,481},{2,482},{3,483},{4,484},{5,485},{6,486},{7,487},{8... | collective-permute-start | bytes 221192 | tf_op jit(solution)/shard_map/ppermute | solution.py:330
  71.0 5.0 %collective-permute-start.5 = (bf16[3,6,4,512]{3,2,1,0:T(4,128)(2,1)S(1)}, bf16[3,6,4,512]{3,2,1,0:T(4,128)(2,1)S(1)}, u32[]{:S(2)}, u32[]{:S(2)}) collective-permute-start(bf16[3,6,4,512]{3,2,1,0:T(4,128)(2,1)S(1)} %get-tuple-element.21), channel_id=1, source_target_pairs={{0,511},{1,480},{2,481},{3,482},{4,483},{5,484},{6,485},{7,486},{8... | collective-permute-start | bytes 221192 | tf_op jit(solution)/shard_map/ppermute | solution.py:331
  76.1 4.6 %collective-permute-start.6 = (bf16[3,6,4,512]{3,2,1,0:T(4,128)(2,1)S(1)}, bf16[3,6,4,512]{3,2,1,0:T(4,128)(2,1)S(1)}, u32[]{:S(2)}, u32[]{:S(2)}) collective-permute-start(bf16[3,6,4,512]{3,2,1,0:T(4,128)(2,1)S(1)} %get-tuple-element.22), channel_id=1, source_target_pairs={{0,31},{1,0},{2,1},{3,2},{4,3},{5,4},{6,5},{7,6},{8,7},{9,8},{10,9... | collective-permute-start | bytes 221192 | tf_op jit(solution)/shard_map/ppermute | solution.py:332
  80.7 0.0 all-gather.6.cloned.1.call-done
  80.7 2.4 %stage.1 = (bf16[16,2,16,512]{3,2,1,0:T(8,128)(2,1)S(1)}, bf16[16,2,64,512]{3,2,1,0:T(8,128)(2,1)S(1)}, bf16[16,2,64,512]{3,2,1,0:T(8,128)(2,1)S(1)}) custom-call(bf16[16,2,144,512]{3,2,1,0:T(8,128)(2,1)} %bitcast.20), custom_call_target="tpu_custom_call" | custom-call | bytes 9437184 | tf_op jit(solution)/shard_map/stage/pallas_call | solution.py:281
  83.2 0.0 collective-permute-done.4.m2
  83.2 0.0 collective-permute-done.5.m3
  83.2 0.0 collective-permute-done.6.m1
  83.2 2.8 %tokens.1 = bf16[6,12,4,512]{3,2,1,0:T(4,128)(2,1)} custom-call(bf16[3,6,4,512]{3,2,1,0:T(4,128)(2,1)S(1)} %collective-permute-done.4.m2, bf16[3,6,4,512]{3,2,1,0:T(4,128)(2,1)S(1)} %collective-permute-done.5.m3, bf16[3,6,4,512]{3,2,1,0:T(4,128)(2,1)S(1)} %collective-permute-done.6.m1, bf16[3,6,4,512]{3,2,1,0:T(4,128)(2,1)S(1)} %get-tuple-element.23.m0, ...), custom_call_target="tpu_custom_call" | custom-call | tf_op jit(solution)/shard_map/tokens/pallas_call | solution.py:296
  (6 shorter events, 0.0 us)
Async XLA Ops:
  6.5 74.2 %all-gather.6.cloned.1.call-start = ((), (), s32[]{:S(2)}) async-start(), calls=%async_computation | async-start | bytes 5013504 | tf_op jit(solution)/shard_map/all_gather | solution.py:312
  43.2 15.5 %collective-permute-start.3 = (bf16[8,16,1536]{2,1,0:T(8,128)(2,1)S(1)}, bf16[8,16,1536]{2,1,0:T(8,128)(2,1)S(1)}, u32[]{:S(2)}, u32[]{:S(2)}) collective-permute-start(bf16[8,16,1536]{2,1,0:T(8,128)(2,1)S(1)} %dynamic-slice_bitcast_fusion), channel_id=1, source_target_pairs={{0,272},{272,0},{1,273},{273,1},{2,274},{274,2},{3,275},{275,3},{4... | collective-permute-start | bytes 1179656 | tf_op jit(solution)/shard_map/ppermute | solution.py:325
  49.5 12.7 %collective-permute-start = (bf16[3,6,4,512]{3,2,1,0:T(4,128)(2,1)S(1)}, bf16[3,6,4,512]{3,2,1,0:T(4,128)(2,1)S(1)}, u32[]{:S(2)}, u32[]{:S(2)}) collective-permute-start(bf16[3,6,4,512]{3,2,1,0:T(4,128)(2,1)S(1)} %get-tuple-element.30), channel_id=1, source_target_pairs={{0,32},{1,33},{2,34},{3,35},{4,36},{5,37},{6,38},{7,39},{8,40},{9,... | collective-permute-start | bytes 221192 | tf_op jit(solution)/shard_map/ppermute | solution.py:318
  52.6 9.6 %collective-permute-start.1 = (bf16[3,6,4,512]{3,2,1,0:T(4,128)(2,1)S(1)}, bf16[3,6,4,512]{3,2,1,0:T(4,128)(2,1)S(1)}, u32[]{:S(2)}, u32[]{:S(2)}) collective-permute-start(bf16[3,6,4,512]{3,2,1,0:T(4,128)(2,1)S(1)} %get-tuple-element.29), channel_id=1, source_target_pairs={{0,1},{1,2},{2,3},{3,4},{4,5},{5,6},{6,7},{7,8},{8,9},{9,10},{10,1... | collective-permute-start | bytes 221192 | tf_op jit(solution)/shard_map/ppermute | solution.py:319
  54.6 8.1 %collective-permute-start.2 = (bf16[3,6,4,512]{3,2,1,0:T(4,128)(2,1)S(1)}, bf16[3,6,4,512]{3,2,1,0:T(4,128)(2,1)S(1)}, u32[]{:S(2)}, u32[]{:S(2)}) collective-permute-start(bf16[3,6,4,512]{3,2,1,0:T(4,128)(2,1)S(1)} %get-tuple-element.28), channel_id=1, source_target_pairs={{0,33},{1,34},{2,35},{3,36},{4,37},{5,38},{6,39},{7,40},{8,41},{9,... | collective-permute-start | bytes 221192 | tf_op jit(solution)/shard_map/ppermute | solution.py:320
  56.5 6.1 %copy-start.1 = (bf16[288,288]{1,0:T(8,128)(2,1)S(1)}, bf16[288,288]{1,0:T(8,128)(2,1)}, u32[]{:S(2)}) copy-start(bf16[288,288]{1,0:T(8,128)(2,1)} %constant.31.clone.hot_ref) | copy-start | bytes 497668
  56.5 6.1 %copy-start.2 = (bf16[2,288,128]{2,1,0:T(8,128)(2,1)S(1)}, bf16[2,288,128]{2,1,0:T(8,128)(2,1)}, u32[]{:S(2)}) copy-start(bf16[2,288,128]{2,1,0:T(8,128)(2,1)} %constant.32.clone.tags_ref) | copy-start | bytes 442372
  66.9 16.3 %copy-start = (bf16[4,6,12,512]{3,0,2,1:T(4,128)(2,1)S(1)}, bf16[4,6,12,512]{3,0,2,1:T(4,128)(2,1)}, u32[]{:S(2)}) copy-start(bf16[4,6,12,512]{3,0,2,1:T(4,128)(2,1)} %param.10) | copy-start | bytes 884740
  66.9 16.3 %copy-start.3 = (f32[512]{0:T(512)S(1)}, f32[512]{0:T(512)}, u32[]{:S(2)}) copy-start(f32[512]{0:T(512)} %param.14) | copy-start | bytes 6148
  66.9 16.3 %copy-start.4 = (f32[512]{0:T(512)S(1)}, f32[512]{0:T(512)}, u32[]{:S(2)}) copy-start(f32[512]{0:T(512)} %param.17) | copy-start | bytes 6148
  66.9 16.3 %collective-permute-start.4 = (bf16[3,6,4,512]{3,2,1,0:T(4,128)(2,1)S(1)}, bf16[3,6,4,512]{3,2,1,0:T(4,128)(2,1)S(1)}, u32[]{:S(2)}, u32[]{:S(2)}) collective-permute-start(bf16[3,6,4,512]{3,2,1,0:T(4,128)(2,1)S(1)} %get-tuple-element.20), channel_id=1, source_target_pairs={{0,480},{1,481},{2,482},{3,483},{4,484},{5,485},{6,486},{7,487},{8... | collective-permute-start | bytes 221192 | tf_op jit(solution)/shard_map/ppermute | solution.py:330
  71.0 12.2 %collective-permute-start.5 = (bf16[3,6,4,512]{3,2,1,0:T(4,128)(2,1)S(1)}, bf16[3,6,4,512]{3,2,1,0:T(4,128)(2,1)S(1)}, u32[]{:S(2)}, u32[]{:S(2)}) collective-permute-start(bf16[3,6,4,512]{3,2,1,0:T(4,128)(2,1)S(1)} %get-tuple-element.21), channel_id=1, source_target_pairs={{0,511},{1,480},{2,481},{3,482},{4,483},{5,484},{6,485},{7,486},{8... | collective-permute-start | bytes 221192 | tf_op jit(solution)/shard_map/ppermute | solution.py:331
  76.1 7.1 %collective-permute-start.6 = (bf16[3,6,4,512]{3,2,1,0:T(4,128)(2,1)S(1)}, bf16[3,6,4,512]{3,2,1,0:T(4,128)(2,1)S(1)}, u32[]{:S(2)}, u32[]{:S(2)}) collective-permute-start(bf16[3,6,4,512]{3,2,1,0:T(4,128)(2,1)S(1)} %get-tuple-element.22), channel_id=1, source_target_pairs={{0,31},{1,0},{2,1},{3,2},{4,3},{5,4},{6,5},{7,6},{8,7},{9,8},{10,9... | collective-permute-start | bytes 221192 | tf_op jit(solution)/shard_map/ppermute | solution.py:332
Sparse Core Ops, SparseCore 0:
  14.2 53.3 all-gather.5

commit v11 on v10

--- a/solution.py
+++ b/solution.py
@@ -127,7 +127,7 @@
 
 
 def attention_kernel(
-    spot_ref, r1, r2, r0, r3, mine_ref, other_ref, hot_ref, tags_ref, bias_ref, o0, o1, o2, o3
+    spot_ref, r0, r2, r1, r3, mine_ref, other_ref, hot_ref, tags_ref, bias_ref, o0, o1, o2, o3
 ):
     hot = hot_ref[...]
     rows = stacked([r[...] for r in (r0, r1, r2, r3)]).astype(BF16)
@@ -315,9 +315,9 @@
     cells = latent.transpose(1, 2, 0, 3)
     cells_after, bias, mine = lax.optimization_barrier((cells, position_bias, mine))
     rolled = [
+        lax.ppermute(corner(cells_after, 1, 1), AXES, shifted(1, 1)),
+        lax.ppermute(corner(cells_after, 0, 1), AXES, shifted(0, 1)),
         lax.ppermute(corner(cells_after, 1, 0), AXES, shifted(1, 0)),
-        lax.ppermute(corner(cells_after, 0, 1), AXES, shifted(0, 1)),
-        lax.ppermute(corner(cells_after, 1, 1), AXES, shifted(1, 1)),
         corner(cells_after, 0, 0),
     ]
     core = lax.axis_index("c")

time: 93.3 us -> 92.9 us (level)
    ppermute x1, starting transfers between devices: 5.05 us -> 2.92 us  [shards(): lax.ppermute(attended[0], AXES, shifted(-1, -1))]
    ppermute x1, starting transfers between devices: 4.62 us -> 6.08 us  [shards(): lax.ppermute(attended[2], AXES, shifted(0, -1))]
  transfers between devices with their start and end apart: 8 -> 8, of which waited for: 1 -> 0; matrix products, arithmetic and copies ran while one was open for 1% -> 1% of each run, Pallas kernels for 9% -> 9%
where the time goes in v11:
time: 92.9 us; the launch traced here: 92.5 us
  blocking collectives  39.6 us (43%)
  starting transfers between devices  25.5 us (27%)
  between operations  13.6 us (15%)
  Pallas kernels  12.4 us (13%)
  local copies, waits for them, and re-layouts  1.17 us (1%)
    all_gather x1, blocking collectives, shards(): mine = lax.all_gather(qkv_weight, ('z', 'c'), axis=0, tiled=False)  29.1 us
    all_gather x1, blocking collectives, shards(): lax.all_gather(own, AXES, axis=0, tiled=False, axis_index_groups=mirrored...  6.6 us
    ppermute x1, starting transfers between devices, shards(): lax.ppermute(attended[2], AXES, shifted(0, -1))  6.08 us
    ppermute x1, starting transfers between devices, shards(): lax.ppermute(sent, AXES, mirrored())  5.15 us
    ppermute x1, starting transfers between devices, shards(): lax.ppermute(attended[1], AXES, shifted(-1, 0))  4.43 us
    pallas_call x1, Pallas kernels, attention(): pl.pallas_call(attention_kernel, in_specs=[scalars()] + [held()] * (len(q...  4.2 us
    all_gather x1, blocking collectives, shards(): lax.all_gather(lax.ppermute(sent, AXES, mirrored()), 'c', axis=0, tiled=F...  3.83 us
    ppermute x1, starting transfers between devices, shards(): lax.ppermute(corner(cells_after, 1, 0), AXES, shifted(1, 0))  3.11 us
  transfers between devices with their start and end apart: 8, of which 0 were waited for; matrix products, arithmetic and copies ran while one was open for 1% of the time, Pallas kernels for 9%

profile of v11, /device:TPU:1, one launch (start us, length us, event | category | flops | bytes accessed | tf_op | source)
XLA Modules:
  0.0 92.5 jit_solution(15688874275197590266)
XLA Ops:
  6.5 0.0 all-gather.6.cloned.1.call-start
  6.5 0.9 pack.1
  7.4 6.6 %all-gather = bf16[288,512]{1,0:T(8,128)(2,1)} all-gather(bf16[144,512]{1,0:T(8,128)(2,1)S(1)} %pack.1), channel_id=2, replica_groups={{0,272},{1,273},{2,274},{3,275},{4,276},{5,277},{6,278},{7,279},{8,280}..., dimensions={0}, use_global_device_ids=true | all-gather | bytes 442368 | tf_op jit(solution)/shard_map/all_gather | solution.py:311
  14.0 0.0 all-gather.6.cloned.1.call-update
  14.1 29.1 %all-gather.1 = bf16[256,1536]{1,0:T(8,128)(2,1)S(1)} all-gather(bf16[16,1536]{1,0:T(8,128)(2,1)} %param.11), channel_id=3, replica_groups=mesh['xl'=2,'y'=8,'xh'=2,'z'=8,'c'=2] {'z','c'}, dimensions={0}, use_global_device_ids=true | all-gather | bytes 835584 | tf_op jit(solution)/shard_map/all_gather | solution.py:314
  43.2 5.2 %collective-permute-start.3 = (bf16[8,16,1536]{2,1,0:T(8,128)(2,1)S(1)}, bf16[8,16,1536]{2,1,0:T(8,128)(2,1)S(1)}, u32[]{:S(2)}, u32[]{:S(2)}) collective-permute-start(bf16[8,16,1536]{2,1,0:T(8,128)(2,1)S(1)} %dynamic-slice_bitcast_fusion), channel_id=1, source_target_pairs={{0,272},{272,0},{1,273},{273,1},{2,274},{274,2},{3,275},{275,3},{4... | collective-permute-start | bytes 1179656 | tf_op jit(solution)/shard_map/ppermute | solution.py:325
  48.4 1.1 %fusion = (bf16[3,6,4,512]{3,2,1,0:T(4,128)(2,1)S(1)}, bf16[3,6,4,512]{3,2,1,0:T(4,128)(2,1)S(1)}, bf16[3,6,4,512]{3,2,1,0:T(4,128)(2,1)S(1)}, bf16[3,6,4,512]{3,2,1,0:T(4,128)(2,1)S(1)}) fusion(bf16[6,12,4,512]{3,2,1,0:T(4,128)(2,1)} %bitcast.16), kind=kLoop, calls=%fused_computation.2 | loop fusion | bytes 589824 | tf_op jit(solution)/shard_map/slice | solution.py:107
  49.5 1.9 %collective-permute-start = (bf16[3,6,4,512]{3,2,1,0:T(4,128)(2,1)S(1)}, bf16[3,6,4,512]{3,2,1,0:T(4,128)(2,1)S(1)}, u32[]{:S(2)}, u32[]{:S(2)}) collective-permute-start(bf16[3,6,4,512]{3,2,1,0:T(4,128)(2,1)S(1)} %get-tuple-element.30), channel_id=1, source_target_pairs={{0,33},{1,34},{2,35},{3,36},{4,37},{5,38},{6,39},{7,40},{8,41},{9,... | collective-permute-start | bytes 221192 | tf_op jit(solution)/shard_map/ppermute | solution.py:318
  51.5 1.9 %collective-permute-start.1 = (bf16[3,6,4,512]{3,2,1,0:T(4,128)(2,1)S(1)}, bf16[3,6,4,512]{3,2,1,0:T(4,128)(2,1)S(1)}, u32[]{:S(2)}, u32[]{:S(2)}) collective-permute-start(bf16[3,6,4,512]{3,2,1,0:T(4,128)(2,1)S(1)} %get-tuple-element.29), channel_id=1, source_target_pairs={{0,1},{1,2},{2,3},{3,4},{4,5},{5,6},{6,7},{7,8},{8,9},{9,10},{10,1... | collective-permute-start | bytes 221192 | tf_op jit(solution)/shard_map/ppermute | solution.py:319
  53.4 3.1 %collective-permute-start.2 = (bf16[3,6,4,512]{3,2,1,0:T(4,128)(2,1)S(1)}, bf16[3,6,4,512]{3,2,1,0:T(4,128)(2,1)S(1)}, u32[]{:S(2)}, u32[]{:S(2)}) collective-permute-start(bf16[3,6,4,512]{3,2,1,0:T(4,128)(2,1)S(1)} %get-tuple-element.28), channel_id=1, source_target_pairs={{0,32},{1,33},{2,34},{3,35},{4,36},{5,37},{6,38},{7,39},{8,40},{9,... | collective-permute-start | bytes 221192 | tf_op jit(solution)/shard_map/ppermute | solution.py:320
  56.5 0.0 copy-start.1
  56.5 0.0 copy-start.2
  56.5 2.1 %bias.1.bias_ref = bf16[16,288,288]{2,1,0:T(8,128)(2,1)S(1)} custom-call(bf16[16,288,288]{2,1,0:T(8,128)(2,1)} %bias_hbm), custom_call_target="tpu_custom_call" | custom-call | bytes 5308416 | tf_op jit(solution)/shard_map/bias/pallas_call | solution.py:255
  58.6 0.1 pad_add_fusion.spot_ref
  58.7 0.0 collective-permute-done.3
  58.7 3.8 %all-gather.2 = bf16[16,16,1536]{2,1,0:T(8,128)(2,1)S(1)} all-gather(bf16[8,16,1536]{2,1,0:T(8,128)(2,1)S(1)} %collective-permute-done.3), channel_id=4, replica_groups=mesh['xl'=2,'y'=8,'xh'=2,'z'=8,'c'=2] {'c'}, dimensions={0}, use_global_device_ids=true | all-gather | bytes 1179648 | tf_op jit(solution)/shard_map/all_gather | solution.py:325
  62.6 0.0 collective-permute-done.r0
  62.6 0.0 collective-permute-done.1.r2
  62.6 0.0 collective-permute-done.2.r1
  62.6 4.2 %attention.1 = (bf16[3,6,4,512]{3,2,1,0:T(4,128)(2,1)S(1)}, bf16[3,6,4,512]{3,2,1,0:T(4,128)(2,1)S(1)}, bf16[3,6,4,512]{3,2,1,0:T(4,128)(2,1)S(1)}, bf16[3,6,4,512]{3,2,1,0:T(4,128)(2,1)S(1)}) custom-call(s32[2]{0:T(128)S(1)} %pad_add_fusion.spot_ref, bf16[3,6,4,512]{3,2,1,0:T(4,128)(2,1)S(1)} %collective-permute-done.r0, ...), custom_call_target="tpu_custom_call" | custom-call | tf_op jit(solution)/shard_map/attention/pallas_call | solution.py:269
  66.8 0.0 copy-start
  66.8 0.0 copy-start.3
  66.8 0.0 copy-start.4
  66.8 4.4 %collective-permute-start.4 = (bf16[3,6,4,512]{3,2,1,0:T(4,128)(2,1)S(1)}, bf16[3,6,4,512]{3,2,1,0:T(4,128)(2,1)S(1)}, u32[]{:S(2)}, u32[]{:S(2)}) collective-permute-start(bf16[3,6,4,512]{3,2,1,0:T(4,128)(2,1)S(1)} %get-tuple-element.20), channel_id=1, source_target_pairs={{0,480},{1,481},{2,482},{3,483},{4,484},{5,485},{6,486},{7,487},{8... | collective-permute-start | bytes 221192 | tf_op jit(solution)/shard_map/ppermute | solution.py:330
  71.3 2.9 %collective-permute-start.5 = (bf16[3,6,4,512]{3,2,1,0:T(4,128)(2,1)S(1)}, bf16[3,6,4,512]{3,2,1,0:T(4,128)(2,1)S(1)}, u32[]{:S(2)}, u32[]{:S(2)}) collective-permute-start(bf16[3,6,4,512]{3,2,1,0:T(4,128)(2,1)S(1)} %get-tuple-element.21), channel_id=1, source_target_pairs={{0,511},{1,480},{2,481},{3,482},{4,483},{5,484},{6,485},{7,486},{8... | collective-permute-start | bytes 221192 | tf_op jit(solution)/shard_map/ppermute | solution.py:331
  74.2 6.1 %collective-permute-start.6 = (bf16[3,6,4,512]{3,2,1,0:T(4,128)(2,1)S(1)}, bf16[3,6,4,512]{3,2,1,0:T(4,128)(2,1)S(1)}, u32[]{:S(2)}, u32[]{:S(2)}) collective-permute-start(bf16[3,6,4,512]{3,2,1,0:T(4,128)(2,1)S(1)} %get-tuple-element.22), channel_id=1, source_target_pairs={{0,31},{1,0},{2,1},{3,2},{4,3},{5,4},{6,5},{7,6},{8,7},{9,8},{10,9... | collective-permute-start | bytes 221192 | tf_op jit(solution)/shard_map/ppermute | solution.py:332
  80.3 0.0 all-gather.6.cloned.1.call-done
  80.3 2.4 %stage.1 = (bf16[16,2,16,512]{3,2,1,0:T(8,128)(2,1)S(1)}, bf16[16,2,64,512]{3,2,1,0:T(8,128)(2,1)S(1)}, bf16[16,2,64,512]{3,2,1,0:T(8,128)(2,1)S(1)}) custom-call(bf16[16,2,144,512]{3,2,1,0:T(8,128)(2,1)} %bitcast.20), custom_call_target="tpu_custom_call" | custom-call | bytes 9437184 | tf_op jit(solution)/shard_map/stage/pallas_call | solution.py:281
  82.7 0.0 collective-permute-done.4.m2
  82.8 0.0 collective-permute-done.5.m3
  82.8 0.0 collective-permute-done.6.m1
  82.8 2.8 %tokens.1 = bf16[6,12,4,512]{3,2,1,0:T(4,128)(2,1)} custom-call(bf16[3,6,4,512]{3,2,1,0:T(4,128)(2,1)S(1)} %collective-permute-done.4.m2, bf16[3,6,4,512]{3,2,1,0:T(4,128)(2,1)S(1)} %collective-permute-done.5.m3, bf16[3,6,4,512]{3,2,1,0:T(4,128)(2,1)S(1)} %collective-permute-done.6.m1, bf16[3,6,4,512]{3,2,1,0:T(4,128)(2,1)S(1)} %get-tuple-element.23.m0, ...), custom_call_target="tpu_custom_call" | custom-call | tf_op jit(solution)/shard_map/tokens/pallas_call | solution.py:296
  (6 shorter events, 0.0 us)
Async XLA Ops:
  6.5 73.8 %all-gather.6.cloned.1.call-start = ((), (), s32[]{:S(2)}) async-start(), calls=%async_computation | async-start | bytes 5013504 | tf_op jit(solution)/shard_map/all_gather | solution.py:312
  43.2 15.5 %collective-permute-start.3 = (bf16[8,16,1536]{2,1,0:T(8,128)(2,1)S(1)}, bf16[8,16,1536]{2,1,0:T(8,128)(2,1)S(1)}, u32[]{:S(2)}, u32[]{:S(2)}) collective-permute-start(bf16[8,16,1536]{2,1,0:T(8,128)(2,1)S(1)} %dynamic-slice_bitcast_fusion), channel_id=1, source_target_pairs={{0,272},{272,0},{1,273},{273,1},{2,274},{274,2},{3,275},{275,3},{4... | collective-permute-start | bytes 1179656 | tf_op jit(solution)/shard_map/ppermute | solution.py:325
  49.5 13.0 %collective-permute-start = (bf16[3,6,4,512]{3,2,1,0:T(4,128)(2,1)S(1)}, bf16[3,6,4,512]{3,2,1,0:T(4,128)(2,1)S(1)}, u32[]{:S(2)}, u32[]{:S(2)}) collective-permute-start(bf16[3,6,4,512]{3,2,1,0:T(4,128)(2,1)S(1)} %get-tuple-element.30), channel_id=1, source_target_pairs={{0,33},{1,34},{2,35},{3,36},{4,37},{5,38},{6,39},{7,40},{8,41},{9,... | collective-permute-start | bytes 221192 | tf_op jit(solution)/shard_map/ppermute | solution.py:318
  51.5 11.1 %collective-permute-start.1 = (bf16[3,6,4,512]{3,2,1,0:T(4,128)(2,1)S(1)}, bf16[3,6,4,512]{3,2,1,0:T(4,128)(2,1)S(1)}, u32[]{:S(2)}, u32[]{:S(2)}) collective-permute-start(bf16[3,6,4,512]{3,2,1,0:T(4,128)(2,1)S(1)} %get-tuple-element.29), channel_id=1, source_target_pairs={{0,1},{1,2},{2,3},{3,4},{4,5},{5,6},{6,7},{7,8},{8,9},{9,10},{10,1... | collective-permute-start | bytes 221192 | tf_op jit(solution)/shard_map/ppermute | solution.py:319
  53.4 9.2 %collective-permute-start.2 = (bf16[3,6,4,512]{3,2,1,0:T(4,128)(2,1)S(1)}, bf16[3,6,4,512]{3,2,1,0:T(4,128)(2,1)S(1)}, u32[]{:S(2)}, u32[]{:S(2)}) collective-permute-start(bf16[3,6,4,512]{3,2,1,0:T(4,128)(2,1)S(1)} %get-tuple-element.28), channel_id=1, source_target_pairs={{0,32},{1,33},{2,34},{3,35},{4,36},{5,37},{6,38},{7,39},{8,40},{9,... | collective-permute-start | bytes 221192 | tf_op jit(solution)/shard_map/ppermute | solution.py:320
  56.5 6.1 %copy-start.1 = (bf16[288,288]{1,0:T(8,128)(2,1)S(1)}, bf16[288,288]{1,0:T(8,128)(2,1)}, u32[]{:S(2)}) copy-start(bf16[288,288]{1,0:T(8,128)(2,1)} %constant.31.clone.hot_ref) | copy-start | bytes 497668
  56.5 6.1 %copy-start.2 = (bf16[2,288,128]{2,1,0:T(8,128)(2,1)S(1)}, bf16[2,288,128]{2,1,0:T(8,128)(2,1)}, u32[]{:S(2)}) copy-start(bf16[2,288,128]{2,1,0:T(8,128)(2,1)} %constant.32.clone.tags_ref) | copy-start | bytes 442372
  66.8 16.0 %copy-start = (bf16[4,6,12,512]{3,0,2,1:T(4,128)(2,1)S(1)}, bf16[4,6,12,512]{3,0,2,1:T(4,128)(2,1)}, u32[]{:S(2)}) copy-start(bf16[4,6,12,512]{3,0,2,1:T(4,128)(2,1)} %param.10) | copy-start | bytes 884740
  66.8 16.0 %copy-start.3 = (f32[512]{0:T(512)S(1)}, f32[512]{0:T(512)}, u32[]{:S(2)}) copy-start(f32[512]{0:T(512)} %param.14) | copy-start | bytes 6148
  66.8 16.0 %copy-start.4 = (f32[512]{0:T(512)S(1)}, f32[512]{0:T(512)}, u32[]{:S(2)}) copy-start(f32[512]{0:T(512)} %param.17) | copy-start | bytes 6148
  66.8 15.9 %collective-permute-start.4 = (bf16[3,6,4,512]{3,2,1,0:T(4,128)(2,1)S(1)}, bf16[3,6,4,512]{3,2,1,0:T(4,128)(2,1)S(1)}, u32[]{:S(2)}, u32[]{:S(2)}) collective-permute-start(bf16[3,6,4,512]{3,2,1,0:T(4,128)(2,1)S(1)} %get-tuple-element.20), channel_id=1, source_target_pairs={{0,480},{1,481},{2,482},{3,483},{4,484},{5,485},{6,486},{7,487},{8... | collective-permute-start | bytes 221192 | tf_op jit(solution)/shard_map/ppermute | solution.py:330
  71.3 11.5 %collective-permute-start.5 = (bf16[3,6,4,512]{3,2,1,0:T(4,128)(2,1)S(1)}, bf16[3,6,4,512]{3,2,1,0:T(4,128)(2,1)S(1)}, u32[]{:S(2)}, u32[]{:S(2)}) collective-permute-start(bf16[3,6,4,512]{3,2,1,0:T(4,128)(2,1)S(1)} %get-tuple-element.21), channel_id=1, source_target_pairs={{0,511},{1,480},{2,481},{3,482},{4,483},{5,484},{6,485},{7,486},{8... | collective-permute-start | bytes 221192 | tf_op jit(solution)/shard_map/ppermute | solution.py:331
  74.2 8.6 %collective-permute-start.6 = (bf16[3,6,4,512]{3,2,1,0:T(4,128)(2,1)S(1)}, bf16[3,6,4,512]{3,2,1,0:T(4,128)(2,1)S(1)}, u32[]{:S(2)}, u32[]{:S(2)}) collective-permute-start(bf16[3,6,4,512]{3,2,1,0:T(4,128)(2,1)S(1)} %get-tuple-element.22), channel_id=1, source_target_pairs={{0,31},{1,0},{2,1},{3,2},{4,3},{5,4},{6,5},{7,6},{8,7},{9,8},{10,9... | collective-permute-start | bytes 221192 | tf_op jit(solution)/shard_map/ppermute | solution.py:332
Sparse Core Ops, SparseCore 0:
  14.2 53.6 all-gather.5

commit v12 on v11

--- a/solution.py
+++ b/solution.py
@@ -181,7 +181,7 @@
 
 
 def token_kernel(
-    m2, m3, m1, m0, cells_ref, wp, wu, wd, attn_gain_ref, mlp_gain_ref, out_hbm,
+    m3, m1, m2, m0, cells_ref, wp, wu, wd, attn_gain_ref, mlp_gain_ref, out_hbm,
     out_ref, sems,
 ):
     attended = stacked([m[...] for m in (m0, m1, m2, m3)]).astype(BF16)
@@ -327,9 +327,9 @@
     spot = jnp.stack([lax.axis_index("xh"), (lax.axis_index(LAT) == 0).astype(jnp.int32)])
     attended = attention(spot, rolled, mine, theirs, held_bias(bias))
     restored = [
-        lax.ppermute(attended[1], AXES, shifted(-1, 0)),
         lax.ppermute(attended[0], AXES, shifted(-1, -1)),
         lax.ppermute(attended[2], AXES, shifted(0, -1)),
+        lax.ppermute(attended[1], AXES, shifted(-1, 0)),
         attended[3],
     ]
     return tokens(restored, cells, staged(gathered), attn_gain, mlp_gain).transpose(2, 0, 1, 3)

time: 92.9 us -> 93.7 us (level)
    ppermute x1, starting transfers between devices: 2.92 us -> 5.42 us  [shards(): lax.ppermute(attended[0], AXES, shifted(-1, -1))]
    ppermute x1, starting transfers between devices: 4.43 us -> 2.8 us  [shards(): lax.ppermute(attended[1], AXES, shifted(-1, 0))]
where the time goes in v12:
time: 93.7 us; the launch traced here: 92.8 us
  blocking collectives  39.6 us (42%)
  starting transfers between devices  25.8 us (28%)
  between operations  13.6 us (15%)
  Pallas kernels  12.4 us (13%)
  local copies, waits for them, and re-layouts  1.17 us (1%)
    all_gather x1, blocking collectives, shards(): mine = lax.all_gather(qkv_weight, ('z', 'c'), axis=0, tiled=False)  29.1 us
    all_gather x1, blocking collectives, shards(): lax.all_gather(own, AXES, axis=0, tiled=False, axis_index_groups=mirrored...  6.6 us
    ppermute x1, starting transfers between devices, shards(): lax.ppermute(attended[2], AXES, shifted(0, -1))  5.49 us
    ppermute x1, starting transfers between devices, shards(): lax.ppermute(attended[0], AXES, shifted(-1, -1))  5.42 us
    ppermute x1, starting transfers between devices, shards(): lax.ppermute(sent, AXES, mirrored())  5.15 us
    pallas_call x1, Pallas kernels, attention(): pl.pallas_call(attention_kernel, in_specs=[scalars()] + [held()] * (len(q...  4.2 us
    all_gather x1, blocking collectives, shards(): lax.all_gather(lax.ppermute(sent, AXES, mirrored()), 'c', axis=0, tiled=F...  3.83 us
    ppermute x1, starting transfers between devices, shards(): lax.ppermute(corner(cells_after, 1, 0), AXES, shifted(1, 0))  3.11 us
  transfers between devices with their start and end apart: 8, of which 0 were waited for; matrix products, arithmetic and copies ran while one was open for 1% of the time, Pallas kernels for 9%

profile of v12, /device:TPU:1, one launch (start us, length us, event | category | flops | bytes accessed | tf_op | source)
XLA Modules:
  0.0 92.8 jit_solution(13169065356247296635)
XLA Ops:
  6.5 0.0 all-gather.6.cloned.1.call-start
  6.5 0.9 pack.1
  7.4 6.6 %all-gather = bf16[288,512]{1,0:T(8,128)(2,1)} all-gather(bf16[144,512]{1,0:T(8,128)(2,1)S(1)} %pack.1), channel_id=2, replica_groups={{0,272},{1,273},{2,274},{3,275},{4,276},{5,277},{6,278},{7,279},{8,280}..., dimensions={0}, use_global_device_ids=true | all-gather | bytes 442368 | tf_op jit(solution)/shard_map/all_gather | solution.py:311
  14.0 0.0 all-gather.6.cloned.1.call-update
  14.1 29.1 %all-gather.1 = bf16[256,1536]{1,0:T(8,128)(2,1)S(1)} all-gather(bf16[16,1536]{1,0:T(8,128)(2,1)} %param.11), channel_id=3, replica_groups=mesh['xl'=2,'y'=8,'xh'=2,'z'=8,'c'=2] {'z','c'}, dimensions={0}, use_global_device_ids=true | all-gather | bytes 835584 | tf_op jit(solution)/shard_map/all_gather | solution.py:314
  43.2 5.2 %collective-permute-start.3 = (bf16[8,16,1536]{2,1,0:T(8,128)(2,1)S(1)}, bf16[8,16,1536]{2,1,0:T(8,128)(2,1)S(1)}, u32[]{:S(2)}, u32[]{:S(2)}) collective-permute-start(bf16[8,16,1536]{2,1,0:T(8,128)(2,1)S(1)} %dynamic-slice_bitcast_fusion), channel_id=1, source_target_pairs={{0,272},{272,0},{1,273},{273,1},{2,274},{274,2},{3,275},{275,3},{4... | collective-permute-start | bytes 1179656 | tf_op jit(solution)/shard_map/ppermute | solution.py:325
  48.4 1.1 %fusion = (bf16[3,6,4,512]{3,2,1,0:T(4,128)(2,1)S(1)}, bf16[3,6,4,512]{3,2,1,0:T(4,128)(2,1)S(1)}, bf16[3,6,4,512]{3,2,1,0:T(4,128)(2,1)S(1)}, bf16[3,6,4,512]{3,2,1,0:T(4,128)(2,1)S(1)}) fusion(bf16[6,12,4,512]{3,2,1,0:T(4,128)(2,1)} %bitcast.16), kind=kLoop, calls=%fused_computation.2 | loop fusion | bytes 589824 | tf_op jit(solution)/shard_map/slice | solution.py:107
  49.5 1.9 %collective-permute-start = (bf16[3,6,4,512]{3,2,1,0:T(4,128)(2,1)S(1)}, bf16[3,6,4,512]{3,2,1,0:T(4,128)(2,1)S(1)}, u32[]{:S(2)}, u32[]{:S(2)}) collective-permute-start(bf16[3,6,4,512]{3,2,1,0:T(4,128)(2,1)S(1)} %get-tuple-element.30), channel_id=1, source_target_pairs={{0,33},{1,34},{2,35},{3,36},{4,37},{5,38},{6,39},{7,40},{8,41},{9,... | collective-permute-start | bytes 221192 | tf_op jit(solution)/shard_map/ppermute | solution.py:318
  51.5 1.9 %collective-permute-start.1 = (bf16[3,6,4,512]{3,2,1,0:T(4,128)(2,1)S(1)}, bf16[3,6,4,512]{3,2,1,0:T(4,128)(2,1)S(1)}, u32[]{:S(2)}, u32[]{:S(2)}) collective-permute-start(bf16[3,6,4,512]{3,2,1,0:T(4,128)(2,1)S(1)} %get-tuple-element.29), channel_id=1, source_target_pairs={{0,1},{1,2},{2,3},{3,4},{4,5},{5,6},{6,7},{7,8},{8,9},{9,10},{10,1... | collective-permute-start | bytes 221192 | tf_op jit(solution)/shard_map/ppermute | solution.py:319
  53.4 3.1 %collective-permute-start.2 = (bf16[3,6,4,512]{3,2,1,0:T(4,128)(2,1)S(1)}, bf16[3,6,4,512]{3,2,1,0:T(4,128)(2,1)S(1)}, u32[]{:S(2)}, u32[]{:S(2)}) collective-permute-start(bf16[3,6,4,512]{3,2,1,0:T(4,128)(2,1)S(1)} %get-tuple-element.28), channel_id=1, source_target_pairs={{0,32},{1,33},{2,34},{3,35},{4,36},{5,37},{6,38},{7,39},{8,40},{9,... | collective-permute-start | bytes 221192 | tf_op jit(solution)/shard_map/ppermute | solution.py:320
  56.5 0.0 copy-start.1
  56.5 0.0 copy-start.2
  56.5 2.1 %bias.1.bias_ref = bf16[16,288,288]{2,1,0:T(8,128)(2,1)S(1)} custom-call(bf16[16,288,288]{2,1,0:T(8,128)(2,1)} %bias_hbm), custom_call_target="tpu_custom_call" | custom-call | bytes 5308416 | tf_op jit(solution)/shard_map/bias/pallas_call | solution.py:255
  58.6 0.1 pad_add_fusion.spot_ref
  58.7 0.0 collective-permute-done.3
  58.7 3.8 %all-gather.2 = bf16[16,16,1536]{2,1,0:T(8,128)(2,1)S(1)} all-gather(bf16[8,16,1536]{2,1,0:T(8,128)(2,1)S(1)} %collective-permute-done.3), channel_id=4, replica_groups=mesh['xl'=2,'y'=8,'xh'=2,'z'=8,'c'=2] {'c'}, dimensions={0}, use_global_device_ids=true | all-gather | bytes 1179648 | tf_op jit(solution)/shard_map/all_gather | solution.py:325
  62.6 0.0 collective-permute-done.r0
  62.6 0.0 collective-permute-done.1.r2
  62.6 0.0 collective-permute-done.2.r1
  62.6 4.2 %attention.1 = (bf16[3,6,4,512]{3,2,1,0:T(4,128)(2,1)S(1)}, bf16[3,6,4,512]{3,2,1,0:T(4,128)(2,1)S(1)}, bf16[3,6,4,512]{3,2,1,0:T(4,128)(2,1)S(1)}, bf16[3,6,4,512]{3,2,1,0:T(4,128)(2,1)S(1)}) custom-call(s32[2]{0:T(128)S(1)} %pad_add_fusion.spot_ref, bf16[3,6,4,512]{3,2,1,0:T(4,128)(2,1)S(1)} %collective-permute-done.r0, ...), custom_call_target="tpu_custom_call" | custom-call | tf_op jit(solution)/shard_map/attention/pallas_call | solution.py:269
  66.8 0.0 copy-start
  66.8 0.0 copy-start.3
  66.8 0.0 copy-start.4
  66.8 5.4 %collective-permute-start.4 = (bf16[3,6,4,512]{3,2,1,0:T(4,128)(2,1)S(1)}, bf16[3,6,4,512]{3,2,1,0:T(4,128)(2,1)S(1)}, u32[]{:S(2)}, u32[]{:S(2)}) collective-permute-start(bf16[3,6,4,512]{3,2,1,0:T(4,128)(2,1)S(1)} %get-tuple-element.20), channel_id=1, source_target_pairs={{0,511},{1,480},{2,481},{3,482},{4,483},{5,484},{6,485},{7,486},{8... | collective-permute-start | bytes 221192 | tf_op jit(solution)/shard_map/ppermute | solution.py:330
  72.3 5.5 %collective-permute-start.5 = (bf16[3,6,4,512]{3,2,1,0:T(4,128)(2,1)S(1)}, bf16[3,6,4,512]{3,2,1,0:T(4,128)(2,1)S(1)}, u32[]{:S(2)}, u32[]{:S(2)}) collective-permute-start(bf16[3,6,4,512]{3,2,1,0:T(4,128)(2,1)S(1)} %get-tuple-element.21), channel_id=1, source_target_pairs={{0,31},{1,0},{2,1},{3,2},{4,3},{5,4},{6,5},{7,6},{8,7},{9,8},{10,9... | collective-permute-start | bytes 221192 | tf_op jit(solution)/shard_map/ppermute | solution.py:331
  77.8 2.8 %collective-permute-start.6 = (bf16[3,6,4,512]{3,2,1,0:T(4,128)(2,1)S(1)}, bf16[3,6,4,512]{3,2,1,0:T(4,128)(2,1)S(1)}, u32[]{:S(2)}, u32[]{:S(2)}) collective-permute-start(bf16[3,6,4,512]{3,2,1,0:T(4,128)(2,1)S(1)} %get-tuple-element.22), channel_id=1, source_target_pairs={{0,480},{1,481},{2,482},{3,483},{4,484},{5,485},{6,486},{7,487},{8... | collective-permute-start | bytes 221192 | tf_op jit(solution)/shard_map/ppermute | solution.py:332
  80.6 0.0 all-gather.6.cloned.1.call-done
  80.6 2.4 %stage.1 = (bf16[16,2,16,512]{3,2,1,0:T(8,128)(2,1)S(1)}, bf16[16,2,64,512]{3,2,1,0:T(8,128)(2,1)S(1)}, bf16[16,2,64,512]{3,2,1,0:T(8,128)(2,1)S(1)}) custom-call(bf16[16,2,144,512]{3,2,1,0:T(8,128)(2,1)} %bitcast.20), custom_call_target="tpu_custom_call" | custom-call | bytes 9437184 | tf_op jit(solution)/shard_map/stage/pallas_call | solution.py:281
  83.0 0.0 collective-permute-done.4.m3
  83.0 0.0 collective-permute-done.5.m1
  83.1 0.0 collective-permute-done.6.m2
  83.1 2.8 %tokens.1 = bf16[6,12,4,512]{3,2,1,0:T(4,128)(2,1)} custom-call(bf16[3,6,4,512]{3,2,1,0:T(4,128)(2,1)S(1)} %collective-permute-done.4.m3, bf16[3,6,4,512]{3,2,1,0:T(4,128)(2,1)S(1)} %collective-permute-done.5.m1, bf16[3,6,4,512]{3,2,1,0:T(4,128)(2,1)S(1)} %collective-permute-done.6.m2, bf16[3,6,4,512]{3,2,1,0:T(4,128)(2,1)S(1)} %get-tuple-element.23.m0, ...), custom_call_target="tpu_custom_call" | custom-call | tf_op jit(solution)/shard_map/tokens/pallas_call | solution.py:296
  (6 shorter events, 0.0 us)
Async XLA Ops:
  6.5 74.1 %all-gather.6.cloned.1.call-start = ((), (), s32[]{:S(2)}) async-start(), calls=%async_computation | async-start | bytes 5013504 | tf_op jit(solution)/shard_map/all_gather | solution.py:312
  43.2 15.5 %collective-permute-start.3 = (bf16[8,16,1536]{2,1,0:T(8,128)(2,1)S(1)}, bf16[8,16,1536]{2,1,0:T(8,128)(2,1)S(1)}, u32[]{:S(2)}, u32[]{:S(2)}) collective-permute-start(bf16[8,16,1536]{2,1,0:T(8,128)(2,1)S(1)} %dynamic-slice_bitcast_fusion), channel_id=1, source_target_pairs={{0,272},{272,0},{1,273},{273,1},{2,274},{274,2},{3,275},{275,3},{4... | collective-permute-start | bytes 1179656 | tf_op jit(solution)/shard_map/ppermute | solution.py:325
  49.5 13.0 %collective-permute-start = (bf16[3,6,4,512]{3,2,1,0:T(4,128)(2,1)S(1)}, bf16[3,6,4,512]{3,2,1,0:T(4,128)(2,1)S(1)}, u32[]{:S(2)}, u32[]{:S(2)}) collective-permute-start(bf16[3,6,4,512]{3,2,1,0:T(4,128)(2,1)S(1)} %get-tuple-element.30), channel_id=1, source_target_pairs={{0,33},{1,34},{2,35},{3,36},{4,37},{5,38},{6,39},{7,40},{8,41},{9,... | collective-permute-start | bytes 221192 | tf_op jit(solution)/shard_map/ppermute | solution.py:318
  51.5 11.1 %collective-permute-start.1 = (bf16[3,6,4,512]{3,2,1,0:T(4,128)(2,1)S(1)}, bf16[3,6,4,512]{3,2,1,0:T(4,128)(2,1)S(1)}, u32[]{:S(2)}, u32[]{:S(2)}) collective-permute-start(bf16[3,6,4,512]{3,2,1,0:T(4,128)(2,1)S(1)} %get-tuple-element.29), channel_id=1, source_target_pairs={{0,1},{1,2},{2,3},{3,4},{4,5},{5,6},{6,7},{7,8},{8,9},{9,10},{10,1... | collective-permute-start | bytes 221192 | tf_op jit(solution)/shard_map/ppermute | solution.py:319
  53.4 9.2 %collective-permute-start.2 = (bf16[3,6,4,512]{3,2,1,0:T(4,128)(2,1)S(1)}, bf16[3,6,4,512]{3,2,1,0:T(4,128)(2,1)S(1)}, u32[]{:S(2)}, u32[]{:S(2)}) collective-permute-start(bf16[3,6,4,512]{3,2,1,0:T(4,128)(2,1)S(1)} %get-tuple-element.28), channel_id=1, source_target_pairs={{0,32},{1,33},{2,34},{3,35},{4,36},{5,37},{6,38},{7,39},{8,40},{9,... | collective-permute-start | bytes 221192 | tf_op jit(solution)/shard_map/ppermute | solution.py:320
  56.5 6.1 %copy-start.1 = (bf16[288,288]{1,0:T(8,128)(2,1)S(1)}, bf16[288,288]{1,0:T(8,128)(2,1)}, u32[]{:S(2)}) copy-start(bf16[288,288]{1,0:T(8,128)(2,1)} %constant.31.clone.hot_ref) | copy-start | bytes 497668
  56.5 6.1 %copy-start.2 = (bf16[2,288,128]{2,1,0:T(8,128)(2,1)S(1)}, bf16[2,288,128]{2,1,0:T(8,128)(2,1)}, u32[]{:S(2)}) copy-start(bf16[2,288,128]{2,1,0:T(8,128)(2,1)} %constant.32.clone.tags_ref) | copy-start | bytes 442372
  66.8 16.3 %copy-start = (bf16[4,6,12,512]{3,0,2,1:T(4,128)(2,1)S(1)}, bf16[4,6,12,512]{3,0,2,1:T(4,128)(2,1)}, u32[]{:S(2)}) copy-start(bf16[4,6,12,512]{3,0,2,1:T(4,128)(2,1)} %param.10) | copy-start | bytes 884740
  66.8 16.3 %copy-start.3 = (f32[512]{0:T(512)S(1)}, f32[512]{0:T(512)}, u32[]{:S(2)}) copy-start(f32[512]{0:T(512)} %param.14) | copy-start | bytes 6148
  66.8 16.3 %copy-start.4 = (f32[512]{0:T(512)S(1)}, f32[512]{0:T(512)}, u32[]{:S(2)}) copy-start(f32[512]{0:T(512)} %param.17) | copy-start | bytes 6148
  66.8 16.2 %collective-permute-start.4 = (bf16[3,6,4,512]{3,2,1,0:T(4,128)(2,1)S(1)}, bf16[3,6,4,512]{3,2,1,0:T(4,128)(2,1)S(1)}, u32[]{:S(2)}, u32[]{:S(2)}) collective-permute-start(bf16[3,6,4,512]{3,2,1,0:T(4,128)(2,1)S(1)} %get-tuple-element.20), channel_id=1, source_target_pairs={{0,511},{1,480},{2,481},{3,482},{4,483},{5,484},{6,485},{7,486},{8... | collective-permute-start | bytes 221192 | tf_op jit(solution)/shard_map/ppermute | solution.py:330
  72.3 10.8 %collective-permute-start.5 = (bf16[3,6,4,512]{3,2,1,0:T(4,128)(2,1)S(1)}, bf16[3,6,4,512]{3,2,1,0:T(4,128)(2,1)S(1)}, u32[]{:S(2)}, u32[]{:S(2)}) collective-permute-start(bf16[3,6,4,512]{3,2,1,0:T(4,128)(2,1)S(1)} %get-tuple-element.21), channel_id=1, source_target_pairs={{0,31},{1,0},{2,1},{3,2},{4,3},{5,4},{6,5},{7,6},{8,7},{9,8},{10,9... | collective-permute-start | bytes 221192 | tf_op jit(solution)/shard_map/ppermute | solution.py:331
  77.8 5.3 %collective-permute-start.6 = (bf16[3,6,4,512]{3,2,1,0:T(4,128)(2,1)S(1)}, bf16[3,6,4,512]{3,2,1,0:T(4,128)(2,1)S(1)}, u32[]{:S(2)}, u32[]{:S(2)}) collective-permute-start(bf16[3,6,4,512]{3,2,1,0:T(4,128)(2,1)S(1)} %get-tuple-element.22), channel_id=1, source_target_pairs={{0,480},{1,481},{2,482},{3,483},{4,484},{5,485},{6,486},{7,487},{8... | collective-permute-start | bytes 221192 | tf_op jit(solution)/shard_map/ppermute | solution.py:332
Sparse Core Ops, SparseCore 0:
  14.2 53.6 all-gather.5

commit v13 on v11

--- a/solution.py
+++ b/solution.py
@@ -181,7 +181,7 @@
 
 
 def token_kernel(
-    m2, m3, m1, m0, cells_ref, wp, wu, wd, attn_gain_ref, mlp_gain_ref, out_hbm,
+    m2, m1, m3, m0, cells_ref, wp, wu, wd, attn_gain_ref, mlp_gain_ref, out_hbm,
     out_ref, sems,
 ):
     attended = stacked([m[...] for m in (m0, m1, m2, m3)]).astype(BF16)
@@ -328,8 +328,8 @@
     attended = attention(spot, rolled, mine, theirs, held_bias(bias))
     restored = [
         lax.ppermute(attended[1], AXES, shifted(-1, 0)),
+        lax.ppermute(attended[2], AXES, shifted(0, -1)),
         lax.ppermute(attended[0], AXES, shifted(-1, -1)),
-        lax.ppermute(attended[2], AXES, shifted(0, -1)),
         attended[3],
     ]
     return tokens(restored, cells, staged(gathered), attn_gain, mlp_gain).transpose(2, 0, 1, 3)

time: 92.9 us -> 93.3 us (level)
    ppermute x1, starting transfers between devices: 2.92 us -> 6.16 us  [shards(): lax.ppermute(attended[0], AXES, shifted(-1, -1))]
    ppermute x1, starting transfers between devices: 6.08 us -> 3.3 us  [shards(): lax.ppermute(attended[2], AXES, shifted(0, -1))]
where the time goes in v13:
time: 93.3 us; the launch traced here: 92.9 us
  blocking collectives  39.6 us (42%)
  starting transfers between devices  26 us (28%)
  between operations  13.6 us (15%)
  Pallas kernels  12.4 us (13%)
  local copies, waits for them, and re-layouts  1.17 us (1%)
    all_gather x1, blocking collectives, shards(): mine = lax.all_gather(qkv_weight, ('z', 'c'), axis=0, tiled=False)  29.1 us
    all_gather x1, blocking collectives, shards(): lax.all_gather(own, AXES, axis=0, tiled=False, axis_index_groups=mirrored...  6.6 us
    ppermute x1, starting transfers between devices, shards(): lax.ppermute(attended[0], AXES, shifted(-1, -1))  6.16 us
    ppermute x1, starting transfers between devices, shards(): lax.ppermute(sent, AXES, mirrored())  5.15 us
    ppermute x1, starting transfers between devices, shards(): lax.ppermute(attended[1], AXES, shifted(-1, 0))  4.43 us
    pallas_call x1, Pallas kernels, attention(): pl.pallas_call(attention_kernel, in_specs=[scalars()] + [held()] * (len(q...  4.2 us
    all_gather x1, blocking collectives, shards(): lax.all_gather(lax.ppermute(sent, AXES, mirrored()), 'c', axis=0, tiled=F...  3.83 us
    ppermute x1, starting transfers between devices, shards(): lax.ppermute(attended[2], AXES, shifted(0, -1))  3.3 us
  transfers between devices with their start and end apart: 8, of which 0 were waited for; matrix products, arithmetic and copies ran while one was open for 1% of the time, Pallas kernels for 9%

profile of v13, /device:TPU:1, one launch (start us, length us, event | category | flops | bytes accessed | tf_op | source)
XLA Modules:
  0.0 92.9 jit_solution(11816510298939971300)
XLA Ops:
  6.5 0.0 all-gather.6.cloned.1.call-start
  6.5 0.9 pack.1
  7.4 6.6 %all-gather = bf16[288,512]{1,0:T(8,128)(2,1)} all-gather(bf16[144,512]{1,0:T(8,128)(2,1)S(1)} %pack.1), channel_id=2, replica_groups={{0,272},{1,273},{2,274},{3,275},{4,276},{5,277},{6,278},{7,279},{8,280}..., dimensions={0}, use_global_device_ids=true | all-gather | bytes 442368 | tf_op jit(solution)/shard_map/all_gather | solution.py:311
  14.0 0.0 all-gather.6.cloned.1.call-update
  14.1 29.1 %all-gather.1 = bf16[256,1536]{1,0:T(8,128)(2,1)S(1)} all-gather(bf16[16,1536]{1,0:T(8,128)(2,1)} %param.11), channel_id=3, replica_groups=mesh['xl'=2,'y'=8,'xh'=2,'z'=8,'c'=2] {'z','c'}, dimensions={0}, use_global_device_ids=true | all-gather | bytes 835584 | tf_op jit(solution)/shard_map/all_gather | solution.py:314
  43.2 5.2 %collective-permute-start.3 = (bf16[8,16,1536]{2,1,0:T(8,128)(2,1)S(1)}, bf16[8,16,1536]{2,1,0:T(8,128)(2,1)S(1)}, u32[]{:S(2)}, u32[]{:S(2)}) collective-permute-start(bf16[8,16,1536]{2,1,0:T(8,128)(2,1)S(1)} %dynamic-slice_bitcast_fusion), channel_id=1, source_target_pairs={{0,272},{272,0},{1,273},{273,1},{2,274},{274,2},{3,275},{275,3},{4... | collective-permute-start | bytes 1179656 | tf_op jit(solution)/shard_map/ppermute | solution.py:325
  48.4 1.1 %fusion = (bf16[3,6,4,512]{3,2,1,0:T(4,128)(2,1)S(1)}, bf16[3,6,4,512]{3,2,1,0:T(4,128)(2,1)S(1)}, bf16[3,6,4,512]{3,2,1,0:T(4,128)(2,1)S(1)}, bf16[3,6,4,512]{3,2,1,0:T(4,128)(2,1)S(1)}) fusion(bf16[6,12,4,512]{3,2,1,0:T(4,128)(2,1)} %bitcast.16), kind=kLoop, calls=%fused_computation.2 | loop fusion | bytes 589824 | tf_op jit(solution)/shard_map/slice | solution.py:107
  49.5 1.9 %collective-permute-start = (bf16[3,6,4,512]{3,2,1,0:T(4,128)(2,1)S(1)}, bf16[3,6,4,512]{3,2,1,0:T(4,128)(2,1)S(1)}, u32[]{:S(2)}, u32[]{:S(2)}) collective-permute-start(bf16[3,6,4,512]{3,2,1,0:T(4,128)(2,1)S(1)} %get-tuple-element.30), channel_id=1, source_target_pairs={{0,33},{1,34},{2,35},{3,36},{4,37},{5,38},{6,39},{7,40},{8,41},{9,... | collective-permute-start | bytes 221192 | tf_op jit(solution)/shard_map/ppermute | solution.py:318
  51.5 1.9 %collective-permute-start.1 = (bf16[3,6,4,512]{3,2,1,0:T(4,128)(2,1)S(1)}, bf16[3,6,4,512]{3,2,1,0:T(4,128)(2,1)S(1)}, u32[]{:S(2)}, u32[]{:S(2)}) collective-permute-start(bf16[3,6,4,512]{3,2,1,0:T(4,128)(2,1)S(1)} %get-tuple-element.29), channel_id=1, source_target_pairs={{0,1},{1,2},{2,3},{3,4},{4,5},{5,6},{6,7},{7,8},{8,9},{9,10},{10,1... | collective-permute-start | bytes 221192 | tf_op jit(solution)/shard_map/ppermute | solution.py:319
  53.4 3.1 %collective-permute-start.2 = (bf16[3,6,4,512]{3,2,1,0:T(4,128)(2,1)S(1)}, bf16[3,6,4,512]{3,2,1,0:T(4,128)(2,1)S(1)}, u32[]{:S(2)}, u32[]{:S(2)}) collective-permute-start(bf16[3,6,4,512]{3,2,1,0:T(4,128)(2,1)S(1)} %get-tuple-element.28), channel_id=1, source_target_pairs={{0,32},{1,33},{2,34},{3,35},{4,36},{5,37},{6,38},{7,39},{8,40},{9,... | collective-permute-start | bytes 221192 | tf_op jit(solution)/shard_map/ppermute | solution.py:320
  56.5 0.0 copy-start.1
  56.5 0.0 copy-start.2
  56.5 2.1 %bias.1.bias_ref = bf16[16,288,288]{2,1,0:T(8,128)(2,1)S(1)} custom-call(bf16[16,288,288]{2,1,0:T(8,128)(2,1)} %bias_hbm), custom_call_target="tpu_custom_call" | custom-call | bytes 5308416 | tf_op jit(solution)/shard_map/bias/pallas_call | solution.py:255
  58.6 0.1 pad_add_fusion.spot_ref
  58.7 0.0 collective-permute-done.3
  58.7 3.8 %all-gather.2 = bf16[16,16,1536]{2,1,0:T(8,128)(2,1)S(1)} all-gather(bf16[8,16,1536]{2,1,0:T(8,128)(2,1)S(1)} %collective-permute-done.3), channel_id=4, replica_groups=mesh['xl'=2,'y'=8,'xh'=2,'z'=8,'c'=2] {'c'}, dimensions={0}, use_global_device_ids=true | all-gather | bytes 1179648 | tf_op jit(solution)/shard_map/all_gather | solution.py:325
  62.6 0.0 collective-permute-done.r0
  62.6 0.0 collective-permute-done.1.r2
  62.6 0.0 collective-permute-done.2.r1
  62.6 4.2 %attention.1 = (bf16[3,6,4,512]{3,2,1,0:T(4,128)(2,1)S(1)}, bf16[3,6,4,512]{3,2,1,0:T(4,128)(2,1)S(1)}, bf16[3,6,4,512]{3,2,1,0:T(4,128)(2,1)S(1)}, bf16[3,6,4,512]{3,2,1,0:T(4,128)(2,1)S(1)}) custom-call(s32[2]{0:T(128)S(1)} %pad_add_fusion.spot_ref, bf16[3,6,4,512]{3,2,1,0:T(4,128)(2,1)S(1)} %collective-permute-done.r0, ...), custom_call_target="tpu_custom_call" | custom-call | tf_op jit(solution)/shard_map/attention/pallas_call | solution.py:269
  66.8 0.0 copy-start
  66.8 0.0 copy-start.3
  66.8 0.0 copy-start.4
  66.8 4.4 %collective-permute-start.4 = (bf16[3,6,4,512]{3,2,1,0:T(4,128)(2,1)S(1)}, bf16[3,6,4,512]{3,2,1,0:T(4,128)(2,1)S(1)}, u32[]{:S(2)}, u32[]{:S(2)}) collective-permute-start(bf16[3,6,4,512]{3,2,1,0:T(4,128)(2,1)S(1)} %get-tuple-element.20), channel_id=1, source_target_pairs={{0,480},{1,481},{2,482},{3,483},{4,484},{5,485},{6,486},{7,487},{8... | collective-permute-start | bytes 221192 | tf_op jit(solution)/shard_map/ppermute | solution.py:330
  71.3 3.3 %collective-permute-start.5 = (bf16[3,6,4,512]{3,2,1,0:T(4,128)(2,1)S(1)}, bf16[3,6,4,512]{3,2,1,0:T(4,128)(2,1)S(1)}, u32[]{:S(2)}, u32[]{:S(2)}) collective-permute-start(bf16[3,6,4,512]{3,2,1,0:T(4,128)(2,1)S(1)} %get-tuple-element.21), channel_id=1, source_target_pairs={{0,31},{1,0},{2,1},{3,2},{4,3},{5,4},{6,5},{7,6},{8,7},{9,8},{10,9... | collective-permute-start | bytes 221192 | tf_op jit(solution)/shard_map/ppermute | solution.py:331
  74.6 6.2 %collective-permute-start.6 = (bf16[3,6,4,512]{3,2,1,0:T(4,128)(2,1)S(1)}, bf16[3,6,4,512]{3,2,1,0:T(4,128)(2,1)S(1)}, u32[]{:S(2)}, u32[]{:S(2)}) collective-permute-start(bf16[3,6,4,512]{3,2,1,0:T(4,128)(2,1)S(1)} %get-tuple-element.22), channel_id=1, source_target_pairs={{0,511},{1,480},{2,481},{3,482},{4,483},{5,484},{6,485},{7,486},{8... | collective-permute-start | bytes 221192 | tf_op jit(solution)/shard_map/ppermute | solution.py:332
  80.7 0.0 all-gather.6.cloned.1.call-done
  80.8 2.4 %stage.1 = (bf16[16,2,16,512]{3,2,1,0:T(8,128)(2,1)S(1)}, bf16[16,2,64,512]{3,2,1,0:T(8,128)(2,1)S(1)}, bf16[16,2,64,512]{3,2,1,0:T(8,128)(2,1)S(1)}) custom-call(bf16[16,2,144,512]{3,2,1,0:T(8,128)(2,1)} %bitcast.20), custom_call_target="tpu_custom_call" | custom-call | bytes 9437184 | tf_op jit(solution)/shard_map/stage/pallas_call | solution.py:281
  83.2 0.0 collective-permute-done.4.m2
  83.2 0.0 collective-permute-done.5.m1
  83.2 0.0 collective-permute-done.6.m3
  83.3 2.8 %tokens.1 = bf16[6,12,4,512]{3,2,1,0:T(4,128)(2,1)} custom-call(bf16[3,6,4,512]{3,2,1,0:T(4,128)(2,1)S(1)} %collective-permute-done.4.m2, bf16[3,6,4,512]{3,2,1,0:T(4,128)(2,1)S(1)} %collective-permute-done.5.m1, bf16[3,6,4,512]{3,2,1,0:T(4,128)(2,1)S(1)} %collective-permute-done.6.m3, bf16[3,6,4,512]{3,2,1,0:T(4,128)(2,1)S(1)} %get-tuple-element.23.m0, ...), custom_call_target="tpu_custom_call" | custom-call | tf_op jit(solution)/shard_map/tokens/pallas_call | solution.py:296
  (6 shorter events, 0.0 us)
Async XLA Ops:
  6.5 74.2 %all-gather.6.cloned.1.call-start = ((), (), s32[]{:S(2)}) async-start(), calls=%async_computation | async-start | bytes 5013504 | tf_op jit(solution)/shard_map/all_gather | solution.py:312
  43.2 15.5 %collective-permute-start.3 = (bf16[8,16,1536]{2,1,0:T(8,128)(2,1)S(1)}, bf16[8,16,1536]{2,1,0:T(8,128)(2,1)S(1)}, u32[]{:S(2)}, u32[]{:S(2)}) collective-permute-start(bf16[8,16,1536]{2,1,0:T(8,128)(2,1)S(1)} %dynamic-slice_bitcast_fusion), channel_id=1, source_target_pairs={{0,272},{272,0},{1,273},{273,1},{2,274},{274,2},{3,275},{275,3},{4... | collective-permute-start | bytes 1179656 | tf_op jit(solution)/shard_map/ppermute | solution.py:325
  49.5 13.0 %collective-permute-start = (bf16[3,6,4,512]{3,2,1,0:T(4,128)(2,1)S(1)}, bf16[3,6,4,512]{3,2,1,0:T(4,128)(2,1)S(1)}, u32[]{:S(2)}, u32[]{:S(2)}) collective-permute-start(bf16[3,6,4,512]{3,2,1,0:T(4,128)(2,1)S(1)} %get-tuple-element.30), channel_id=1, source_target_pairs={{0,33},{1,34},{2,35},{3,36},{4,37},{5,38},{6,39},{7,40},{8,41},{9,... | collective-permute-start | bytes 221192 | tf_op jit(solution)/shard_map/ppermute | solution.py:318
  51.5 11.1 %collective-permute-start.1 = (bf16[3,6,4,512]{3,2,1,0:T(4,128)(2,1)S(1)}, bf16[3,6,4,512]{3,2,1,0:T(4,128)(2,1)S(1)}, u32[]{:S(2)}, u32[]{:S(2)}) collective-permute-start(bf16[3,6,4,512]{3,2,1,0:T(4,128)(2,1)S(1)} %get-tuple-element.29), channel_id=1, source_target_pairs={{0,1},{1,2},{2,3},{3,4},{4,5},{5,6},{6,7},{7,8},{8,9},{9,10},{10,1... | collective-permute-start | bytes 221192 | tf_op jit(solution)/shard_map/ppermute | solution.py:319
  53.4 9.2 %collective-permute-start.2 = (bf16[3,6,4,512]{3,2,1,0:T(4,128)(2,1)S(1)}, bf16[3,6,4,512]{3,2,1,0:T(4,128)(2,1)S(1)}, u32[]{:S(2)}, u32[]{:S(2)}) collective-permute-start(bf16[3,6,4,512]{3,2,1,0:T(4,128)(2,1)S(1)} %get-tuple-element.28), channel_id=1, source_target_pairs={{0,32},{1,33},{2,34},{3,35},{4,36},{5,37},{6,38},{7,39},{8,40},{9,... | collective-permute-start | bytes 221192 | tf_op jit(solution)/shard_map/ppermute | solution.py:320
  56.5 6.1 %copy-start.1 = (bf16[288,288]{1,0:T(8,128)(2,1)S(1)}, bf16[288,288]{1,0:T(8,128)(2,1)}, u32[]{:S(2)}) copy-start(bf16[288,288]{1,0:T(8,128)(2,1)} %constant.31.clone.hot_ref) | copy-start | bytes 497668
  56.5 6.1 %copy-start.2 = (bf16[2,288,128]{2,1,0:T(8,128)(2,1)S(1)}, bf16[2,288,128]{2,1,0:T(8,128)(2,1)}, u32[]{:S(2)}) copy-start(bf16[2,288,128]{2,1,0:T(8,128)(2,1)} %constant.32.clone.tags_ref) | copy-start | bytes 442372
  66.8 16.4 %copy-start = (bf16[4,6,12,512]{3,0,2,1:T(4,128)(2,1)S(1)}, bf16[4,6,12,512]{3,0,2,1:T(4,128)(2,1)}, u32[]{:S(2)}) copy-start(bf16[4,6,12,512]{3,0,2,1:T(4,128)(2,1)} %param.10) | copy-start | bytes 884740
  66.8 16.4 %copy-start.3 = (f32[512]{0:T(512)S(1)}, f32[512]{0:T(512)}, u32[]{:S(2)}) copy-start(f32[512]{0:T(512)} %param.14) | copy-start | bytes 6148
  66.8 16.4 %copy-start.4 = (f32[512]{0:T(512)S(1)}, f32[512]{0:T(512)}, u32[]{:S(2)}) copy-start(f32[512]{0:T(512)} %param.17) | copy-start | bytes 6148
  66.8 16.4 %collective-permute-start.4 = (bf16[3,6,4,512]{3,2,1,0:T(4,128)(2,1)S(1)}, bf16[3,6,4,512]{3,2,1,0:T(4,128)(2,1)S(1)}, u32[]{:S(2)}, u32[]{:S(2)}) collective-permute-start(bf16[3,6,4,512]{3,2,1,0:T(4,128)(2,1)S(1)} %get-tuple-element.20), channel_id=1, source_target_pairs={{0,480},{1,481},{2,482},{3,483},{4,484},{5,485},{6,486},{7,487},{8... | collective-permute-start | bytes 221192 | tf_op jit(solution)/shard_map/ppermute | solution.py:330
  71.3 12.0 %collective-permute-start.5 = (bf16[3,6,4,512]{3,2,1,0:T(4,128)(2,1)S(1)}, bf16[3,6,4,512]{3,2,1,0:T(4,128)(2,1)S(1)}, u32[]{:S(2)}, u32[]{:S(2)}) collective-permute-start(bf16[3,6,4,512]{3,2,1,0:T(4,128)(2,1)S(1)} %get-tuple-element.21), channel_id=1, source_target_pairs={{0,31},{1,0},{2,1},{3,2},{4,3},{5,4},{6,5},{7,6},{8,7},{9,8},{10,9... | collective-permute-start | bytes 221192 | tf_op jit(solution)/shard_map/ppermute | solution.py:331
  74.6 8.7 %collective-permute-start.6 = (bf16[3,6,4,512]{3,2,1,0:T(4,128)(2,1)S(1)}, bf16[3,6,4,512]{3,2,1,0:T(4,128)(2,1)S(1)}, u32[]{:S(2)}, u32[]{:S(2)}) collective-permute-start(bf16[3,6,4,512]{3,2,1,0:T(4,128)(2,1)S(1)} %get-tuple-element.22), channel_id=1, source_target_pairs={{0,511},{1,480},{2,481},{3,482},{4,483},{5,484},{6,485},{7,486},{8... | collective-permute-start | bytes 221192 | tf_op jit(solution)/shard_map/ppermute | solution.py:332
Sparse Core Ops, SparseCore 0:
  14.2 53.6 all-gather.5

commit v14 on v11

--- a/solution.py
+++ b/solution.py
@@ -123,12 +123,15 @@
 
 
 def bias_kernel(bias_hbm, bias_ref, sems):
-    copy_all([(bias_hbm, bias_ref)], sems)
+    copy_all([(bias_hbm.at[: HEADS // 2], bias_ref)], sems)
 
 
 def attention_kernel(
-    spot_ref, r0, r2, r1, r3, mine_ref, other_ref, hot_ref, tags_ref, bias_ref, o0, o1, o2, o3
+    spot_ref, r0, r2, r1, r3, mine_ref, other_ref, hot_ref, tags_ref, bias_ref, bias_hbm,
+    o0, o1, o2, o3, late_ref, sem,
 ):
+    fetch = pltpu.make_async_copy(bias_hbm.at[HEADS // 2 :], late_ref, sem)
+    fetch.start()
     hot = hot_ref[...]
     rows = stacked([r[...] for r in (r0, r1, r2, r3)]).astype(BF16)
     rows = lax.dot_general(hot, rows, (((0,), (0,)), ((), ())), preferred_element_type=F32)
@@ -152,6 +155,8 @@
     key_tags = tags_ref[1]
     groups = []
     for group in range(GROUPS):
+        if group == GROUPS // 2:
+            fetch.wait()
         lanes = slice(group * LANES, (group + 1) * LANES)
         group_q = jnp.concatenate([queries[:, lanes], query_tags], 1)
         group_k, group_v = keys[:, lanes], values[:, lanes]
@@ -164,7 +169,9 @@
         scores = dot_t(group_q, jnp.concatenate(key_rows, 0))
         weights = []
         for j in range(PER_GROUP):
-            bias = bias_ref[group * PER_GROUP + j].astype(F32)
+            head = group * PER_GROUP + j
+            early = head < HEADS // 2
+            bias = (bias_ref[head] if early else late_ref[head - HEADS // 2]).astype(F32)
             bias = jnp.concatenate([bias, beyond], 1)
             head = scores[:, j * PADDED : (j + 1) * PADDED] * HEAD_DIM ** (-0.5) + bias
             weights.append(jnp.exp(head - jnp.max(head, -1, keepdims=True)).astype(BF16))
@@ -256,24 +263,25 @@
         bias_kernel,
         in_specs=[fetched()],
         out_specs=held(),
-        out_shape=jax.ShapeDtypeStruct(bias.shape, BF16),
+        out_shape=jax.ShapeDtypeStruct((HEADS // 2, WN, WN), BF16),
         scratch_shapes=[pltpu.SemaphoreType.DMA((1,))],
         compiler_params=params(),
-        cost_estimate=pl.CostEstimate(flops=0, bytes_accessed=2 * bias.size * 2, transcendentals=0),
+        cost_estimate=pl.CostEstimate(flops=0, bytes_accessed=bias.size * 2, transcendentals=0),
         name="bias",
     )(*off_chip(bias))
 
 
-def attention(spot, quarters, mine, other, bias):
+def attention(spot, quarters, mine, other, early_bias, bias):
     constants = (jnp.asarray(to_quarters(), BF16), jnp.asarray(tags(), BF16))
     return pl.pallas_call(
         attention_kernel,
-        in_specs=[scalars()] + [held()] * (len(quarters) + 5),
+        in_specs=[scalars()] + [held()] * (len(quarters) + 5) + [fetched()],
         out_specs=[held()] * 4,
         out_shape=[jax.ShapeDtypeStruct(CORNER, BF16)] * 4,
+        scratch_shapes=[pltpu.VMEM((HEADS // 2, WN, WN), BF16), pltpu.SemaphoreType.DMA(())],
         compiler_params=pltpu.CompilerParams(vmem_limit_bytes=ATTENTION_LIMIT),
         name="attention",
-    )(spot, *quarters, mine, other, *constants, bias)
+    )(spot, *quarters, mine, other, *constants, early_bias, *off_chip(bias))
 
 
 def staged(gathered):
@@ -325,7 +333,7 @@
     theirs = lax.all_gather(lax.ppermute(sent, AXES, mirrored()), "c", axis=0, tiled=False)
 
     spot = jnp.stack([lax.axis_index("xh"), (lax.axis_index(LAT) == 0).astype(jnp.int32)])
-    attended = attention(spot, rolled, mine, theirs, held_bias(bias))
+    attended = attention(spot, rolled, mine, theirs, held_bias(bias), bias)
     restored = [
         lax.ppermute(attended[1], AXES, shifted(-1, 0)),
         lax.ppermute(attended[0], AXES, shifted(-1, -1)),

time: 92.9 us -> 92 us (level)
  waiting for transfers between devices: 0.06 us -> 1.45 us
  local copies, waits for them, and re-layouts: 1.17 us -> 0.16 us
    ppermute x1, starting transfers between devices: 2.92 us -> 5.52 us  [shards(): lax.ppermute(attended[0], AXES, shifted(-1, -1))]
    ppermute x1, starting transfers between devices: 6.08 us -> 4.04 us  [shards(): lax.ppermute(attended[2], AXES, shifted(0, -1))]
    slice x1, local copies, waits for them, and re-layouts: 1.11 us -> 0.1 us  [corner(): cells[i * HALF_LAT:(i + 1) * HALF_LAT, j * HALF_LON:(j + 1) * HALF_LON]]
  transfers between devices with their start and end apart: 8 -> 8, of which waited for: 0 -> 2; matrix products, arithmetic and copies ran while one was open for 1% -> 0% of each run, Pallas kernels for 9% -> 9%
where the time goes in v14:
time: 92 us; the launch traced here: 91.6 us
  blocking collectives  38.8 us (42%)
  starting transfers between devices  25.2 us (27%)
  between operations  13.6 us (15%)
  Pallas kernels  12.4 us (13%)
  waiting for transfers between devices  1.45 us (2%)
    all_gather x1, blocking collectives, shards(): mine = lax.all_gather(qkv_weight, ('z', 'c'), axis=0, tiled=False)  29.1 us
    all_gather x1, blocking collectives, shards(): lax.all_gather(own, AXES, axis=0, tiled=False, axis_index_groups=mirrored...  6.6 us
    ppermute x1, starting transfers between devices, shards(): lax.ppermute(attended[0], AXES, shifted(-1, -1))  5.52 us
    ppermute x1, starting transfers between devices, shards(): lax.ppermute(sent, AXES, mirrored())  5.15 us
    pallas_call x1, Pallas kernels, attention(): pl.pallas_call(attention_kernel, in_specs=[scalars()] + [held()] * (len(q...  4.61 us
    ppermute x1, starting transfers between devices, shards(): lax.ppermute(attended[2], AXES, shifted(0, -1))  4.04 us
    ppermute x1, starting transfers between devices, shards(): lax.ppermute(attended[1], AXES, shifted(-1, 0))  3.5 us
    ppermute x1, starting transfers between devices, shards(): lax.ppermute(corner(cells_after, 1, 0), AXES, shifted(1, 0))  3.11 us
  transfers between devices with their start and end apart: 8, of which 2 were waited for; matrix products, arithmetic and copies ran while one was open for 0% of the time, Pallas kernels for 9%

profile of v14, /device:TPU:1, one launch (start us, length us, event | category | flops | bytes accessed | tf_op | source)
XLA Modules:
  0.0 91.6 jit_solution(18224203885880625095)
XLA Ops:
  6.5 0.0 all-gather.6.cloned.1.call-start
  6.5 0.9 %pack.1 = bf16[144,512]{1,0:T(8,128)(2,1)S(1)} custom-call(bf16[64,512]{1,0:T(8,128)(2,1)} %up_ref.1, bf16[64,512]{1,0:T(8,128)(2,1)} %down_ref.1, bf16[16,512]{1,0:T(8,128)(2,1)} %proj_ref.1), custom_call_target="tpu_custom_call" | custom-call | tf_op jit(solution)/shard_map/pack/pallas_call | solution.py:250
  7.5 6.6 %all-gather = bf16[288,512]{1,0:T(8,128)(2,1)} all-gather(bf16[144,512]{1,0:T(8,128)(2,1)S(1)} %pack.1), channel_id=2, replica_groups={{0,272},{1,273},{2,274},{3,275},{4,276},{5,277},{6,278},{7,279},{8,280}..., dimensions={0}, use_global_device_ids=true | all-gather | bytes 442368 | tf_op jit(solution)/shard_map/all_gather | solution.py:319
  14.1 0.0 all-gather.6.cloned.1.call-update
  14.1 29.1 %all-gather.1 = bf16[256,1536]{1,0:T(8,128)(2,1)S(1)} all-gather(bf16[16,1536]{1,0:T(8,128)(2,1)} %param.11), channel_id=3, replica_groups=mesh['xl'=2,'y'=8,'xh'=2,'z'=8,'c'=2] {'z','c'}, dimensions={0}, use_global_device_ids=true | all-gather | bytes 835584 | tf_op jit(solution)/shard_map/all_gather | solution.py:322
  43.3 5.2 %collective-permute-start.3 = (bf16[8,16,1536]{2,1,0:T(8,128)(2,1)S(1)}, bf16[8,16,1536]{2,1,0:T(8,128)(2,1)S(1)}, u32[]{:S(2)}, u32[]{:S(2)}) collective-permute-start(bf16[8,16,1536]{2,1,0:T(8,128)(2,1)S(1)} %dynamic-slice_bitcast_fusion), channel_id=1, source_target_pairs={{0,272},{272,0},{1,273},{273,1},{2,274},{274,2},{3,275},{275,3},{4... | collective-permute-start | bytes 1179656 | tf_op jit(solution)/shard_map/ppermute | solution.py:333
  48.5 0.0 copy-done
  48.5 0.1 fusion
  48.6 3.1 %collective-permute-start.2 = (bf16[3,6,4,512]{3,2,1,0:T(4,128)(2,1)S(1)}, bf16[3,6,4,512]{3,2,1,0:T(4,128)(2,1)S(1)}, u32[]{:S(2)}, u32[]{:S(2)}) collective-permute-start(bf16[3,6,4,512]{3,2,1,0:T(4,128)(2,1)S(1)} %get-tuple-element.28), channel_id=1, source_target_pairs={{0,32},{1,33},{2,34},{3,35},{4,36},{5,37},{6,38},{7,39},{8,40},{9,... | collective-permute-start | bytes 221192 | tf_op jit(solution)/shard_map/ppermute | solution.py:328
  51.7 1.9 %collective-permute-start.1 = (bf16[3,6,4,512]{3,2,1,0:T(4,128)(2,1)S(1)}, bf16[3,6,4,512]{3,2,1,0:T(4,128)(2,1)S(1)}, u32[]{:S(2)}, u32[]{:S(2)}) collective-permute-start(bf16[3,6,4,512]{3,2,1,0:T(4,128)(2,1)S(1)} %get-tuple-element.29), channel_id=1, source_target_pairs={{0,1},{1,2},{2,3},{3,4},{4,5},{5,6},{6,7},{7,8},{8,9},{9,10},{10,1... | collective-permute-start | bytes 221192 | tf_op jit(solution)/shard_map/ppermute | solution.py:327
  53.6 1.9 %collective-permute-start = (bf16[3,6,4,512]{3,2,1,0:T(4,128)(2,1)S(1)}, bf16[3,6,4,512]{3,2,1,0:T(4,128)(2,1)S(1)}, u32[]{:S(2)}, u32[]{:S(2)}) collective-permute-start(bf16[3,6,4,512]{3,2,1,0:T(4,128)(2,1)S(1)} %get-tuple-element.30), channel_id=1, source_target_pairs={{0,33},{1,34},{2,35},{3,36},{4,37},{5,38},{6,39},{7,40},{8,41},{9,... | collective-permute-start | bytes 221192 | tf_op jit(solution)/shard_map/ppermute | solution.py:326
  55.6 0.0 copy-start.1
  55.6 0.0 copy-start.2
  55.6 1.6 %bias.1.bias_ref = bf16[8,288,288]{2,1,0:T(8,128)(2,1)S(1)} custom-call(bf16[16,288,288]{2,1,0:T(8,128)(2,1)} %bias_hbm.1), custom_call_target="tpu_custom_call" | custom-call | bytes 2654208 | tf_op jit(solution)/shard_map/bias/pallas_call | solution.py:262
  57.2 0.1 pad_add_fusion.spot_ref
  57.2 0.6 collective-permute-done.3
  57.9 3.1 %all-gather.2 = bf16[16,16,1536]{2,1,0:T(8,128)(2,1)S(1)} all-gather(bf16[8,16,1536]{2,1,0:T(8,128)(2,1)S(1)} %collective-permute-done.3), channel_id=4, replica_groups=mesh['xl'=2,'y'=8,'xh'=2,'z'=8,'c'=2] {'c'}, dimensions={0}, use_global_device_ids=true | all-gather | bytes 1179648 | tf_op jit(solution)/shard_map/all_gather | solution.py:333
  60.9 0.0 collective-permute-done.2.r1
  60.9 0.0 collective-permute-done.1.r2
  60.9 0.8 collective-permute-done.r0
  61.7 4.6 %attention.1 = (bf16[3,6,4,512]{3,2,1,0:T(4,128)(2,1)S(1)}, bf16[3,6,4,512]{3,2,1,0:T(4,128)(2,1)S(1)}, bf16[3,6,4,512]{3,2,1,0:T(4,128)(2,1)S(1)}, bf16[3,6,4,512]{3,2,1,0:T(4,128)(2,1)S(1)}) custom-call(s32[2]{0:T(128)S(1)} %pad_add_fusion.spot_ref, bf16[3,6,4,512]{3,2,1,0:T(4,128)(2,1)S(1)} %collective-permute-done.r0, ...), custom_call_target="tpu_custom_call" | custom-call | tf_op jit(solution)/shard_map/attention/pallas_call | solution.py:276
  66.3 3.5 %collective-permute-start.4 = (bf16[3,6,4,512]{3,2,1,0:T(4,128)(2,1)S(1)}, bf16[3,6,4,512]{3,2,1,0:T(4,128)(2,1)S(1)}, u32[]{:S(2)}, u32[]{:S(2)}) collective-permute-start(bf16[3,6,4,512]{3,2,1,0:T(4,128)(2,1)S(1)} %get-tuple-element.20), channel_id=1, source_target_pairs={{0,480},{1,481},{2,482},{3,483},{4,484},{5,485},{6,486},{7,487},{8... | collective-permute-start | bytes 221192 | tf_op jit(solution)/shard_map/ppermute | solution.py:338
  69.8 5.5 %collective-permute-start.5 = (bf16[3,6,4,512]{3,2,1,0:T(4,128)(2,1)S(1)}, bf16[3,6,4,512]{3,2,1,0:T(4,128)(2,1)S(1)}, u32[]{:S(2)}, u32[]{:S(2)}) collective-permute-start(bf16[3,6,4,512]{3,2,1,0:T(4,128)(2,1)S(1)} %get-tuple-element.21), channel_id=1, source_target_pairs={{0,511},{1,480},{2,481},{3,482},{4,483},{5,484},{6,485},{7,486},{8... | collective-permute-start | bytes 221192 | tf_op jit(solution)/shard_map/ppermute | solution.py:339
  75.4 4.0 %collective-permute-start.6 = (bf16[3,6,4,512]{3,2,1,0:T(4,128)(2,1)S(1)}, bf16[3,6,4,512]{3,2,1,0:T(4,128)(2,1)S(1)}, u32[]{:S(2)}, u32[]{:S(2)}) collective-permute-start(bf16[3,6,4,512]{3,2,1,0:T(4,128)(2,1)S(1)} %get-tuple-element.22), channel_id=1, source_target_pairs={{0,31},{1,0},{2,1},{3,2},{4,3},{5,4},{6,5},{7,6},{8,7},{9,8},{10,9... | collective-permute-start | bytes 221192 | tf_op jit(solution)/shard_map/ppermute | solution.py:340
  79.4 0.0 all-gather.6.cloned.1.call-done
  79.4 0.0 copy-start.3
  79.5 0.0 copy-start.4
  79.5 2.4 %stage.1 = (bf16[16,2,16,512]{3,2,1,0:T(8,128)(2,1)S(1)}, bf16[16,2,64,512]{3,2,1,0:T(8,128)(2,1)S(1)}, bf16[16,2,64,512]{3,2,1,0:T(8,128)(2,1)S(1)}) custom-call(bf16[16,2,144,512]{3,2,1,0:T(8,128)(2,1)} %bitcast.20), custom_call_target="tpu_custom_call" | custom-call | bytes 9437184 | tf_op jit(solution)/shard_map/stage/pallas_call | solution.py:289
  81.9 0.0 collective-permute-done.4.m2
  81.9 0.0 collective-permute-done.5.m3
  81.9 0.0 collective-permute-done.6.m1
  82.0 2.8 %tokens.1 = bf16[6,12,4,512]{3,2,1,0:T(4,128)(2,1)} custom-call(bf16[3,6,4,512]{3,2,1,0:T(4,128)(2,1)S(1)} %collective-permute-done.4.m2, bf16[3,6,4,512]{3,2,1,0:T(4,128)(2,1)S(1)} %collective-permute-done.5.m3, bf16[3,6,4,512]{3,2,1,0:T(4,128)(2,1)S(1)} %collective-permute-done.6.m1, bf16[3,6,4,512]{3,2,1,0:T(4,128)(2,1)S(1)} %get-tuple-element.23.m0, ...), custom_call_target="tpu_custom_call" | custom-call | tf_op jit(solution)/shard_map/tokens/pallas_call | solution.py:304
  (6 shorter events, 0.0 us)
Async XLA Ops:
  6.5 41.9 %copy-start = (bf16[4,6,12,512]{3,0,2,1:T(4,128)(2,1)S(1)}, bf16[4,6,12,512]{3,0,2,1:T(4,128)(2,1)}, u32[]{:S(2)}) copy-start(bf16[4,6,12,512]{3,0,2,1:T(4,128)(2,1)} %param.10) | copy-start | bytes 884740
  6.5 72.9 %all-gather.6.cloned.1.call-start = ((), (), s32[]{:S(2)}) async-start(), calls=%async_computation | async-start | bytes 5013504 | tf_op jit(solution)/shard_map/all_gather | solution.py:320
  43.3 14.6 %collective-permute-start.3 = (bf16[8,16,1536]{2,1,0:T(8,128)(2,1)S(1)}, bf16[8,16,1536]{2,1,0:T(8,128)(2,1)S(1)}, u32[]{:S(2)}, u32[]{:S(2)}) collective-permute-start(bf16[8,16,1536]{2,1,0:T(8,128)(2,1)S(1)} %dynamic-slice_bitcast_fusion), channel_id=1, source_target_pairs={{0,272},{272,0},{1,273},{273,1},{2,274},{274,2},{3,275},{275,3},{4... | collective-permute-start | bytes 1179656 | tf_op jit(solution)/shard_map/ppermute | solution.py:333
  48.6 12.4 %collective-permute-start.2 = (bf16[3,6,4,512]{3,2,1,0:T(4,128)(2,1)S(1)}, bf16[3,6,4,512]{3,2,1,0:T(4,128)(2,1)S(1)}, u32[]{:S(2)}, u32[]{:S(2)}) collective-permute-start(bf16[3,6,4,512]{3,2,1,0:T(4,128)(2,1)S(1)} %get-tuple-element.28), channel_id=1, source_target_pairs={{0,32},{1,33},{2,34},{3,35},{4,36},{5,37},{6,38},{7,39},{8,40},{9,... | collective-permute-start | bytes 221192 | tf_op jit(solution)/shard_map/ppermute | solution.py:328
  51.7 9.2 %collective-permute-start.1 = (bf16[3,6,4,512]{3,2,1,0:T(4,128)(2,1)S(1)}, bf16[3,6,4,512]{3,2,1,0:T(4,128)(2,1)S(1)}, u32[]{:S(2)}, u32[]{:S(2)}) collective-permute-start(bf16[3,6,4,512]{3,2,1,0:T(4,128)(2,1)S(1)} %get-tuple-element.29), channel_id=1, source_target_pairs={{0,1},{1,2},{2,3},{3,4},{4,5},{5,6},{6,7},{7,8},{8,9},{9,10},{10,1... | collective-permute-start | bytes 221192 | tf_op jit(solution)/shard_map/ppermute | solution.py:327
  53.6 8.1 %collective-permute-start = (bf16[3,6,4,512]{3,2,1,0:T(4,128)(2,1)S(1)}, bf16[3,6,4,512]{3,2,1,0:T(4,128)(2,1)S(1)}, u32[]{:S(2)}, u32[]{:S(2)}) collective-permute-start(bf16[3,6,4,512]{3,2,1,0:T(4,128)(2,1)S(1)} %get-tuple-element.30), channel_id=1, source_target_pairs={{0,33},{1,34},{2,35},{3,36},{4,37},{5,38},{6,39},{7,40},{8,41},{9,... | collective-permute-start | bytes 221192 | tf_op jit(solution)/shard_map/ppermute | solution.py:326
  55.6 6.1 %copy-start.1 = (bf16[288,288]{1,0:T(8,128)(2,1)S(1)}, bf16[288,288]{1,0:T(8,128)(2,1)}, u32[]{:S(2)}) copy-start(bf16[288,288]{1,0:T(8,128)(2,1)} %constant.31.clone.hot_ref) | copy-start | bytes 497668
  55.6 6.1 %copy-start.2 = (bf16[2,288,128]{2,1,0:T(8,128)(2,1)S(1)}, bf16[2,288,128]{2,1,0:T(8,128)(2,1)}, u32[]{:S(2)}) copy-start(bf16[2,288,128]{2,1,0:T(8,128)(2,1)} %constant.32.clone.tags_ref) | copy-start | bytes 442372
  66.3 15.6 %collective-permute-start.4 = (bf16[3,6,4,512]{3,2,1,0:T(4,128)(2,1)S(1)}, bf16[3,6,4,512]{3,2,1,0:T(4,128)(2,1)S(1)}, u32[]{:S(2)}, u32[]{:S(2)}) collective-permute-start(bf16[3,6,4,512]{3,2,1,0:T(4,128)(2,1)S(1)} %get-tuple-element.20), channel_id=1, source_target_pairs={{0,480},{1,481},{2,482},{3,483},{4,484},{5,485},{6,486},{7,487},{8... | collective-permute-start | bytes 221192 | tf_op jit(solution)/shard_map/ppermute | solution.py:338
  69.8 12.1 %collective-permute-start.5 = (bf16[3,6,4,512]{3,2,1,0:T(4,128)(2,1)S(1)}, bf16[3,6,4,512]{3,2,1,0:T(4,128)(2,1)S(1)}, u32[]{:S(2)}, u32[]{:S(2)}) collective-permute-start(bf16[3,6,4,512]{3,2,1,0:T(4,128)(2,1)S(1)} %get-tuple-element.21), channel_id=1, source_target_pairs={{0,511},{1,480},{2,481},{3,482},{4,483},{5,484},{6,485},{7,486},{8... | collective-permute-start | bytes 221192 | tf_op jit(solution)/shard_map/ppermute | solution.py:339
  75.4 6.6 %collective-permute-start.6 = (bf16[3,6,4,512]{3,2,1,0:T(4,128)(2,1)S(1)}, bf16[3,6,4,512]{3,2,1,0:T(4,128)(2,1)S(1)}, u32[]{:S(2)}, u32[]{:S(2)}) collective-permute-start(bf16[3,6,4,512]{3,2,1,0:T(4,128)(2,1)S(1)} %get-tuple-element.22), channel_id=1, source_target_pairs={{0,31},{1,0},{2,1},{3,2},{4,3},{5,4},{6,5},{7,6},{8,7},{9,8},{10,9... | collective-permute-start | bytes 221192 | tf_op jit(solution)/shard_map/ppermute | solution.py:340
  79.4 2.5 %copy-start.3 = (f32[512]{0:T(512)S(1)}, f32[512]{0:T(512)}, u32[]{:S(2)}) copy-start(f32[512]{0:T(512)} %param.14) | copy-start | bytes 6148
  79.5 2.5 %copy-start.4 = (f32[512]{0:T(512)S(1)}, f32[512]{0:T(512)}, u32[]{:S(2)}) copy-start(f32[512]{0:T(512)} %param.17) | copy-start | bytes 6148
Sparse Core Ops, SparseCore 0:
  14.2 53.4 all-gather.5
